TPU v7x, 32 devices: a whole 2x2x4 slice. The times are simulated.
32 devices in a mesh: seq: 8 (over y, x, core), dp: 4 (over z).
Axes of the slice: x: 2, y: 2, z: 4, core: 2. Of those that a mesh axis runs over, the one named last changes fastest.
Arguments:
- queries: bfloat16 [4, 2048, 2048], P('dp', 'seq'), may hold values from -32 to 32
- keys: bfloat16 [4, 2048, 2048], P('dp', 'seq'), may hold values from -9 to 9
- values: bfloat16 [4, 2048, 2048], P('dp', 'seq'), may hold values from -6 to 6
- out_grad: bfloat16 [4, 2048, 2048], P('dp', 'seq'), may hold values from -6 to 6
- adjacency: int32 [4, 16, 8], P('dp', 'seq'), may hold values from 0 to 15, as said below
- counts: int32 [4, 16], P('dp', 'seq'), may hold values from 1 to 8, as said below
- sink: float32 [16], replicated, may hold values from 4 to 10
Outputs:
- attended: bfloat16 [4, 2048, 2048], P('dp', 'seq')
- query_grad: bfloat16 [4, 2048, 2048], P('dp', 'seq')
- key_grad: bfloat16 [4, 2048, 2048], P('dp', 'seq')
- value_grad: bfloat16 [4, 2048, 2048], P('dp', 'seq')
- sink_grad: float32 [16], replicated
Inputs may be any that keep to these rules, and one draw needn't show every extreme that they name: `adjacency`: row b of a sequence lists key blocks of the same sequence; slot 0 is b itself; the first counts[b] entries are distinct, and each lies on a device at most 2 seq indices from the device of block b (block c lies at seq index c // 2); entries after counts[b] equal b. `counts`: some block has 8 live entries.
All inputs are finite; a program needn't handle non-finite values.
Results may differ from a plain program's by a relative error of at most 0.014.
Values may be sent and summed in bfloat16 or wider, within the bound.
No kernel may reach another device: no remote copies, remote signals or barrier semaphores. Data moves between devices by JAX's collectives and lax.ppermute only.
A program may use at most 192 MiB of HBM per device.

v0:
```python
import jax
import jax.numpy as jnp
from jax import lax
from jax.sharding import PartitionSpec as P

H = 16
HD = 128
BLK = 128
RADIUS = 2
MAXADJ = 8


def shifted(block, axis, distance):
    devices = range(lax.axis_size(axis))
    route = [(i - distance, i) for i in devices if i - distance in devices]
    return lax.ppermute(block, axis, route)


def local(queries, keys, values, out_grad, adjacency, counts, sink):
    tokens = queries.shape[1]
    block_count = tokens // BLK
    score_scale = HD ** (-0.5)
    seq_rank = lax.axis_index("seq")
    query_blocks = queries.reshape(block_count, BLK, H, HD)
    key_blocks = keys.reshape(block_count, BLK, H, HD)
    value_blocks = values.reshape(block_count, BLK, H, HD)
    grad_blocks = out_grad.reshape(block_count, BLK, H, HD)
    slot_lists = adjacency[0]
    live_count = counts[0]
    sink_col = sink[None, :, None]
    near_keys = []
    near_values = []
    for offset in range(-RADIUS, RADIUS + 1):
        if offset == 0:
            near_keys.append(key_blocks)
            near_values.append(value_blocks)
        else:
            moved_key, moved_value = shifted((key_blocks, value_blocks), "seq", -offset)
            near_keys.append(moved_key)
            near_values.append(moved_value)
    key_window = jnp.concatenate(near_keys, axis=0)
    value_window = jnp.concatenate(near_values, axis=0)
    window_first = (seq_rank - RADIUS) * block_count
    slot_local = slot_lists - window_first
    slot_bound = MAXADJ

    def slot_index(slot_no):
        return lax.dynamic_index_in_dim(slot_local, slot_no, 1, keepdims=False)

    def fill_scores(slot_no, buffer):
        key_slot = jnp.take(key_window, slot_index(slot_no), axis=0)
        scores = (
            jnp.einsum(
                "bqhd,bkhd->bhqk", query_blocks, key_slot, preferred_element_type=jnp.float32
            )
            * score_scale
        )
        scores = jnp.where((slot_no < live_count)[:, None, None, None], scores, -jnp.inf)
        return lax.dynamic_update_index_in_dim(buffer, scores, slot_no, 0)

    empty_scores = jnp.full((MAXADJ, block_count, H, BLK, BLK), -jnp.inf, jnp.float32)
    buffer = lax.fori_loop(0, slot_bound, fill_scores, empty_scores)
    row_max = jnp.maximum(jnp.max(buffer, axis=(0, 4)), sink_col)
    row_total = jnp.sum(jnp.exp(buffer - row_max[None, :, :, :, None]), axis=(0, 4)) + jnp.exp(
        sink_col - row_max
    )

    def prob_at(slot_no):
        scores = lax.dynamic_index_in_dim(buffer, slot_no, 0, keepdims=False)
        return jnp.exp(scores - row_max[..., None]) / row_total[..., None]

    def forward_slot(slot_no, accum):
        value_slot = jnp.take(value_window, slot_index(slot_no), axis=0)
        probs_low = prob_at(slot_no).astype(jnp.bfloat16)
        return accum + jnp.einsum(
            "bhqk,bkhd->bqhd", probs_low, value_slot, preferred_element_type=jnp.float32
        )

    zero_rows = jnp.zeros((block_count, BLK, H, HD), jnp.float32)
    attended_wide = lax.fori_loop(0, slot_bound, forward_slot, zero_rows)
    attended_low = attended_wide.astype(jnp.bfloat16)
    row_delta = jnp.transpose(
        jnp.sum(grad_blocks.astype(jnp.float32) * attended_low.astype(jnp.float32), axis=3),
        (0, 2, 1),
    )
    sink_prob = jnp.exp(sink_col - row_max) / row_total
    sink_part = -jnp.sum(sink_prob * row_delta, axis=(0, 2))
    sink_grad = lax.psum(sink_part, ("seq", "dp"))

    def slot_terms(slot_no):
        slot_at = slot_index(slot_no)
        key_slot = jnp.take(key_window, slot_at, axis=0)
        value_slot = jnp.take(value_window, slot_at, axis=0)
        probs = prob_at(slot_no)
        probs_low = probs.astype(jnp.bfloat16)
        dprobs = jnp.einsum(
            "bqhd,bkhd->bhqk", grad_blocks, value_slot, preferred_element_type=jnp.float32
        )
        dscores = (probs * (dprobs - row_delta[..., None])).astype(jnp.bfloat16)
        return (slot_at, key_slot, probs_low, dscores)

    def with_window(slot_no, carried):
        query_accum, key_accum, value_accum = carried
        slot_at, key_slot, probs_low, dscores = slot_terms(slot_no)
        query_accum = query_accum + jnp.einsum(
            "bhqk,bkhd->bqhd", dscores, key_slot, preferred_element_type=jnp.float32
        )
        key_terms = (
            jnp.einsum("bhqk,bqhd->bkhd", dscores, query_blocks, preferred_element_type=jnp.float32)
            * score_scale
        )
        value_terms = jnp.einsum(
            "bhqk,bqhd->bkhd", probs_low, grad_blocks, preferred_element_type=jnp.float32
        )
        return (
            query_accum,
            key_accum.at[slot_at].add(key_terms),
            value_accum.at[slot_at].add(value_terms),
        )

    zero_window = jnp.zeros(((2 * RADIUS + 1) * block_count, BLK, H, HD), jnp.float32)
    query_accum, key_accum, value_accum = lax.fori_loop(
        0, slot_bound, with_window, (zero_rows, zero_window, zero_window)
    )
    key_total = zero_rows
    value_total = zero_rows
    for offset in range(-RADIUS, RADIUS + 1):
        first_row = (offset + RADIUS) * block_count
        key_piece = key_accum[first_row : first_row + block_count]
        value_piece = value_accum[first_row : first_row + block_count]
        if offset != 0:
            key_piece, value_piece = shifted((key_piece, value_piece), "seq", offset)
        key_total = key_total + key_piece
        value_total = value_total + value_piece
    query_grad = (query_accum * score_scale).astype(jnp.bfloat16)
    out_shape = (1, tokens, H * HD)
    return (
        attended_low.reshape(out_shape),
        query_grad.reshape(out_shape),
        key_total.astype(jnp.bfloat16).reshape(out_shape),
        value_total.astype(jnp.bfloat16).reshape(out_shape),
        sink_grad,
    )


def solution(mesh):
    return jax.shard_map(
        local,
        mesh=mesh,
        in_specs=(
            P("dp", "seq", None),
            P("dp", "seq", None),
            P("dp", "seq", None),
            P("dp", "seq", None),
            P("dp", "seq", None),
            P("dp", "seq"),
            P(),
        ),
        out_specs=(
            P("dp", "seq", None),
            P("dp", "seq", None),
            P("dp", "seq", None),
            P("dp", "seq", None),
            P(),
        ),
        check_vma=False,
    )
```

profile of v0, /device:TPU:0, one launch (start us, length us, event | category | flops | bytes accessed | tf_op | source)
XLA Modules:
  0.0 827.9 jit_solution(9556348393110584165)
XLA Ops:
  2.3 5.8 collective-permute-start.4
  17.9 12.8 %collective-permute-done.4 = bf16[2,128,16,128]{3,2,1,0:T(8,128)(2,1)} collective-permute-done((bf16[2,128,16,128]{3,2,1,0:T(8,128)(2,1)S(1)}, bf16[2,128,16,128]{3,2,1,0:T(8,128)(2,1)}, u32[]{:S(2)}, u32[]{:S(2)}) %collective-permute-start.4) | collective-permute-done | bytes 1048608 | tf_op jit(solution)/shard_map/ppermute | solution.py:16
  33.4 10.4 %collective-permute-start.1 = (bf16[2,128,16,128]{3,2,1,0:T(8,128)(2,1)}, bf16[2,128,16,128]{3,2,1,0:T(8,128)(2,1)}, u32[]{:S(2)}, u32[]{:S(2)}) collective-permute-start(bf16[2,128,16,128]{3,2,1,0:T(8,128)(2,1)} %bitcast.20), channel_id=1, source_target_pairs={{0,4},{4,8},{8,12},{12,16},{16,20},{20,24},{24,28},{1,5},{5,9},{9,... | collective-permute-start | bytes 3145736 | tf_op jit(solution)/shard_map/ppermute | solution.py:16
  45.5 13.5 %collective-permute-start = (bf16[2,128,16,128]{3,2,1,0:T(8,128)(2,1)}, bf16[2,128,16,128]{3,2,1,0:T(8,128)(2,1)}, u32[]{:S(2)}, u32[]{:S(2)}) collective-permute-start(bf16[2,128,16,128]{3,2,1,0:T(8,128)(2,1)} %bitcast.20), channel_id=1, source_target_pairs={{0,8},{4,12},{8,16},{12,20},{16,24},{20,28},{1,9},{5,13},{9,17},{1... | collective-permute-start | bytes 3145736 | tf_op jit(solution)/shard_map/ppermute | solution.py:16
  60.5 17.2 %collective-permute-done.7 = bf16[2,128,16,128]{3,2,1,0:T(8,128)(2,1)} collective-permute-done((bf16[2,128,16,128]{3,2,1,0:T(8,128)(2,1)S(1)}, bf16[2,128,16,128]{3,2,1,0:T(8,128)(2,1)}, u32[]{:S(2)}, u32[]{:S(2)}) %collective-permute-start.7) | collective-permute-done | bytes 1048608 | tf_op jit(solution)/shard_map/ppermute | solution.py:16
  81.4 45.1 %while.45 = (s32[]{:T(128)}, f32[8,2,16,128,128]{3,4,2,1,0:T(8,128)}, s32[2]{0:T(128)S(1)}, s32[2,8]{0,1:T(8,128)S(1)}, bf16[10,128,16,128]{3,2,1,0:T(8,128)(2,1...) while((s32[]{:T(128)}, f32[8,2,16,128,128]{3,4,2,1,0:T(8,128)}, s32[2]{0:T(128)S(1)}, ...), condition=%wide.region_1.0_spmd, body=%wide.region_0.2_spmd.sunk | while | flops 135791632 | bytes 8393865 | solution.py:62
  126.5 7.6 reduce_max.9
  140.1 8.2 exponential_reduce_fusion
  152.2 107.7 %while.46 = (s32[]{:T(128)}, f32[2,128,16,128]{1,3,2,0:T(8,128)}, s32[2,8]{0,1:T(8,128)S(1)}, bf16[10,128,16,128]{3,2,1,0:T(8,128)(2,1)}, f32[8,2,16,128,128]{3,...) while((s32[]{:T(128)}, f32[2,128,16,128]{1,3,2,0:T(8,128)}, ...), condition=%wide.region_5.7_spmd.clone, body=%wide.region_4.6_spmd.clone.sunk | while | flops 137364496 | bytes 19959964 | solution.py:80
  160.2 4.9 bitcast_add_fusion.4
  173.1 5.6 bitcast_add_fusion.4
  186.6 5.6 bitcast_add_fusion.4
  200.2 5.6 bitcast_add_fusion.4
  213.7 5.6 bitcast_add_fusion.4
  227.3 5.6 bitcast_add_fusion.4
  240.8 5.6 bitcast_add_fusion.4
  254.3 5.6 bitcast_add_fusion.4
  262.9 4.9 broadcast_in_dim.78.clone
  267.9 5.0 broadcast_in_dim.78
  272.8 217.9 %while.47 = (s32[]{:T(128)}, f32[2,128,16,128]{1,3,2,0:T(8,128)}, f32[10,128,16,128]{3,2,1,0:T(8,128)}, f32[10,128,16,128]{3,2,1,0:T(8,128)}, s32[2,8]{0,1:T(8,1...) while((s32[]{:T(128)}, f32[2,128,16,128]{1,3,2,0:T(8,128)}, ...), condition=%wide.region_10.12_spmd.clone, body=%wide.region_7.11_spmd.clone.sunk | while | flops 544736256 | bytes 71389520 | solution.py:122
  291.3 4.7 scatter_fusion.1
  318.5 4.8 scatter_fusion.1
  345.7 4.7 scatter_fusion.1
  373.0 4.7 scatter_fusion.1
  400.2 4.7 scatter_fusion.1
  490.7 5.5 fusion.17
  499.0 14.1 %collective-permute-start.15 = (f32[2,128,16,128]{3,2,1,0:T(8,128)S(1)}, f32[2,128,16,128]{3,2,1,0:T(8,128)}, u32[]{:S(2)}, u32[]{:S(2)}) collective-permute-start(f32[2,128,16,128]{3,2,1,0:T(8,128)S(1)} %get-tuple-element.693), channel_id=1, source_target_pairs={{0,8},{4,12},{8,16},{12,20},{16,24},{20,28},{1,9},{5,13},{9,17},{1... | collective-permute-start | bytes 6291464 | tf_op jit(solution)/shard_map/ppermute | solution.py:16
  522.7 74.8 %collective-permute-done.12 = f32[2,128,16,128]{3,2,1,0:T(8,128)} collective-permute-done((f32[2,128,16,128]{3,2,1,0:T(8,128)S(1)}, f32[2,128,16,128]{3,2,1,0:T(8,128)}, u32[]{:S(2)}, u32[]{:S(2)}) %collective-permute-start.12) | collective-permute-done | bytes 2097184 | tf_op jit(solution)/shard_map/ppermute | solution.py:16
  597.5 5.3 collective-permute-start.11
  605.6 206.4 %psum.7 = f32[16]{0:T(128)} all-reduce(f32[16]{0:T(128)S(1)} %neg.3), channel_id=1, replica_groups=mesh['seq'=8,'dp'=4] {'seq','dp'}, use_global_device_ids=true, to_apply=%region_12.14 | all-reduce | flops 16 | bytes 128 | tf_op jit(solution)/shard_map/psum | solution.py:88
  815.9 4.7 add_convert_fusion
  821.9 4.7 add_convert_fusion.1
  (330 shorter events, 357.3 us)
Async XLA Ops:
  0.6 12.5 %copy-start.10 = (bf16[1,256,2048]{2,1,0:T(8,128)(2,1)S(1)}, bf16[1,256,2048]{2,1,0:T(8,128)(2,1)}, u32[]{:S(2)}) copy-start(bf16[1,256,2048]{2,1,0:T(8,128)(2,1)} %param.17) | copy-start | bytes 3145732
  0.6 15.0 %copy-start.16 = (s32[1,2,8]{2,1,0:T(2,128)S(1)}, s32[1,2,8]{2,1,0:T(2,128)}, u32[]{:S(2)}) copy-start(s32[1,2,8]{2,1,0:T(2,128)} %param.19) | copy-start | bytes 196
  0.7 15.1 %copy-start.11 = (bf16[1,256,2048]{2,1,0:T(8,128)(2,1)S(1)}, bf16[1,256,2048]{2,1,0:T(8,128)(2,1)}, u32[]{:S(2)}) copy-start(bf16[1,256,2048]{2,1,0:T(8,128)(2,1)} %param.18) | copy-start | bytes 3145732
  2.3 28.4 %collective-permute-start.4 = (bf16[2,128,16,128]{3,2,1,0:T(8,128)(2,1)S(1)}, bf16[2,128,16,128]{3,2,1,0:T(8,128)(2,1)}, u32[]{:S(2)}, u32[]{:S(2)}) collective-permute-start(bf16[2,128,16,128]{3,2,1,0:T(8,128)(2,1)S(1)} %bitcast.122), channel_id=1, source_target_pairs={{0,8},{4,12},{8,16},{12,20},{16,24},{20,28},{1,9},{5,13},{9,17},{1... | collective-permute-start | bytes 3145736 | tf_op jit(solution)/shard_map/ppermute | solution.py:16
  8.1 25.3 %collective-permute-start.5 = (bf16[2,128,16,128]{3,2,1,0:T(8,128)(2,1)S(1)}, bf16[2,128,16,128]{3,2,1,0:T(8,128)(2,1)}, u32[]{:S(2)}, u32[]{:S(2)}) collective-permute-start(bf16[2,128,16,128]{3,2,1,0:T(8,128)(2,1)S(1)} %bitcast.123), channel_id=1, source_target_pairs={{0,4},{4,8},{8,12},{12,16},{16,20},{20,24},{24,28},{1,5},{5,9},{9,... | collective-permute-start | bytes 3145736 | tf_op jit(solution)/shard_map/ppermute | solution.py:16
  10.5 34.9 %collective-permute-start.6 = (bf16[2,128,16,128]{3,2,1,0:T(8,128)(2,1)S(1)}, bf16[2,128,16,128]{3,2,1,0:T(8,128)(2,1)}, u32[]{:S(2)}, u32[]{:S(2)}) collective-permute-start(bf16[2,128,16,128]{3,2,1,0:T(8,128)(2,1)S(1)} %bitcast.124), channel_id=1, source_target_pairs={{4,0},{8,4},{12,8},{16,12},{20,16},{24,20},{28,24},{5,1},{9,5},{13... | collective-permute-start | bytes 3145736 | tf_op jit(solution)/shard_map/ppermute | solution.py:16
  11.8 65.8 %collective-permute-start.7 = (bf16[2,128,16,128]{3,2,1,0:T(8,128)(2,1)S(1)}, bf16[2,128,16,128]{3,2,1,0:T(8,128)(2,1)}, u32[]{:S(2)}, u32[]{:S(2)}) collective-permute-start(bf16[2,128,16,128]{3,2,1,0:T(8,128)(2,1)S(1)} %bitcast.125), channel_id=1, source_target_pairs={{8,0},{12,4},{16,8},{20,12},{24,16},{28,20},{9,1},{13,5},{17,9},{2... | collective-permute-start | bytes 3145736 | tf_op jit(solution)/shard_map/ppermute | solution.py:16
  14.4 134.0 %collective-permute-start.3 = (bf16[2,128,16,128]{3,2,1,0:T(8,128)(2,1)}, bf16[2,128,16,128]{3,2,1,0:T(8,128)(2,1)}, u32[]{:S(2)}, u32[]{:S(2)}) collective-permute-start(bf16[2,128,16,128]{3,2,1,0:T(8,128)(2,1)} %bitcast.20), channel_id=1, source_target_pairs={{8,0},{12,4},{16,8},{20,12},{24,16},{28,20},{9,1},{13,5},{17,9},{2... | collective-permute-start | bytes 3145736 | tf_op jit(solution)/shard_map/ppermute | solution.py:16
  30.7 107.9 %collective-permute-start.2 = (bf16[2,128,16,128]{3,2,1,0:T(8,128)(2,1)}, bf16[2,128,16,128]{3,2,1,0:T(8,128)(2,1)}, u32[]{:S(2)}, u32[]{:S(2)}) collective-permute-start(bf16[2,128,16,128]{3,2,1,0:T(8,128)(2,1)} %bitcast.20), channel_id=1, source_target_pairs={{4,0},{8,4},{12,8},{16,12},{20,16},{24,20},{28,24},{5,1},{9,5},{13... | collective-permute-start | bytes 3145736 | tf_op jit(solution)/shard_map/ppermute | solution.py:16
  33.4 102.2 %collective-permute-start.1 = (bf16[2,128,16,128]{3,2,1,0:T(8,128)(2,1)}, bf16[2,128,16,128]{3,2,1,0:T(8,128)(2,1)}, u32[]{:S(2)}, u32[]{:S(2)}) collective-permute-start(bf16[2,128,16,128]{3,2,1,0:T(8,128)(2,1)} %bitcast.20), channel_id=1, source_target_pairs={{0,4},{4,8},{8,12},{12,16},{16,20},{20,24},{24,28},{1,5},{5,9},{9,... | collective-permute-start | bytes 3145736 | tf_op jit(solution)/shard_map/ppermute | solution.py:16
  45.5 35.9 %copy-start.14 = (s32[1,2]{1,0:T(1,128)S(1)}, s32[1,2]{1,0:T(1,128)}, u32[]{:S(2)}) copy-start(s32[1,2]{1,0:T(1,128)} %param.20) | copy-start | bytes 28
  45.5 88.6 %collective-permute-start = (bf16[2,128,16,128]{3,2,1,0:T(8,128)(2,1)}, bf16[2,128,16,128]{3,2,1,0:T(8,128)(2,1)}, u32[]{:S(2)}, u32[]{:S(2)}) collective-permute-start(bf16[2,128,16,128]{3,2,1,0:T(8,128)(2,1)} %bitcast.20), channel_id=1, source_target_pairs={{0,8},{4,12},{8,16},{12,20},{16,24},{20,28},{1,9},{5,13},{9,17},{1... | collective-permute-start | bytes 3145736 | tf_op jit(solution)/shard_map/ppermute | solution.py:16
  135.5 3.0 copy-start.15
  262.2 5.6 copy-start.6
  280.6 2.6 copy-start.1
  307.8 2.6 copy-start.1
  335.0 2.6 copy-start.1
  362.3 2.6 copy-start.1
  389.5 2.6 copy-start.1
  444.0 2.6 copy-start.1
  471.2 2.6 copy-start.1
  490.7 25.8 %copy-start = (f32[10,128,16,128]{3,2,1,0:T(8,128)S(1)}, f32[10,128,16,128]{3,2,1,0:T(8,128)}, u32[]{:S(2)}) copy-start(f32[10,128,16,128]{3,2,1,0:T(8,128)} %get-tuple-element.458) | copy-start | bytes 31457284
  496.2 25.2 %collective-permute-start.13 = (f32[2,128,16,128]{3,2,1,0:T(8,128)S(1)}, f32[2,128,16,128]{3,2,1,0:T(8,128)}, u32[]{:S(2)}, u32[]{:S(2)}) collective-permute-start(f32[2,128,16,128]{3,2,1,0:T(8,128)S(1)} %get-tuple-element.691), channel_id=1, source_target_pairs={{4,0},{8,4},{12,8},{16,12},{20,16},{24,20},{28,24},{5,1},{9,5},{13... | collective-permute-start | bytes 6291464 | tf_op jit(solution)/shard_map/ppermute | solution.py:16
  497.7 99.8 %collective-permute-start.12 = (f32[2,128,16,128]{3,2,1,0:T(8,128)S(1)}, f32[2,128,16,128]{3,2,1,0:T(8,128)}, u32[]{:S(2)}, u32[]{:S(2)}) collective-permute-start(f32[2,128,16,128]{3,2,1,0:T(8,128)S(1)} %get-tuple-element.692), channel_id=1, source_target_pairs={{8,0},{12,4},{16,8},{20,12},{24,16},{28,20},{9,1},{13,5},{17,9},{2... | collective-permute-start | bytes 6291464 | tf_op jit(solution)/shard_map/ppermute | solution.py:16
  499.0 103.8 %collective-permute-start.15 = (f32[2,128,16,128]{3,2,1,0:T(8,128)S(1)}, f32[2,128,16,128]{3,2,1,0:T(8,128)}, u32[]{:S(2)}, u32[]{:S(2)}) collective-permute-start(f32[2,128,16,128]{3,2,1,0:T(8,128)S(1)} %get-tuple-element.693), channel_id=1, source_target_pairs={{0,8},{4,12},{8,16},{12,20},{16,24},{20,28},{1,9},{5,13},{9,17},{1... | collective-permute-start | bytes 6291464 | tf_op jit(solution)/shard_map/ppermute | solution.py:16
  513.0 302.8 %collective-permute-start.14 = (f32[2,128,16,128]{3,2,1,0:T(8,128)}, f32[2,128,16,128]{3,2,1,0:T(8,128)}, u32[]{:S(2)}, u32[]{:S(2)}) collective-permute-start(f32[2,128,16,128]{3,2,1,0:T(8,128)} %get-tuple-element.694), channel_id=1, source_target_pairs={{0,4},{4,8},{8,12},{12,16},{16,20},{20,24},{24,28},{1,5},{5,9},{9,... | collective-permute-start | bytes 6291464 | tf_op jit(solution)/shard_map/ppermute | solution.py:16
  516.5 295.5 %copy-start.7 = (bf16[2,128,16,128]{3,2,1,0:T(8,128)(2,1)S(1)}, bf16[2,128,16,128]{3,2,1,0:T(8,128)(2,1)}, u32[]{:S(2)}) copy-start(bf16[2,128,16,128]{3,2,1,0:T(8,128)(2,1)} %copy-done.6) | copy-start | bytes 3145732
  520.0 293.3 %copy-start.3 = (f32[2,128,16,128]{1,3,2,0:T(8,128)S(1)}, f32[2,128,16,128]{1,3,2,0:T(8,128)}, u32[]{:S(2)}) copy-start(f32[2,128,16,128]{1,3,2,0:T(8,128)} %get-tuple-element.457) | copy-start | bytes 6291460
  520.0 301.9 %collective-permute-start.9 = (f32[2,128,16,128]{3,2,1,0:T(8,128)}, f32[2,128,16,128]{3,2,1,0:T(8,128)}, u32[]{:S(2)}, u32[]{:S(2)}) collective-permute-start(f32[2,128,16,128]{3,2,1,0:T(8,128)} %get-tuple-element.695), channel_id=1, source_target_pairs={{4,0},{8,4},{12,8},{16,12},{20,16},{24,20},{28,24},{5,1},{9,5},{13... | collective-permute-start | bytes 6291464 | tf_op jit(solution)/shard_map/ppermute | solution.py:16
  521.4 300.5 %collective-permute-start.8 = (f32[2,128,16,128]{3,2,1,0:T(8,128)}, f32[2,128,16,128]{3,2,1,0:T(8,128)}, u32[]{:S(2)}, u32[]{:S(2)}) collective-permute-start(f32[2,128,16,128]{3,2,1,0:T(8,128)} %get-tuple-element.696), channel_id=1, source_target_pairs={{8,0},{12,4},{16,8},{20,12},{24,16},{28,20},{9,1},{13,5},{17,9},{2... | collective-permute-start | bytes 6291464 | tf_op jit(solution)/shard_map/ppermute | solution.py:16
  597.5 224.4 %collective-permute-start.11 = (f32[2,128,16,128]{3,2,1,0:T(8,128)}, f32[2,128,16,128]{3,2,1,0:T(8,128)}, u32[]{:S(2)}, u32[]{:S(2)}) collective-permute-start(f32[2,128,16,128]{3,2,1,0:T(8,128)} %get-tuple-element.697), channel_id=1, source_target_pairs={{0,8},{4,12},{8,16},{12,20},{16,24},{20,28},{1,9},{5,13},{9,17},{1... | collective-permute-start | bytes 6291464 | tf_op jit(solution)/shard_map/ppermute | solution.py:16
  602.8 219.1 %collective-permute-start.10 = (f32[2,128,16,128]{3,2,1,0:T(8,128)}, f32[2,128,16,128]{3,2,1,0:T(8,128)}, u32[]{:S(2)}, u32[]{:S(2)}) collective-permute-start(f32[2,128,16,128]{3,2,1,0:T(8,128)} %get-tuple-element.698), channel_id=1, source_target_pairs={{0,4},{4,8},{8,12},{12,16},{16,20},{20,24},{24,28},{1,5},{5,9},{9,... | collective-permute-start | bytes 6291464 | tf_op jit(solution)/shard_map/ppermute | solution.py:16
  (22 other events, 33.1 us)
where the time goes:
time: 831 us; the launch traced here: 828 us
  local copies, waits for them, and re-layouts  227 us (27%)
  blocking collectives  206 us (25%)
  other arithmetic  110 us (13%)
  matrix products  110 us (13%)
  waiting for transfers between devices  105 us (13%)
  starting transfers between devices  68.2 us (8%)
    psum x1, blocking collectives, local(): sink_grad = lax.psum(sink_part, ('seq', 'dp'))  206 us
    ppermute x16, waiting for transfers between devices, shifted(): return lax.ppermute(block, axis, route)  105 us
    ppermute x16, starting transfers between devices, shifted(): return lax.ppermute(block, axis, route)  68.2 us
    dot_general x8, matrix products, forward_slot(): jnp.einsum('bhqk,bkhd->bqhd', probs_low, value_slot, preferred_element_ty...  43.9 us
    scatter-add x8, other arithmetic, with_window(): value_accum.at[slot_at].add(value_terms)  37.9 us
    scatter-add x8, other arithmetic, with_window(): key_accum.at[slot_at].add(key_terms)  32.6 us
    dynamic_slice x16, local copies, waits for them, and re-layouts, prob_at(): scores = lax.dynamic_index_in_dim(buffer, slot_no, 0, keepdims=False)  28.5 us
    gather x8, local copies, waits for them, and re-layouts, fill_scores(): key_slot = jnp.take(key_window, slot_index(slot_no), axis=0)  25.9 us
  transfers between devices with their start and end apart: 16, of which 3 were waited for; matrix products, arithmetic and copies ran while one was open for 11% of the time, Pallas kernels for 0%

commit v1 on v0

v1 whole, which is shorter than its diff:
```python
import functools

import jax
import jax.numpy as jnp
from jax import lax
from jax.experimental import pallas as pl
from jax.experimental.pallas import tpu as pltpu
from jax.sharding import PartitionSpec as P

HD = 128
BLK = 128
RADIUS = 2
GROUP = 8
NOTE = 16
LOG2E = 1.4426950408889634
VMEM_LIMIT = 48 * 1024 * 1024
NT = (((1,), (1,)), ((), ()))
NN = (((1,), (0,)), ((), ()))
ANY = pl.BlockSpec(memory_space=pl.ANY)
SMEM = pl.BlockSpec(memory_space=pltpu.SMEM)
VMEM = pl.BlockSpec(memory_space=pltpu.VMEM)


def sending_order(group):
    return sorted(range(group), key=lambda k: (k & 2 == 0, k & 4 == 0, k == 0))


def pack_kernel(group, per_device, head, adjacency, counts, *refs):
    sources, parcels = refs[:4], refs[4 : 4 + group]
    stage, note, in_sems, out_sems = refs[4 + group :]
    tokens = sources[0].shape[1]
    rank = lax.axis_index("seq")
    spot = lax.rem(rank, group)
    order = sending_order(group)
    reads = {}
    for k in order:
        column = pl.multiple_of(((spot ^ k) * per_device + head) * HD, HD)
        for a, source in enumerate(sources):
            reads[k, a] = pltpu.make_async_copy(
                source.at[0, :, pl.ds(column, HD)],
                stage.at[k, pl.ds(a * tokens, tokens)],
                in_sems.at[k, a],
            )
            reads[k, a].start()
    own_blocks, slots = adjacency.shape[1:]
    rows = lax.broadcasted_iota(jnp.int32, note.shape, 0)
    lanes = lax.broadcasted_iota(jnp.int32, note.shape, 1)
    marks = jnp.zeros(note.shape, jnp.int32)
    for b in range(own_blocks):
        for j in range(slots):
            marks = jnp.where(
                (rows == b) & (lanes == j), adjacency[0, b, j] - rank * own_blocks, marks
            )
        marks = jnp.where((rows == b) & (lanes == slots), counts[0, b], marks)
    note[...] = marks.astype(jnp.float32)
    for k in range(group):
        stage[k, 4 * tokens :, :] = note[...].astype(jnp.bfloat16)
    writes = []
    for k in order:
        for a in range(4):
            reads[k, a].wait()
        writes.append(pltpu.make_async_copy(stage.at[k], parcels[k], out_sems.at[k]))
        writes[-1].start()
    for write in writes:
        write.wait()


def pack(adjacency, counts, sources, group, per_device, head):
    tokens = sources[0].shape[1]
    rows = 4 * tokens + NOTE
    return pl.pallas_call(
        functools.partial(pack_kernel, group, per_device, head),
        out_shape=[jax.ShapeDtypeStruct((rows, HD), jnp.bfloat16)] * group,
        in_specs=[SMEM] * 2 + [ANY] * 4,
        out_specs=[ANY] * group,
        scratch_shapes=[
            pltpu.VMEM((group, rows, HD), jnp.bfloat16),
            pltpu.VMEM((NOTE, HD), jnp.float32),
            pltpu.SemaphoreType.DMA((group, 4)),
            pltpu.SemaphoreType.DMA((group,)),
        ],
        compiler_params=pltpu.CompilerParams(vmem_limit_bytes=VMEM_LIMIT),
        cost_estimate=pl.CostEstimate(
            flops=0, bytes_accessed=group * rows * HD * 4, transcendentals=0
        ),
        name="pack",
    )(adjacency, counts, *sources)


def unpack_kernel(group, per_device, head, *refs):
    parcels, outs = refs[:group], refs[-7:-3]
    stage, in_sems, out_sems = refs[-3:]
    tokens = outs[0].shape[1]
    spot = lax.rem(lax.axis_index("seq"), group)
    reads = []
    for k in range(group):
        reads.append(pltpu.make_async_copy(parcels[k], stage.at[k], in_sems.at[k]))
        reads[-1].start()
    writes = []
    for k in range(group):
        column = pl.multiple_of(((spot ^ k) * per_device + head) * HD, HD)
        reads[k].wait()
        for a, out in enumerate(outs):
            writes.append(
                pltpu.make_async_copy(
                    stage.at[k, pl.ds(a * tokens, tokens)],
                    out.at[0, :, pl.ds(column, HD)],
                    out_sems.at[k, a],
                )
            )
            writes[-1].start()
    for write in writes:
        write.wait()


def unpack(parcels, outs, group, per_device, head):
    rows = parcels[0].shape[0]
    shape = jax.ShapeDtypeStruct((1, rows // 4, group * per_device * HD), jnp.bfloat16)
    held = [] if outs is None else list(outs)
    return pl.pallas_call(
        functools.partial(unpack_kernel, group, per_device, head),
        out_shape=[shape] * 4,
        in_specs=[ANY] * (group + len(held)),
        out_specs=[ANY] * 4,
        scratch_shapes=[
            pltpu.VMEM((group, rows, HD), jnp.bfloat16),
            pltpu.SemaphoreType.DMA((group,)),
            pltpu.SemaphoreType.DMA((group, 4)),
        ],
        input_output_aliases={group + a: a for a in range(len(held))},
        compiler_params=pltpu.CompilerParams(vmem_limit_bytes=VMEM_LIMIT),
        cost_estimate=pl.CostEstimate(
            flops=0, bytes_accessed=group * rows * HD * 4, transcendentals=0
        ),
        name="unpack",
    )(*parcels, *held)


def attend_kernel(group, per_device, head, halo, slots, own_blocks, scale, *refs):
    sink, sink_in = refs[:2]
    parcels = refs[2 : 2 + group]
    refs = refs[2 + group :]
    if halo:
        halo_in, refs = refs[0], refs[1:]
    results, sink_out = refs[:group], refs[group]
    refs = refs[group + 1 :]
    if halo:
        halo_out, refs = refs[0], refs[1:]
    kv, qd, notes, marks, lists, kt, vt, diag, diag_back, scored, paired, acc, out = refs[:13]
    sink_acc, sems, list_sem, out_sems = refs[13:]

    blocks = own_blocks * group
    span = own_blocks * BLK
    edge = halo * BLK
    window = blocks + 2 * halo
    spot = lax.rem(lax.axis_index("seq"), group)
    number = spot * per_device + head
    note_copies, copies = [], []
    for k in range(group):
        other = spot ^ k
        note_copies.append(
            pltpu.make_async_copy(
                parcels[k].at[pl.ds(4 * span, NOTE)], notes.at[other], sems.at[k, 4]
            )
        )
    for k in range(group):
        row = pl.multiple_of((spot ^ k) * span, span)
        targets = (
            kv.at[pl.ds(row + edge, span), pl.ds(0, HD)],
            kv.at[pl.ds(row + edge, span), pl.ds(HD, HD)],
            qd.at[pl.ds(row, span), pl.ds(0, HD)],
            qd.at[pl.ds(row, span), pl.ds(HD, HD)],
        )
        for a, target in enumerate(targets):
            copies.append(
                pltpu.make_async_copy(parcels[k].at[pl.ds(a * span, span)], target, sems.at[k, a])
            )
    if halo:
        copies.append(pltpu.make_async_copy(halo_in.at[0], kv.at[pl.ds(0, edge)], sems.at[group, 0]))
        copies.append(
            pltpu.make_async_copy(
                halo_in.at[1], kv.at[pl.ds(edge + blocks * BLK, edge)], sems.at[group, 1]
            )
        )
    for copy in note_copies + copies:
        copy.start()
    diag[...] = jnp.zeros_like(diag)
    diag_back[...] = jnp.zeros_like(diag_back)
    acc[...] = jnp.zeros_like(acc)
    sink_acc[...] = jnp.zeros_like(sink_acc)
    for copy in note_copies:
        copy.wait()
    for j in range(group):
        marks[pl.ds(j * own_blocks, own_blocks), :] = (
            notes[j].astype(jnp.float32).astype(jnp.int32)[:own_blocks]
        )
    list_copy = pltpu.make_async_copy(marks, lists, list_sem)
    list_copy.start()
    for copy in copies:
        copy.wait()

    def turn(c, carry):
        rows = kv[pl.ds(pl.multiple_of(c * BLK, BLK), BLK), :]
        kt[c] = rows[:, :HD].T
        vt[c] = rows[:, HD:].T
        return carry

    lax.fori_loop(0, window, turn, 0)
    list_copy.wait()

    to_log2 = scale * LOG2E
    sink_log2 = sink[number] * LOG2E

    def folded(x, op):
        return functools.reduce(op, [x[r : r + 8] for r in range(0, x.shape[0], 8)])

    def one_block(b, carry):
        rows = pl.ds(pl.multiple_of(b * BLK, BLK), BLK)
        home = b // own_blocks * own_blocks + halo
        query = qd[rows, :HD]
        grad = qd[rows, HD:]
        diag[:BLK, :HD] = query
        diag[BLK:, HD:] = grad
        diag_back[:BLK, :HD] = grad
        diag_back[BLK:, HD:] = query

        def with_slots(live):
            at = [lists[b, j] + home for j in range(live)]
            key_rows = [pl.ds(pl.multiple_of(c * BLK, BLK), BLK) for c in at]
            weights = diag[...]
            top = None
            for j in range(live):
                both = lax.dot_general(kv[key_rows[j], :], weights, NT, preferred_element_type=jnp.float32)
                scored[j] = both
                part = folded(both[:, :BLK], jnp.maximum)
                top = part if top is None else jnp.maximum(top, part)
            top = jnp.maximum(jnp.max(top, axis=0, keepdims=True) * to_log2, sink_log2)
            total = jnp.zeros((8, BLK), jnp.float32)
            dotted = jnp.zeros((8, BLK), jnp.float32)
            for j in range(live):
                power = jnp.exp2(scored[j, :, :BLK] * to_log2 - top)
                scored[j, :, :BLK] = power
                total = total + folded(power, jnp.add)
                dotted = dotted + folded(power * scored[j, :, BLK:], jnp.add)
            sink_power = jnp.exp2(sink_log2 - top)
            inverse = 1.0 / (jnp.sum(total, axis=0, keepdims=True) + sink_power)
            delta = jnp.sum(dotted, axis=0, keepdims=True) * inverse
            sink_acc[...] += sink_power * inverse * delta
            weights = diag_back[...]
            for j in range(live):
                probs = scored[j, :, :BLK] * inverse
                dscores = probs * (scored[j, :, BLK:] - delta)
                pair = jnp.concatenate([probs, dscores], axis=1).astype(jnp.bfloat16)
                paired[pl.ds(j * BLK, BLK), :] = pair
                acc[key_rows[j], :] += lax.dot_general(
                    pair, weights, NN, preferred_element_type=jnp.float32
                )
            attended = lax.dot_general(
                jnp.concatenate([vt[c] for c in at], axis=1),
                paired[: live * BLK, :BLK],
                NN,
                preferred_element_type=jnp.float32,
            )
            query_grad = lax.dot_general(
                jnp.concatenate([kt[c] for c in at], axis=1),
                paired[: live * BLK, BLK:],
                NN,
                preferred_element_type=jnp.float32,
            )
            out[2, rows, :] = attended.astype(jnp.bfloat16).T
            out[3, rows, :] = (query_grad * scale).astype(jnp.bfloat16).T

        for live in range(1, slots + 1):
            pl.when(lists[b, slots] == live)(functools.partial(with_slots, live))
        return carry

    lax.fori_loop(0, blocks, one_block, 0)

    def finish(b, carry):
        rows = pl.ds(pl.multiple_of(b * BLK, BLK), BLK)
        from_rows = pl.ds(pl.multiple_of((b + halo) * BLK, BLK), BLK)
        out[0, rows, :] = acc[from_rows, :HD].astype(jnp.bfloat16)
        out[1, rows, :] = (acc[from_rows, HD:] * scale).astype(jnp.bfloat16)
        return carry

    lax.fori_loop(0, blocks, finish, 0)
    lanes = lax.broadcasted_iota(jnp.int32, (1, BLK), 1)
    sink_sum = jnp.sum(sink_acc[...], axis=1, keepdims=True)
    sink_out[...] = sink_in[...] - jnp.where(lanes == number, sink_sum, 0.0)
    copies = []
    for k in sending_order(group):
        row = pl.multiple_of((spot ^ k) * span, span)
        for a in range(4):
            copies.append(
                pltpu.make_async_copy(
                    out.at[a, pl.ds(row, span)],
                    results[k].at[pl.ds(a * span, span)],
                    out_sems.at[k, a],
                )
            )
    for copy in copies:
        copy.start()
    if halo:
        for side, row in ((0, 0), (1, edge + blocks * BLK)):
            halo_out[side, :, :HD] = acc[pl.ds(row, edge), :HD]
            halo_out[side, :, HD:] = acc[pl.ds(row, edge), HD:] * scale
    for copy in copies:
        copy.wait()


def attend(sink, sink_in, parcels, halo_in, group, per_device, head, halo, slots, own_blocks, scale):
    span = own_blocks * BLK
    edge = halo * BLK
    blocks = own_blocks * group
    window = blocks + 2 * halo
    out_shape = [jax.ShapeDtypeStruct((4 * span, HD), jnp.bfloat16)] * group
    out_shape.append(jax.ShapeDtypeStruct((1, BLK), jnp.float32))
    out_specs = [ANY] * group + [VMEM]
    extra = []
    if halo:
        extra = [halo_in]
        out_shape.append(jax.ShapeDtypeStruct((2, edge, 2 * HD), jnp.float32))
        out_specs.append(VMEM)
    work = blocks * 4
    return pl.pallas_call(
        functools.partial(attend_kernel, group, per_device, head, halo, slots, own_blocks, scale),
        out_shape=out_shape,
        in_specs=[SMEM, VMEM] + [ANY] * (group + len(extra)),
        out_specs=out_specs,
        scratch_shapes=[
            pltpu.VMEM((window * BLK, 2 * HD), jnp.bfloat16),
            pltpu.VMEM((blocks * BLK, 2 * HD), jnp.bfloat16),
            pltpu.VMEM((group, NOTE, HD), jnp.bfloat16),
            pltpu.VMEM((blocks, HD), jnp.int32),
            pltpu.SMEM((blocks, HD), jnp.int32),
            pltpu.VMEM((window, HD, BLK), jnp.bfloat16),
            pltpu.VMEM((window, HD, BLK), jnp.bfloat16),
            pltpu.VMEM((2 * BLK, 2 * HD), jnp.bfloat16),
            pltpu.VMEM((2 * BLK, 2 * HD), jnp.bfloat16),
            pltpu.VMEM((slots, BLK, 2 * BLK), jnp.float32),
            pltpu.VMEM((slots * BLK, 2 * BLK), jnp.bfloat16),
            pltpu.VMEM((window * BLK, 2 * HD), jnp.float32),
            pltpu.VMEM((4, blocks * BLK, HD), jnp.bfloat16),
            pltpu.VMEM((1, BLK), jnp.float32),
            pltpu.SemaphoreType.DMA((group + 1, 5)),
            pltpu.SemaphoreType.DMA,
            pltpu.SemaphoreType.DMA((group, 4)),
        ],
        compiler_params=pltpu.CompilerParams(vmem_limit_bytes=VMEM_LIMIT),
        cost_estimate=pl.CostEstimate(
            flops=work * 10 * BLK * BLK * HD,
            bytes_accessed=blocks * BLK * HD * 16,
            transcendentals=work * BLK * BLK,
        ),
        name="attend",
    )(sink, sink_in, *parcels, *extra)


def local(queries, keys, values, out_grad, adjacency, counts, sink):
    seq = lax.axis_size("seq")
    group = min(seq, GROUP)
    groups = seq // group
    heads = sink.shape[0]
    per_device = heads // group
    slots = adjacency.shape[2]
    own_blocks = adjacency.shape[1]
    span = own_blocks * BLK
    halo = RADIUS * own_blocks if groups > 1 else 0
    scale = HD ** (-0.5)
    spot = lax.rem(lax.axis_index("seq"), group)

    def swap(x, k, axis="seq"):
        if k == 0:
            return x
        return lax.ppermute(x, axis, [(i, i ^ k) for i in range(lax.axis_size(axis))])

    def beside(x, step):
        route = [(i, i + step * group) for i in range(seq) if 0 <= i + step * group < seq]
        return lax.ppermute(x, "seq", route)

    sources = (keys, values, queries, out_grad)
    arrived = []
    for head in range(per_device):
        parcels = pack(adjacency, counts, sources, group, per_device, head)
        moved = {k: swap(parcels[k], k) for k in sending_order(group)}
        arrived.append([moved[k] for k in range(group)])

    sink_row = jnp.zeros((1, BLK), jnp.float32)
    outs = None
    returned = []
    for head in range(per_device):
        parcels = arrived[head]
        halo_in = None
        if halo:
            stacked = jnp.stack(parcels)
            ends = []
            for side, step in ((group - RADIUS, 1), (0, -1)):
                near = [stacked[(side + r) ^ spot] for r in range(RADIUS)]
                near = [jnp.concatenate([x[:span], x[span : 2 * span]], axis=1) for x in near]
                ends.append(beside(jnp.concatenate(near, axis=0), step))
            halo_in = jnp.stack(ends)
        done = attend(
            sink, sink_row, parcels, halo_in, group, per_device, head, halo, slots, own_blocks, scale
        )
        results, sink_row = list(done[:group]), done[group]
        if halo:
            stacked = jnp.stack(results)
            for side, step, half in ((group - RADIUS, -1, 0), (0, 1, 1)):
                grads = beside(done[group + 1][half], step)
                for r in range(RADIUS):
                    at = (side + r) ^ spot
                    rows = stacked[at]
                    more = grads[r * span : (r + 1) * span]
                    more = jnp.concatenate([more[:, :HD], more[:, HD:]], axis=0)
                    wide = rows[: 2 * span].astype(jnp.float32) + more
                    rows = jnp.concatenate([wide.astype(jnp.bfloat16), rows[2 * span :]], axis=0)
                    stacked = lax.dynamic_update_index_in_dim(stacked, rows, at, 0)
            results = [stacked[k] for k in range(group)]
        moved = {k: swap(results[k], k) for k in sending_order(group)}
        returned.append([moved[k] for k in range(group)])
    for axis in ("dp", "seq"):
        step = 1
        while step < lax.axis_size(axis):
            sink_row = sink_row + swap(sink_row, step, axis)
            step *= 2
    for head in range(per_device):
        outs = unpack(returned[head], outs, group, per_device, head)
    value_grad, key_grad, attended, query_grad = outs
    return attended, query_grad, key_grad, value_grad, sink_row[0, :heads]


def solution(mesh):
    tokens = P("dp", "seq", None)
    return jax.shard_map(
        local,
        mesh=mesh,
        in_specs=(tokens, tokens, tokens, tokens, tokens, P("dp", "seq"), P()),
        out_specs=(tokens, tokens, tokens, tokens, P()),
        check_vma=False,
    )
```

time: 831 us -> 153 us (0.18)
  local copies, waits for them, and re-layouts: 227 us -> 6.17 us
  blocking collectives: 206 us -> 0 us
  matrix products: 110 us -> 0 us
  other arithmetic: 110 us -> 0.02 us
  Pallas kernels: 0 us -> 45.4 us
  waiting for transfers between devices: 105 us -> 65.5 us
  starting transfers between devices: 68.2 us -> 34.6 us
    psum x1 -> x0, blocking collectives: 206 us -> none  [local(): sink_grad = lax.psum(sink_part, ('seq', 'dp'))]
    dot_general x48 -> x0, matrix products: 110 us -> none  [the longest x8 43.9 us: forward_slot(): jnp.einsum('bhqk,bkhd->bqhd', probs_low, value_slot, preferred_element_ty...]
    gather x32 -> x0, local copies, waits for them, and re-layouts: 104 us -> none  [the longest x8 25.9 us: fill_scores(): key_slot = jnp.take(key_window, slot_index(slot_no), axis=0)]
    scatter-add x16 -> x0, other arithmetic: 70.5 us -> none  [the longest x8 37.9 us: with_window(): value_accum.at[slot_at].add(value_terms)]
    pallas_call x0 -> x6, Pallas kernels: none -> 45.4 us  [the longest x2 37.2 us: attend(): pl.pallas_call(functools.partial(attend_kernel, group, per_device, head,...]
    ppermute x16 -> x33, waiting for transfers between devices: 105 us -> 65.5 us  [swap(): lax.ppermute(x, axis, [(i, i ^ k) for i in range(lax.axis_size(axis))])]
    ppermute x16 -> x33, starting transfers between devices: 68.2 us -> 34.6 us  [swap(): lax.ppermute(x, axis, [(i, i ^ k) for i in range(lax.axis_size(axis))])]
    dynamic_slice x16 -> x0, local copies, waits for them, and re-layouts: 28.5 us -> none  [prob_at(): scores = lax.dynamic_index_in_dim(buffer, slot_no, 0, keepdims=False)]
  transfers between devices with their start and end apart: 16 -> 33, of which waited for: 3 -> 15; matrix products, arithmetic and copies ran while one was open for 11% -> 0% of each run, Pallas kernels for 0% -> 15%
where the time goes in v1:
time: 153 us
  waiting for transfers between devices  65.5 us (43%)
  Pallas kernels  45.4 us (30%)
  starting transfers between devices  34.6 us (23%)
  local copies, waits for them, and re-layouts  6.17 us (4%)
    ppermute x33, waiting for transfers between devices, swap(): lax.ppermute(x, axis, [(i, i ^ k) for i in range(lax.axis_size(axis))])  65.5 us
    pallas_call x2, Pallas kernels, attend(): pl.pallas_call(functools.partial(attend_kernel, group, per_device, head,...  37.2 us
    ppermute x33, starting transfers between devices, swap(): lax.ppermute(x, axis, [(i, i ^ k) for i in range(lax.axis_size(axis))])  34.6 us
    unnamed x12, local copies, waits for them, and re-layouts  5.65 us
    pallas_call x2, Pallas kernels, pack(): pl.pallas_call(functools.partial(pack_kernel, group, per_device, head), o...  4.6 us
    pallas_call x2, Pallas kernels, unpack(): pl.pallas_call(functools.partial(unpack_kernel, group, per_device, head),...  3.57 us
  transfers between devices with their start and end apart: 33, of which 15 were waited for; matrix products, arithmetic and copies ran while one was open for 0% of the time, Pallas kernels for 15%

profile of v1, /device:TPU:0, one launch (start us, length us, event | category | flops | bytes accessed | tf_op | source)
XLA Modules:
  0.0 152.6 jit_solution(12925184963041438589)
XLA Ops:
  5.6 2.3 %pack.3 = (bf16[1040,128]{1,0:T(8,128)(2,1)S(1)}, bf16[1040,128]{1,0:T(8,128)(2,1)S(1)}, bf16[1040,128]{1,0:T(8,128)(2,1)S(1)}, bf16[1040,128]{1,0:T(8,128)(2,1)...) custom-call(s32[1,2,8]{2,1,0:T(2,128)S(1)} %copy-done.3, ...), custom_call_target="tpu_custom_call" | custom-call | bytes 4259840 | tf_op jit(solution)/shard_map/pack/pallas_call | solution.py:71
  8.5 2.6 %collective-permute-start.8 = (bf16[1040,128]{1,0:T(8,128)(2,1)S(1)}, bf16[1040,128]{1,0:T(8,128)(2,1)S(1)}, u32[]{:S(2)}, u32[]{:S(2)}) collective-permute-start(bf16[1040,128]{1,0:T(8,128)(2,1)S(1)} %get-tuple-element.58), channel_id=1, source_target_pairs={{0,8},{4,12},{8,0},{12,4},{16,24},{20,28},{24,16},{28,20},{1,9},{5... | collective-permute-start | bytes 798728 | tf_op jit(solution)/shard_map/ppermute | solution.py:375
  11.0 2.3 %pack.2 = (bf16[1040,128]{1,0:T(8,128)(2,1)S(1)}, bf16[1040,128]{1,0:T(8,128)(2,1)S(1)}, bf16[1040,128]{1,0:T(8,128)(2,1)S(1)}, bf16[1040,128]{1,0:T(8,128)(2,1)...) custom-call(s32[1,2,8]{2,1,0:T(2,128)S(1)} %copy-done.3, ...), custom_call_target="tpu_custom_call" | custom-call | bytes 4259840 | tf_op jit(solution)/shard_map/pack/pallas_call | solution.py:71
  15.3 1.5 collective-permute-start.3
  16.8 1.5 collective-permute-done.8.refs_4_
  19.1 2.1 %collective-permute-start.5 = (bf16[1040,128]{1,0:T(8,128)(2,1)S(1)}, bf16[1040,128]{1,0:T(8,128)(2,1)S(1)}, u32[]{:S(2)}, u32[]{:S(2)}) collective-permute-start(bf16[1040,128]{1,0:T(8,128)(2,1)S(1)} %get-tuple-element.53), channel_id=1, source_target_pairs={{0,24},{4,28},{8,16},{12,20},{16,8},{20,12},{24,0},{28,4},{1,25},{... | collective-permute-start | bytes 798728 | tf_op jit(solution)/shard_map/ppermute | solution.py:375
  21.2 2.8 %collective-permute-done.1.refs_4_ = bf16[1040,128]{1,0:T(8,128)(2,1)S(1)} collective-permute-done((bf16[1040,128]{1,0:T(8,128)(2,1)S(1)}, bf16[1040,128]{1,0:T(8,128)(2,1)S(1)}, u32[]{:S(2)}, u32[]{:S(2)}) %collective-permute-start.1) | collective-permute-done | bytes 266272 | tf_op jit(solution)/shard_map/ppermute | solution.py:375
  24.0 1.7 %collective-permute-start.6 = (bf16[1040,128]{1,0:T(8,128)(2,1)S(1)}, bf16[1040,128]{1,0:T(8,128)(2,1)S(1)}, u32[]{:S(2)}, u32[]{:S(2)}) collective-permute-start(bf16[1040,128]{1,0:T(8,128)(2,1)S(1)} %get-tuple-element.54), channel_id=1, source_target_pairs={{0,28},{4,24},{8,20},{12,16},{16,12},{20,8},{24,4},{28,0},{1,29},{... | collective-permute-start | bytes 798728 | tf_op jit(solution)/shard_map/ppermute | solution.py:375
  25.7 3.5 %collective-permute-done.2.refs_5_ = bf16[1040,128]{1,0:T(8,128)(2,1)S(1)} collective-permute-done((bf16[1040,128]{1,0:T(8,128)(2,1)S(1)}, bf16[1040,128]{1,0:T(8,128)(2,1)S(1)}, u32[]{:S(2)}, u32[]{:S(2)}) %collective-permute-start.2) | collective-permute-done | bytes 266272 | tf_op jit(solution)/shard_map/ppermute | solution.py:375
  29.2 1.9 %collective-permute-start.9 = (bf16[1040,128]{1,0:T(8,128)(2,1)S(1)}, bf16[1040,128]{1,0:T(8,128)(2,1)S(1)}, u32[]{:S(2)}, u32[]{:S(2)}) collective-permute-start(bf16[1040,128]{1,0:T(8,128)(2,1)S(1)} %get-tuple-element.59), channel_id=1, source_target_pairs={{0,12},{4,8},{8,4},{12,0},{16,28},{20,24},{24,20},{28,16},{1,13},{... | collective-permute-start | bytes 798728 | tf_op jit(solution)/shard_map/ppermute | solution.py:375
  31.1 1.8 %collective-permute-start.10 = (bf16[1040,128]{1,0:T(8,128)(2,1)S(1)}, bf16[1040,128]{1,0:T(8,128)(2,1)S(1)}, u32[]{:S(2)}, u32[]{:S(2)}) collective-permute-start(bf16[1040,128]{1,0:T(8,128)(2,1)S(1)} %get-tuple-element.60), channel_id=1, source_target_pairs={{0,16},{4,20},{8,24},{12,28},{16,0},{20,4},{24,8},{28,12},{1,17},{... | collective-permute-start | bytes 798728 | tf_op jit(solution)/shard_map/ppermute | solution.py:375
  32.9 7.2 %collective-permute-done.4.refs_7_ = bf16[1040,128]{1,0:T(8,128)(2,1)S(1)} collective-permute-done((bf16[1040,128]{1,0:T(8,128)(2,1)S(1)}, bf16[1040,128]{1,0:T(8,128)(2,1)S(1)}, u32[]{:S(2)}, u32[]{:S(2)}) %collective-permute-start.4) | collective-permute-done | bytes 266272 | tf_op jit(solution)/shard_map/ppermute | solution.py:375
  40.1 2.5 %collective-permute-start.11 = (bf16[1040,128]{1,0:T(8,128)(2,1)S(1)}, bf16[1040,128]{1,0:T(8,128)(2,1)S(1)}, u32[]{:S(2)}, u32[]{:S(2)}) collective-permute-start(bf16[1040,128]{1,0:T(8,128)(2,1)S(1)} %get-tuple-element.61), channel_id=1, source_target_pairs={{0,20},{4,16},{8,28},{12,24},{16,4},{20,0},{24,12},{28,8},{1,21},{... | collective-permute-start | bytes 798728 | tf_op jit(solution)/shard_map/ppermute | solution.py:375
  44.1 18.5 %attend.2 = (bf16[1024,128]{1,0:T(8,128)(2,1)S(1)}, bf16[1024,128]{1,0:T(8,128)(2,1)S(1)}, bf16[1024,128]{1,0:T(8,128)(2,1)S(1)}, bf16[1024,128]{1,0:T(8,128)(2,...) custom-call(f32[16]{0:T(128)S(1)} %copy-done.5, ...), custom_call_target="tpu_custom_call" | custom-call | flops 1342177280 | bytes 4194304 | tf_op jit(solution)/shard_map/attend/pallas_call | solution.py:325
  62.6 2.2 %collective-permute-done.11.refs_7_ = bf16[1040,128]{1,0:T(8,128)(2,1)S(1)} collective-permute-done((bf16[1040,128]{1,0:T(8,128)(2,1)S(1)}, bf16[1040,128]{1,0:T(8,128)(2,1)S(1)}, u32[]{:S(2)}, u32[]{:S(2)}) %collective-permute-start.11) | collective-permute-done | bytes 266272 | tf_op jit(solution)/shard_map/ppermute | solution.py:375
  64.8 18.7 %attend.3 = (bf16[1024,128]{1,0:T(8,128)(2,1)S(1)}, bf16[1024,128]{1,0:T(8,128)(2,1)S(1)}, bf16[1024,128]{1,0:T(8,128)(2,1)S(1)}, bf16[1024,128]{1,0:T(8,128)(2,...) custom-call(f32[16]{0:T(128)S(1)} %copy-done.5, ...), custom_call_target="tpu_custom_call" | custom-call | flops 1342177280 | bytes 4194304 | tf_op jit(solution)/shard_map/attend/pallas_call | solution.py:325
  83.7 1.5 collective-permute-start.15
  85.9 1.7 %collective-permute-start.28 = (f32[1,128]{1,0:T(1,128)S(1)}, f32[1,128]{1,0:T(1,128)S(1)}, u32[]{:S(2)}, u32[]{:S(2)}) collective-permute-start(f32[1,128]{1,0:T(1,128)S(1)} %get-tuple-element.88), channel_id=1, source_target_pairs={{0,1},{1,0},{2,3},{3,2},{4,5},{5,4},{6,7},{7,6},{8,9},{9,8},{10,11... | collective-permute-start | bytes 1544 | tf_op jit(solution)/shard_map/ppermute | solution.py:375
  87.6 1.8 %collective-permute-done.28 = f32[1,128]{1,0:T(1,128)S(1)} collective-permute-done((f32[1,128]{1,0:T(1,128)S(1)}, f32[1,128]{1,0:T(1,128)S(1)}, u32[]{:S(2)}, u32[]{:S(2)}) %collective-permute-start.28) | collective-permute-done | bytes 544 | tf_op jit(solution)/shard_map/ppermute | solution.py:375
  89.4 2.6 %collective-permute-start.29 = (f32[1,128]{1,0:T(1,128)S(1)}, f32[1,128]{1,0:T(1,128)S(1)}, u32[]{:S(2)}, u32[]{:S(2)}) collective-permute-start(f32[1,128]{1,0:T(1,128)S(1)} %add.15), channel_id=1, source_target_pairs={{0,2},{1,3},{2,0},{3,1},{4,6},{5,7},{6,4},{7,5},{8,10},{9,11},{10,... | collective-permute-start | bytes 1544 | tf_op jit(solution)/shard_map/ppermute | solution.py:375
  92.0 1.9 %collective-permute-done.29 = f32[1,128]{1,0:T(1,128)S(1)} collective-permute-done((f32[1,128]{1,0:T(1,128)S(1)}, f32[1,128]{1,0:T(1,128)S(1)}, u32[]{:S(2)}, u32[]{:S(2)}) %collective-permute-start.29) | collective-permute-done | bytes 544 | tf_op jit(solution)/shard_map/ppermute | solution.py:375
  95.0 1.5 collective-permute-start.31
  96.5 2.0 %collective-permute-done.31 = f32[1,128]{1,0:T(1,128)S(1)} collective-permute-done((f32[1,128]{1,0:T(1,128)S(1)}, f32[1,128]{1,0:T(1,128)S(1)}, u32[]{:S(2)}, u32[]{:S(2)}) %collective-permute-start.31) | collective-permute-done | bytes 544 | tf_op jit(solution)/shard_map/ppermute | solution.py:375
  99.1 3.0 %collective-permute-done.32 = f32[1,128]{1,0:T(1,128)S(1)} collective-permute-done((f32[1,128]{1,0:T(1,128)S(1)}, f32[1,128]{1,0:T(1,128)S(1)}, u32[]{:S(2)}, u32[]{:S(2)}) %collective-permute-start.32) | collective-permute-done | bytes 544 | tf_op jit(solution)/shard_map/ppermute | solution.py:375
  102.6 2.5 %collective-permute-start.25 = (bf16[1024,128]{1,0:T(8,128)(2,1)S(1)}, bf16[1024,128]{1,0:T(8,128)(2,1)S(1)}, u32[]{:S(2)}, u32[]{:S(2)}) collective-permute-start(bf16[1024,128]{1,0:T(8,128)(2,1)S(1)} %get-tuple-element.77), channel_id=1, source_target_pairs={{0,20},{4,16},{8,28},{12,24},{16,4},{20,0},{24,12},{28,8},{1,21},{... | collective-permute-start | bytes 786440 | tf_op jit(solution)/shard_map/ppermute | solution.py:375
  106.5 4.1 %collective-permute-done.23.refs_3_ = bf16[1024,128]{1,0:T(8,128)(2,1)S(1)} collective-permute-done((bf16[1024,128]{1,0:T(8,128)(2,1)S(1)}, bf16[1024,128]{1,0:T(8,128)(2,1)S(1)}, u32[]{:S(2)}, u32[]{:S(2)}) %collective-permute-start.23) | collective-permute-done | bytes 262176 | tf_op jit(solution)/shard_map/ppermute | solution.py:375
  111.2 17.5 %collective-permute-done.25.refs_5_ = bf16[1024,128]{1,0:T(8,128)(2,1)S(1)} collective-permute-done((bf16[1024,128]{1,0:T(8,128)(2,1)S(1)}, bf16[1024,128]{1,0:T(8,128)(2,1)S(1)}, u32[]{:S(2)}, u32[]{:S(2)}) %collective-permute-start.25) | collective-permute-done | bytes 262176 | tf_op jit(solution)/shard_map/ppermute | solution.py:375
  128.7 1.7 %collective-permute-start.19 = (bf16[1024,128]{1,0:T(8,128)(2,1)S(1)}, bf16[1024,128]{1,0:T(8,128)(2,1)S(1)}, u32[]{:S(2)}, u32[]{:S(2)}) collective-permute-start(bf16[1024,128]{1,0:T(8,128)(2,1)S(1)} %get-tuple-element.70), channel_id=1, source_target_pairs={{0,24},{4,28},{8,16},{12,20},{16,8},{20,12},{24,0},{28,4},{1,25},{... | collective-permute-start | bytes 786440 | tf_op jit(solution)/shard_map/ppermute | solution.py:375
  132.1 1.8 %unpack.2 = (bf16[1,256,2048]{2,1,0:T(8,128)(2,1)}, bf16[1,256,2048]{2,1,0:T(8,128)(2,1)}, bf16[1,256,2048]{2,1,0:T(8,128)(2,1)}, bf16[1,256,2048]{2,1,0:T(8,128)(2,1)}) custom-call(bf16[1024,128]{1,0:T(8,128)(2,1)S(1)} %get-tuple-element.72.refs_0_, bf16[1024,128]{1,0:T(8,128)(2,1)S(1)} %collective-permute-done.21.refs_1_, ...), custom_call_target="tpu_custom_call" | custom-call | bytes 4194304 | tf_op jit(solution)/shard_map/unpack/pallas_call | solution.py:120
  133.9 10.5 %collective-permute-done.17.refs_4_ = bf16[1024,128]{1,0:T(8,128)(2,1)S(1)} collective-permute-done((bf16[1024,128]{1,0:T(8,128)(2,1)S(1)}, bf16[1024,128]{1,0:T(8,128)(2,1)S(1)}, u32[]{:S(2)}, u32[]{:S(2)}) %collective-permute-start.17) | collective-permute-done | bytes 262176 | tf_op jit(solution)/shard_map/ppermute | solution.py:375
  144.4 6.2 %collective-permute-done.18.refs_5_ = bf16[1024,128]{1,0:T(8,128)(2,1)S(1)} collective-permute-done((bf16[1024,128]{1,0:T(8,128)(2,1)S(1)}, bf16[1024,128]{1,0:T(8,128)(2,1)S(1)}, u32[]{:S(2)}, u32[]{:S(2)}) %collective-permute-start.18) | collective-permute-done | bytes 262176 | tf_op jit(solution)/shard_map/ppermute | solution.py:375
  150.6 1.8 %unpack.3 = (bf16[1,256,2048]{2,1,0:T(8,128)(2,1)}, bf16[1,256,2048]{2,1,0:T(8,128)(2,1)}, bf16[1,256,2048]{2,1,0:T(8,128)(2,1)}, bf16[1,256,2048]{2,1,0:T(8,128)(2,1)}) custom-call(bf16[1024,128]{1,0:T(8,128)(2,1)S(1)} %get-tuple-element.64.refs_0_, ...), custom_call_target="tpu_custom_call", output_to_operand_aliasing={{0}: (8, {}), {1}: (9, {}), {2}: (10, {}), {3}: (11, {})} | custom-call | bytes 4194304 | tf_op jit(solution)/shard_map/unpack/pallas_call | solution.py:120
  (59 shorter events, 16.4 us)
Async XLA Ops:
  8.0 7.3 %collective-permute-start.7 = (bf16[1040,128]{1,0:T(8,128)(2,1)S(1)}, bf16[1040,128]{1,0:T(8,128)(2,1)S(1)}, u32[]{:S(2)}, u32[]{:S(2)}) collective-permute-start(bf16[1040,128]{1,0:T(8,128)(2,1)S(1)} %get-tuple-element.57), channel_id=1, source_target_pairs={{0,4},{4,0},{8,12},{12,8},{16,20},{20,16},{24,28},{28,24},{1,5},{5... | collective-permute-start | bytes 798728 | tf_op jit(solution)/shard_map/ppermute | solution.py:375
  8.5 9.8 %collective-permute-start.8 = (bf16[1040,128]{1,0:T(8,128)(2,1)S(1)}, bf16[1040,128]{1,0:T(8,128)(2,1)S(1)}, u32[]{:S(2)}, u32[]{:S(2)}) collective-permute-start(bf16[1040,128]{1,0:T(8,128)(2,1)S(1)} %get-tuple-element.58), channel_id=1, source_target_pairs={{0,8},{4,12},{8,0},{12,4},{16,24},{20,28},{24,16},{28,20},{1,9},{5... | collective-permute-start | bytes 798728 | tf_op jit(solution)/shard_map/ppermute | solution.py:375
  13.3 5.7 %collective-permute-start = (bf16[1040,128]{1,0:T(8,128)(2,1)S(1)}, bf16[1040,128]{1,0:T(8,128)(2,1)S(1)}, u32[]{:S(2)}, u32[]{:S(2)}) collective-permute-start(bf16[1040,128]{1,0:T(8,128)(2,1)S(1)} %get-tuple-element.48), channel_id=1, source_target_pairs={{0,4},{4,0},{8,12},{12,8},{16,20},{20,16},{24,28},{28,24},{1,5},{5... | collective-permute-start | bytes 798728 | tf_op jit(solution)/shard_map/ppermute | solution.py:375
  13.6 10.4 %collective-permute-start.1 = (bf16[1040,128]{1,0:T(8,128)(2,1)S(1)}, bf16[1040,128]{1,0:T(8,128)(2,1)S(1)}, u32[]{:S(2)}, u32[]{:S(2)}) collective-permute-start(bf16[1040,128]{1,0:T(8,128)(2,1)S(1)} %get-tuple-element.49), channel_id=1, source_target_pairs={{0,8},{4,12},{8,0},{12,4},{16,24},{20,28},{24,16},{28,20},{1,9},{5... | collective-permute-start | bytes 798728 | tf_op jit(solution)/shard_map/ppermute | solution.py:375
  13.8 15.3 %collective-permute-start.2 = (bf16[1040,128]{1,0:T(8,128)(2,1)S(1)}, bf16[1040,128]{1,0:T(8,128)(2,1)S(1)}, u32[]{:S(2)}, u32[]{:S(2)}) collective-permute-start(bf16[1040,128]{1,0:T(8,128)(2,1)S(1)} %get-tuple-element.50), channel_id=1, source_target_pairs={{0,12},{4,8},{8,4},{12,0},{16,28},{20,24},{24,20},{28,16},{1,13},{... | collective-permute-start | bytes 798728 | tf_op jit(solution)/shard_map/ppermute | solution.py:375
  15.3 15.8 %collective-permute-start.3 = (bf16[1040,128]{1,0:T(8,128)(2,1)S(1)}, bf16[1040,128]{1,0:T(8,128)(2,1)S(1)}, u32[]{:S(2)}, u32[]{:S(2)}) collective-permute-start(bf16[1040,128]{1,0:T(8,128)(2,1)S(1)} %get-tuple-element.51), channel_id=1, source_target_pairs={{0,16},{4,20},{8,24},{12,28},{16,0},{20,4},{24,8},{28,12},{1,17},{... | collective-permute-start | bytes 798728 | tf_op jit(solution)/shard_map/ppermute | solution.py:375
  18.3 21.8 %collective-permute-start.4 = (bf16[1040,128]{1,0:T(8,128)(2,1)S(1)}, bf16[1040,128]{1,0:T(8,128)(2,1)S(1)}, u32[]{:S(2)}, u32[]{:S(2)}) collective-permute-start(bf16[1040,128]{1,0:T(8,128)(2,1)S(1)} %get-tuple-element.52), channel_id=1, source_target_pairs={{0,20},{4,16},{8,28},{12,24},{16,4},{20,0},{24,12},{28,8},{1,21},{... | collective-permute-start | bytes 798728 | tf_op jit(solution)/shard_map/ppermute | solution.py:375
  19.1 23.5 %collective-permute-start.5 = (bf16[1040,128]{1,0:T(8,128)(2,1)S(1)}, bf16[1040,128]{1,0:T(8,128)(2,1)S(1)}, u32[]{:S(2)}, u32[]{:S(2)}) collective-permute-start(bf16[1040,128]{1,0:T(8,128)(2,1)S(1)} %get-tuple-element.53), channel_id=1, source_target_pairs={{0,24},{4,28},{8,16},{12,20},{16,8},{20,12},{24,0},{28,4},{1,25},{... | collective-permute-start | bytes 798728 | tf_op jit(solution)/shard_map/ppermute | solution.py:375
  24.0 18.6 %collective-permute-start.6 = (bf16[1040,128]{1,0:T(8,128)(2,1)S(1)}, bf16[1040,128]{1,0:T(8,128)(2,1)S(1)}, u32[]{:S(2)}, u32[]{:S(2)}) collective-permute-start(bf16[1040,128]{1,0:T(8,128)(2,1)S(1)} %get-tuple-element.54), channel_id=1, source_target_pairs={{0,28},{4,24},{8,20},{12,16},{16,12},{20,8},{24,4},{28,0},{1,29},{... | collective-permute-start | bytes 798728 | tf_op jit(solution)/shard_map/ppermute | solution.py:375
  29.2 33.4 %collective-permute-start.9 = (bf16[1040,128]{1,0:T(8,128)(2,1)S(1)}, bf16[1040,128]{1,0:T(8,128)(2,1)S(1)}, u32[]{:S(2)}, u32[]{:S(2)}) collective-permute-start(bf16[1040,128]{1,0:T(8,128)(2,1)S(1)} %get-tuple-element.59), channel_id=1, source_target_pairs={{0,12},{4,8},{8,4},{12,0},{16,28},{20,24},{24,20},{28,16},{1,13},{... | collective-permute-start | bytes 798728 | tf_op jit(solution)/shard_map/ppermute | solution.py:375
  31.1 31.6 %collective-permute-start.10 = (bf16[1040,128]{1,0:T(8,128)(2,1)S(1)}, bf16[1040,128]{1,0:T(8,128)(2,1)S(1)}, u32[]{:S(2)}, u32[]{:S(2)}) collective-permute-start(bf16[1040,128]{1,0:T(8,128)(2,1)S(1)} %get-tuple-element.60), channel_id=1, source_target_pairs={{0,16},{4,20},{8,24},{12,28},{16,0},{20,4},{24,8},{28,12},{1,17},{... | collective-permute-start | bytes 798728 | tf_op jit(solution)/shard_map/ppermute | solution.py:375
  40.1 24.7 %collective-permute-start.11 = (bf16[1040,128]{1,0:T(8,128)(2,1)S(1)}, bf16[1040,128]{1,0:T(8,128)(2,1)S(1)}, u32[]{:S(2)}, u32[]{:S(2)}) collective-permute-start(bf16[1040,128]{1,0:T(8,128)(2,1)S(1)} %get-tuple-element.61), channel_id=1, source_target_pairs={{0,20},{4,16},{8,28},{12,24},{16,4},{20,0},{24,12},{28,8},{1,21},{... | collective-permute-start | bytes 798728 | tf_op jit(solution)/shard_map/ppermute | solution.py:375
  42.6 22.2 %collective-permute-start.12 = (bf16[1040,128]{1,0:T(8,128)(2,1)S(1)}, bf16[1040,128]{1,0:T(8,128)(2,1)S(1)}, u32[]{:S(2)}, u32[]{:S(2)}) collective-permute-start(bf16[1040,128]{1,0:T(8,128)(2,1)S(1)} %get-tuple-element.62), channel_id=1, source_target_pairs={{0,24},{4,28},{8,16},{12,20},{16,8},{20,12},{24,0},{28,4},{1,25},{... | collective-permute-start | bytes 798728 | tf_op jit(solution)/shard_map/ppermute | solution.py:375
  42.6 22.2 %collective-permute-start.13 = (bf16[1040,128]{1,0:T(8,128)(2,1)S(1)}, bf16[1040,128]{1,0:T(8,128)(2,1)S(1)}, u32[]{:S(2)}, u32[]{:S(2)}) collective-permute-start(bf16[1040,128]{1,0:T(8,128)(2,1)S(1)} %get-tuple-element.63), channel_id=1, source_target_pairs={{0,28},{4,24},{8,20},{12,16},{16,12},{20,8},{24,4},{28,0},{1,29},{... | collective-permute-start | bytes 798728 | tf_op jit(solution)/shard_map/ppermute | solution.py:375
  83.5 18.6 %collective-permute-start.14 = (bf16[1024,128]{1,0:T(8,128)(2,1)S(1)}, bf16[1024,128]{1,0:T(8,128)(2,1)S(1)}, u32[]{:S(2)}, u32[]{:S(2)}) collective-permute-start(bf16[1024,128]{1,0:T(8,128)(2,1)S(1)} %get-tuple-element.65), channel_id=1, source_target_pairs={{0,4},{4,0},{8,12},{12,8},{16,20},{20,16},{24,28},{28,24},{1,5},{5... | collective-permute-start | bytes 786440 | tf_op jit(solution)/shard_map/ppermute | solution.py:375
  83.7 18.9 %collective-permute-start.15 = (bf16[1024,128]{1,0:T(8,128)(2,1)S(1)}, bf16[1024,128]{1,0:T(8,128)(2,1)S(1)}, u32[]{:S(2)}, u32[]{:S(2)}) collective-permute-start(bf16[1024,128]{1,0:T(8,128)(2,1)S(1)} %get-tuple-element.66), channel_id=1, source_target_pairs={{0,8},{4,12},{8,0},{12,4},{16,24},{20,28},{24,16},{28,20},{1,9},{5... | collective-permute-start | bytes 786440 | tf_op jit(solution)/shard_map/ppermute | solution.py:375
  85.2 19.9 %collective-permute-start.21 = (bf16[1024,128]{1,0:T(8,128)(2,1)S(1)}, bf16[1024,128]{1,0:T(8,128)(2,1)S(1)}, u32[]{:S(2)}, u32[]{:S(2)}) collective-permute-start(bf16[1024,128]{1,0:T(8,128)(2,1)S(1)} %get-tuple-element.73), channel_id=1, source_target_pairs={{0,4},{4,0},{8,12},{12,8},{16,20},{20,16},{24,28},{28,24},{1,5},{5... | collective-permute-start | bytes 786440 | tf_op jit(solution)/shard_map/ppermute | solution.py:375
  85.4 20.2 %collective-permute-start.22 = (bf16[1024,128]{1,0:T(8,128)(2,1)S(1)}, bf16[1024,128]{1,0:T(8,128)(2,1)S(1)}, u32[]{:S(2)}, u32[]{:S(2)}) collective-permute-start(bf16[1024,128]{1,0:T(8,128)(2,1)S(1)} %get-tuple-element.74), channel_id=1, source_target_pairs={{0,8},{4,12},{8,0},{12,4},{16,24},{20,28},{24,16},{28,20},{1,9},{5... | collective-permute-start | bytes 786440 | tf_op jit(solution)/shard_map/ppermute | solution.py:375
  85.9 3.5 %collective-permute-start.28 = (f32[1,128]{1,0:T(1,128)S(1)}, f32[1,128]{1,0:T(1,128)S(1)}, u32[]{:S(2)}, u32[]{:S(2)}) collective-permute-start(f32[1,128]{1,0:T(1,128)S(1)} %get-tuple-element.88), channel_id=1, source_target_pairs={{0,1},{1,0},{2,3},{3,2},{4,5},{5,4},{6,7},{7,6},{8,9},{9,8},{10,11... | collective-permute-start | bytes 1544 | tf_op jit(solution)/shard_map/ppermute | solution.py:375
  89.4 4.4 %collective-permute-start.29 = (f32[1,128]{1,0:T(1,128)S(1)}, f32[1,128]{1,0:T(1,128)S(1)}, u32[]{:S(2)}, u32[]{:S(2)}) collective-permute-start(f32[1,128]{1,0:T(1,128)S(1)} %add.15), channel_id=1, source_target_pairs={{0,2},{1,3},{2,0},{3,1},{4,6},{5,7},{6,4},{7,5},{8,10},{9,11},{10,... | collective-permute-start | bytes 1544 | tf_op jit(solution)/shard_map/ppermute | solution.py:375
  95.0 3.5 %collective-permute-start.31 = (f32[1,128]{1,0:T(1,128)S(1)}, f32[1,128]{1,0:T(1,128)S(1)}, u32[]{:S(2)}, u32[]{:S(2)}) collective-permute-start(f32[1,128]{1,0:T(1,128)S(1)} %add.17), channel_id=1, source_target_pairs={{0,8},{4,12},{8,0},{12,4},{16,24},{20,28},{24,16},{28,20},{1,9},{5... | collective-permute-start | bytes 1544 | tf_op jit(solution)/shard_map/ppermute | solution.py:375
  98.6 3.5 %collective-permute-start.32 = (f32[1,128]{1,0:T(1,128)S(1)}, f32[1,128]{1,0:T(1,128)S(1)}, u32[]{:S(2)}, u32[]{:S(2)}) collective-permute-start(f32[1,128]{1,0:T(1,128)S(1)} %add.18), channel_id=1, source_target_pairs={{0,16},{4,20},{8,24},{12,28},{16,0},{20,4},{24,8},{28,12},{1,17},{... | collective-permute-start | bytes 1544 | tf_op jit(solution)/shard_map/ppermute | solution.py:375
  102.1 8.5 %collective-permute-start.23 = (bf16[1024,128]{1,0:T(8,128)(2,1)S(1)}, bf16[1024,128]{1,0:T(8,128)(2,1)S(1)}, u32[]{:S(2)}, u32[]{:S(2)}) collective-permute-start(bf16[1024,128]{1,0:T(8,128)(2,1)S(1)} %get-tuple-element.75), channel_id=1, source_target_pairs={{0,12},{4,8},{8,4},{12,0},{16,28},{20,24},{24,20},{28,16},{1,13},{... | collective-permute-start | bytes 786440 | tf_op jit(solution)/shard_map/ppermute | solution.py:375
  102.1 8.6 %collective-permute-start.24 = (bf16[1024,128]{1,0:T(8,128)(2,1)S(1)}, bf16[1024,128]{1,0:T(8,128)(2,1)S(1)}, u32[]{:S(2)}, u32[]{:S(2)}) collective-permute-start(bf16[1024,128]{1,0:T(8,128)(2,1)S(1)} %get-tuple-element.76), channel_id=1, source_target_pairs={{0,16},{4,20},{8,24},{12,28},{16,0},{20,4},{24,8},{28,12},{1,17},{... | collective-permute-start | bytes 786440 | tf_op jit(solution)/shard_map/ppermute | solution.py:375
  102.6 26.1 %collective-permute-start.25 = (bf16[1024,128]{1,0:T(8,128)(2,1)S(1)}, bf16[1024,128]{1,0:T(8,128)(2,1)S(1)}, u32[]{:S(2)}, u32[]{:S(2)}) collective-permute-start(bf16[1024,128]{1,0:T(8,128)(2,1)S(1)} %get-tuple-element.77), channel_id=1, source_target_pairs={{0,20},{4,16},{8,28},{12,24},{16,4},{20,0},{24,12},{28,8},{1,21},{... | collective-permute-start | bytes 786440 | tf_op jit(solution)/shard_map/ppermute | solution.py:375
  105.1 23.7 %collective-permute-start.26 = (bf16[1024,128]{1,0:T(8,128)(2,1)S(1)}, bf16[1024,128]{1,0:T(8,128)(2,1)S(1)}, u32[]{:S(2)}, u32[]{:S(2)}) collective-permute-start(bf16[1024,128]{1,0:T(8,128)(2,1)S(1)} %get-tuple-element.78), channel_id=1, source_target_pairs={{0,24},{4,28},{8,16},{12,20},{16,8},{20,12},{24,0},{28,4},{1,25},{... | collective-permute-start | bytes 786440 | tf_op jit(solution)/shard_map/ppermute | solution.py:375
  105.5 24.9 %collective-permute-start.27 = (bf16[1024,128]{1,0:T(8,128)(2,1)S(1)}, bf16[1024,128]{1,0:T(8,128)(2,1)S(1)}, u32[]{:S(2)}, u32[]{:S(2)}) collective-permute-start(bf16[1024,128]{1,0:T(8,128)(2,1)S(1)} %get-tuple-element.79), channel_id=1, source_target_pairs={{0,28},{4,24},{8,20},{12,16},{16,12},{20,8},{24,4},{28,0},{1,29},{... | collective-permute-start | bytes 786440 | tf_op jit(solution)/shard_map/ppermute | solution.py:375
  110.6 23.3 %collective-permute-start.16 = (bf16[1024,128]{1,0:T(8,128)(2,1)S(1)}, bf16[1024,128]{1,0:T(8,128)(2,1)S(1)}, u32[]{:S(2)}, u32[]{:S(2)}) collective-permute-start(bf16[1024,128]{1,0:T(8,128)(2,1)S(1)} %get-tuple-element.67), channel_id=1, source_target_pairs={{0,12},{4,8},{8,4},{12,0},{16,28},{20,24},{24,20},{28,16},{1,13},{... | collective-permute-start | bytes 786440 | tf_op jit(solution)/shard_map/ppermute | solution.py:375
  110.7 33.6 %collective-permute-start.17 = (bf16[1024,128]{1,0:T(8,128)(2,1)S(1)}, bf16[1024,128]{1,0:T(8,128)(2,1)S(1)}, u32[]{:S(2)}, u32[]{:S(2)}) collective-permute-start(bf16[1024,128]{1,0:T(8,128)(2,1)S(1)} %get-tuple-element.68), channel_id=1, source_target_pairs={{0,16},{4,20},{8,24},{12,28},{16,0},{20,4},{24,8},{28,12},{1,17},{... | collective-permute-start | bytes 786440 | tf_op jit(solution)/shard_map/ppermute | solution.py:375
  128.7 21.9 %collective-permute-start.18 = (bf16[1024,128]{1,0:T(8,128)(2,1)S(1)}, bf16[1024,128]{1,0:T(8,128)(2,1)S(1)}, u32[]{:S(2)}, u32[]{:S(2)}) collective-permute-start(bf16[1024,128]{1,0:T(8,128)(2,1)S(1)} %get-tuple-element.69), channel_id=1, source_target_pairs={{0,20},{4,16},{8,28},{12,24},{16,4},{20,0},{24,12},{28,8},{1,21},{... | collective-permute-start | bytes 786440 | tf_op jit(solution)/shard_map/ppermute | solution.py:375
  128.7 21.9 %collective-permute-start.19 = (bf16[1024,128]{1,0:T(8,128)(2,1)S(1)}, bf16[1024,128]{1,0:T(8,128)(2,1)S(1)}, u32[]{:S(2)}, u32[]{:S(2)}) collective-permute-start(bf16[1024,128]{1,0:T(8,128)(2,1)S(1)} %get-tuple-element.70), channel_id=1, source_target_pairs={{0,24},{4,28},{8,16},{12,20},{16,8},{20,12},{24,0},{28,4},{1,25},{... | collective-permute-start | bytes 786440 | tf_op jit(solution)/shard_map/ppermute | solution.py:375
  130.5 20.2 %collective-permute-start.20 = (bf16[1024,128]{1,0:T(8,128)(2,1)S(1)}, bf16[1024,128]{1,0:T(8,128)(2,1)S(1)}, u32[]{:S(2)}, u32[]{:S(2)}) collective-permute-start(bf16[1024,128]{1,0:T(8,128)(2,1)S(1)} %get-tuple-element.71), channel_id=1, source_target_pairs={{0,28},{4,24},{8,20},{12,16},{16,12},{20,8},{24,4},{28,0},{1,29},{... | collective-permute-start | bytes 786440 | tf_op jit(solution)/shard_map/ppermute | solution.py:375
  (7 other events, 6.8 us)

commit v2 on v1

v2 whole, which is shorter than its diff:
```python
import functools

import jax
import jax.numpy as jnp
from jax import lax
from jax.experimental import pallas as pl
from jax.experimental.pallas import tpu as pltpu
from jax.sharding import PartitionSpec as P

HD = 128
BLK = 128
RADIUS = 2
GROUP = 8
NOTE = 16
LOG2E = 1.4426950408889634
VMEM_LIMIT = 48 * 1024 * 1024
NT = (((1,), (1,)), ((), ()))
NN = (((1,), (0,)), ((), ()))
ANY = pl.BlockSpec(memory_space=pl.ANY)
SMEM = pl.BlockSpec(memory_space=pltpu.SMEM)
VMEM = pl.BlockSpec(memory_space=pltpu.VMEM)
PARAMS = pltpu.CompilerParams(vmem_limit_bytes=VMEM_LIMIT)

DIRECT = {
    "steps": (0, 2, 3, 4, 5, 6),
    "rows": (1, 1, 1, 1, 1, 2, 2),
    "sent": ((0, 0), (6, 0), (1, 0), (2, 0), (3, 0), (4, 0), (5, 0), (6, 1)),
    "arrived": ((0, 0), (6, 0), (1, 0), (2, 0), (3, 0), (4, 0), (5, 0), (5, 1)),
    "merged": ((1, 5),),
}
PAIRED = {
    "steps": (0, 2, 4, 6),
    "rows": (1, 2, 2, 2, 4),
    "sent": ((0, 0), (4, 0), (1, 0), (4, 1), (2, 0), (4, 2), (3, 0), (4, 3)),
    "arrived": ((0, 0), (4, 0), (1, 0), (1, 1), (2, 0), (2, 1), (3, 0), (3, 1)),
    "merged": ((1, 1), (2, 2), (3, 3)),
}


def bytes_cost(count):
    return pl.CostEstimate(flops=0, bytes_accessed=count, transcendentals=0)


def run_copies(copies):
    for copy in copies:
        copy.start()
    for copy in copies:
        copy.wait()


def pack_kernel(group, per_device, head, tokens, layout, awaited, *refs):
    adjacency, counts = refs[:2]
    sources, outs = refs[2:6], refs[6 + awaited : -5]
    slots_here, counts_here, note, sems, list_sems = refs[-5:]
    rank = lax.axis_index("seq")
    spot = lax.rem(rank, group)
    copies = []
    for k in range(group):
        n, row = layout[k]
        column = pl.multiple_of(((spot ^ k) * per_device + head) * HD, HD)
        for a, source in enumerate(sources):
            copies.append(
                pltpu.make_async_copy(
                    source.at[0, :, pl.ds(column, HD)],
                    outs[n].at[pl.ds(row + a * tokens, tokens)],
                    sems.at[k, a],
                )
            )
    for copy in copies:
        copy.start()
    if head == 0:
        run_copies(
            (
                pltpu.make_async_copy(adjacency, slots_here, list_sems.at[0]),
                pltpu.make_async_copy(counts, counts_here, list_sems.at[1]),
            )
        )
        own_blocks, slots = adjacency.shape[1:]
        rows = lax.broadcasted_iota(jnp.int32, note.shape, 0)
        lanes = lax.broadcasted_iota(jnp.int32, note.shape, 1)
        marks = jnp.zeros(note.shape, jnp.int32)
        for b in range(own_blocks):
            for j in range(slots):
                near = slots_here[0, b, j] - rank * own_blocks
                marks = jnp.where((rows == b) & (lanes == j), near, marks)
            marks = jnp.where((rows == b) & (lanes == slots), counts_here[0, b], marks)
        note[...] = marks.astype(jnp.float32)
        for out in outs:
            row = out.shape[0] // (4 * tokens) * 4 * tokens
            out[row : row + NOTE, :] = note[...].astype(jnp.bfloat16)
    for copy in copies:
        copy.wait()


def pack(adjacency, counts, sources, awaited, route, group, per_device, head):
    tokens = sources[0].shape[1]
    size = 4 * tokens
    layout = [(n, row * size) for n, row in route["sent"]]
    rows = [n * size for n in route["rows"]]
    if head == 0:
        rows = [n * (size + NOTE) for n in route["rows"][:-1]] + [rows[-1] + NOTE]
    return pl.pallas_call(
        functools.partial(
            pack_kernel, group, per_device, head, tokens, layout, len(awaited)
        ),
        out_shape=[jax.ShapeDtypeStruct((r, HD), jnp.bfloat16) for r in rows],
        in_specs=[ANY] * (6 + len(awaited)),
        out_specs=[VMEM] * len(rows),
        scratch_shapes=[
            pltpu.SMEM(adjacency.shape, jnp.int32),
            pltpu.SMEM(counts.shape, jnp.int32),
            pltpu.VMEM((NOTE, HD), jnp.float32),
            pltpu.SemaphoreType.DMA((group, 4)),
            pltpu.SemaphoreType.DMA((2,)),
        ],
        compiler_params=PARAMS,
        cost_estimate=bytes_cost(group * size * HD * 4),
        name="pack",
    )(adjacency, counts, *sources, *awaited)


def pass_kernel(*refs):
    pass


def after(awaited, arrays):
    return pl.pallas_call(
        pass_kernel,
        out_shape=[jax.ShapeDtypeStruct(x.shape, x.dtype) for x in arrays],
        in_specs=[ANY] * (len(arrays) + len(awaited)),
        out_specs=[ANY] * len(arrays),
        input_output_aliases={n: n for n in range(len(arrays))},
        compiler_params=PARAMS,
        cost_estimate=bytes_cost(0),
        name="after",
    )(*arrays, *awaited)


def merge_kernel(moves, *refs):
    swapped, outs, sems = refs[0], refs[-1 - len(moves) : -1], refs[-1]
    copies = []
    for n, parts in enumerate(moves):
        for i, (row, to, count) in enumerate(parts):
            copies.append(
                pltpu.make_async_copy(
                    swapped.at[pl.ds(row, count)], outs[n].at[pl.ds(to, count)], sems.at[n, i]
                )
            )
    run_copies(copies)


def merge(swapped, buffers, route, size):
    buffers = list(buffers)
    noted = swapped.shape[0] % size != 0
    moves = []
    for row, _ in route["merged"]:
        parts = [(row * size, size, size)]
        if noted:
            parts.append((route["rows"][-1] * size, 2 * size + NOTE, NOTE))
        moves.append(parts)
    held = [buffers[n] for _, n in route["merged"]]
    filled = pl.pallas_call(
        functools.partial(merge_kernel, moves),
        out_shape=[jax.ShapeDtypeStruct(x.shape, x.dtype) for x in held],
        in_specs=[VMEM] + [ANY] * len(held),
        out_specs=[ANY] * len(held),
        scratch_shapes=[pltpu.SemaphoreType.DMA((len(held), 2))],
        input_output_aliases={1 + n: n for n in range(len(held))},
        compiler_params=PARAMS,
        cost_estimate=bytes_cost(len(held) * size * HD * 4),
        name="merge",
    )(swapped, *held)
    for (_, n), x in zip(route["merged"], filled):
        buffers[n] = x
    return buffers


def unpack_kernel(group, per_device, head, tokens, count, layout, *refs):
    parcels, outs, sems = refs[:count], refs[-5:-1], refs[-1]
    spot = lax.rem(lax.axis_index("seq"), group)
    copies = []
    for k, (n, from_row) in enumerate(layout):
        column = pl.multiple_of(((spot ^ k) * per_device + head) * HD, HD)
        for a, out in enumerate(outs):
            copies.append(
                pltpu.make_async_copy(
                    parcels[n].at[pl.ds(from_row + a * tokens, tokens)],
                    out.at[0, :, pl.ds(column, HD)],
                    sems.at[k, a],
                )
            )
    run_copies(copies)


def unpack(parcels, outs, route, group, per_device, head):
    count = len(parcels)
    tokens = parcels[0].shape[0] // 4
    layout = [(n, row * 4 * tokens) for n, row in route["arrived"]]
    shape = jax.ShapeDtypeStruct((1, tokens, group * per_device * HD), jnp.bfloat16)
    return pl.pallas_call(
        functools.partial(unpack_kernel, group, per_device, head, tokens, count, layout),
        out_shape=[shape] * 4,
        in_specs=[VMEM] * count + [ANY] * len(outs),
        out_specs=[ANY] * 4,
        scratch_shapes=[pltpu.SemaphoreType.DMA((group, 4))],
        input_output_aliases={count + a: a for a in range(len(outs))},
        compiler_params=PARAMS,
        cost_estimate=bytes_cost(group * tokens * HD * 16),
        name="unpack",
    )(*parcels, *outs)


def attend_kernel(group, per_device, head, halo, slots, own_blocks, scale, route, *refs):
    sink, sink_in, marks_in = refs[:3]
    arriving, leaving = route
    count = len(arriving["rows"])
    parcels, refs = refs[3 : 3 + count], refs[3 + count :]
    if halo:
        halo_in, refs = refs[0], refs[1:]
    count = len(leaving["rows"])
    results, sink_out, marks = refs[:count], refs[count], refs[count + 1]
    refs = refs[count + 2 :]
    if halo:
        halo_out, refs = refs[0], refs[1:]
    kv, qd, notes, lists, kt, vt, diag, diag_back, scored, paired, acc, out = refs[:12]
    sink_acc, sems, list_sem, out_sems = refs[12:]

    blocks = own_blocks * group
    span = own_blocks * BLK
    edge = halo * BLK
    window = blocks + 2 * halo
    spot = lax.rem(lax.axis_index("seq"), group)
    number = spot * per_device + head
    note_copies, copies = [], []
    for k, (n, row) in enumerate(arriving["arrived"] if head == 0 else ()):
        row = arriving["rows"][n] * 4 * span + row * NOTE
        note_copies.append(
            pltpu.make_async_copy(
                parcels[n].at[pl.ds(row, NOTE)], notes.at[spot ^ k], sems.at[k, 4]
            )
        )
    for k in range(group):
        row = pl.multiple_of((spot ^ k) * span, span)
        targets = (
            kv.at[pl.ds(row + edge, span), pl.ds(0, HD)],
            kv.at[pl.ds(row + edge, span), pl.ds(HD, HD)],
            qd.at[pl.ds(row, span), pl.ds(0, HD)],
            qd.at[pl.ds(row, span), pl.ds(HD, HD)],
        )
        n, part = arriving["arrived"][k]
        from_row = part * 4 * span
        for a, target in enumerate(targets):
            copies.append(
                pltpu.make_async_copy(
                    parcels[n].at[pl.ds(from_row + a * span, span)], target, sems.at[k, a]
                )
            )
    if halo:
        copies.append(pltpu.make_async_copy(halo_in.at[0], kv.at[pl.ds(0, edge)], sems.at[group, 0]))
        copies.append(
            pltpu.make_async_copy(
                halo_in.at[1], kv.at[pl.ds(edge + blocks * BLK, edge)], sems.at[group, 1]
            )
        )
    for copy in note_copies + copies:
        copy.start()
    diag[...] = jnp.zeros_like(diag)
    diag_back[...] = jnp.zeros_like(diag_back)
    acc[...] = jnp.zeros_like(acc)
    sink_acc[...] = jnp.zeros_like(sink_acc)
    for copy in note_copies:
        copy.wait()
    if head == 0:
        for j in range(group):
            marks[pl.ds(j * own_blocks, own_blocks), :] = (
                notes[j].astype(jnp.float32).astype(jnp.int32)[:own_blocks]
            )
    else:
        marks[...] = marks_in[...]
    list_copy = pltpu.make_async_copy(marks, lists, list_sem)
    list_copy.start()
    for copy in copies:
        copy.wait()

    def turn(c, carry):
        rows = kv[pl.ds(pl.multiple_of(c * BLK, BLK), BLK), :]
        kt[c] = rows[:, :HD].T
        vt[c] = rows[:, HD:].T
        return carry

    lax.fori_loop(0, window, turn, 0)
    list_copy.wait()

    to_log2 = scale * LOG2E
    sink_log2 = sink[number] * LOG2E

    def folded(x, op):
        return functools.reduce(op, [x[r : r + 8] for r in range(0, x.shape[0], 8)])

    def one_block(b, carry):
        rows = pl.ds(pl.multiple_of(b * BLK, BLK), BLK)
        home = b // own_blocks * own_blocks + halo
        query = qd[rows, :HD]
        grad = qd[rows, HD:]
        diag[:BLK, :HD] = query
        diag[BLK:, HD:] = grad
        diag_back[:BLK, :HD] = grad
        diag_back[BLK:, HD:] = query

        def with_slots(live):
            at = [lists[b, j] + home for j in range(live)]
            key_rows = [pl.ds(pl.multiple_of(c * BLK, BLK), BLK) for c in at]
            weights = diag[...]
            top = None
            for j in range(live):
                both = lax.dot_general(kv[key_rows[j], :], weights, NT, preferred_element_type=jnp.float32)
                scored[j] = both
                part = folded(both[:, :BLK], jnp.maximum)
                top = part if top is None else jnp.maximum(top, part)
            top = jnp.maximum(jnp.max(top, axis=0, keepdims=True) * to_log2, sink_log2)
            total = jnp.zeros((8, BLK), jnp.float32)
            dotted = jnp.zeros((8, BLK), jnp.float32)
            for j in range(live):
                power = jnp.exp2(scored[j, :, :BLK] * to_log2 - top)
                scored[j, :, :BLK] = power
                total = total + folded(power, jnp.add)
                dotted = dotted + folded(power * scored[j, :, BLK:], jnp.add)
            sink_power = jnp.exp2(sink_log2 - top)
            inverse = 1.0 / (jnp.sum(total, axis=0, keepdims=True) + sink_power)
            delta = jnp.sum(dotted, axis=0, keepdims=True) * inverse
            sink_acc[...] += sink_power * inverse * delta
            weights = diag_back[...]
            for j in range(live):
                probs = scored[j, :, :BLK] * inverse
                dscores = probs * (scored[j, :, BLK:] - delta)
                pair = jnp.concatenate([probs, dscores], axis=1).astype(jnp.bfloat16)
                paired[pl.ds(j * BLK, BLK), :] = pair
                acc[key_rows[j], :] += lax.dot_general(
                    pair, weights, NN, preferred_element_type=jnp.float32
                )
            attended = lax.dot_general(
                jnp.concatenate([vt[c] for c in at], axis=1),
                paired[: live * BLK, :BLK],
                NN,
                preferred_element_type=jnp.float32,
            )
            query_grad = lax.dot_general(
                jnp.concatenate([kt[c] for c in at], axis=1),
                paired[: live * BLK, BLK:],
                NN,
                preferred_element_type=jnp.float32,
            )
            out[2, rows, :] = attended.astype(jnp.bfloat16).T
            out[3, rows, :] = (query_grad * scale).astype(jnp.bfloat16).T

        for live in range(1, slots + 1):
            pl.when(lists[b, slots] == live)(functools.partial(with_slots, live))
        return carry

    lax.fori_loop(0, blocks, one_block, 0)

    def finish(b, carry):
        rows = pl.ds(pl.multiple_of(b * BLK, BLK), BLK)
        from_rows = pl.ds(pl.multiple_of((b + halo) * BLK, BLK), BLK)
        out[0, rows, :] = acc[from_rows, :HD].astype(jnp.bfloat16)
        out[1, rows, :] = (acc[from_rows, HD:] * scale).astype(jnp.bfloat16)
        return carry

    lax.fori_loop(0, blocks, finish, 0)
    lanes = lax.broadcasted_iota(jnp.int32, (1, BLK), 1)
    sink_sum = jnp.sum(sink_acc[...], axis=1, keepdims=True)
    sink_out[...] = sink_in[...] - jnp.where(lanes == number, sink_sum, 0.0)
    copies = []
    for k in range(group):
        row = pl.multiple_of((spot ^ k) * span, span)
        n, part = leaving["sent"][k]
        to_row = part * 4 * span
        for a in range(4):
            copies.append(
                pltpu.make_async_copy(
                    out.at[a, pl.ds(row, span)],
                    results[n].at[pl.ds(to_row + a * span, span)],
                    out_sems.at[k, a],
                )
            )
    for copy in copies:
        copy.start()
    if halo:
        for side, row in ((0, 0), (1, edge + blocks * BLK)):
            halo_out[side, :, :HD] = acc[pl.ds(row, edge), :HD]
            halo_out[side, :, HD:] = acc[pl.ds(row, edge), HD:] * scale
    for copy in copies:
        copy.wait()


def attend(sink, sink_in, marks_in, parcels, halo_in, routes, group, per_device, head, halo, slots, own_blocks, scale):
    span = own_blocks * BLK
    edge = halo * BLK
    blocks = own_blocks * group
    window = blocks + 2 * halo
    out_shape = [
        jax.ShapeDtypeStruct((n * 4 * span, HD), jnp.bfloat16) for n in routes[1]["rows"]
    ]
    out_specs = [ANY] * len(out_shape) + [VMEM] * 2
    out_shape.append(jax.ShapeDtypeStruct((1, BLK), jnp.float32))
    out_shape.append(jax.ShapeDtypeStruct((blocks, HD), jnp.int32))
    extra = []
    if halo:
        extra = [halo_in]
        out_shape.append(jax.ShapeDtypeStruct((2, edge, 2 * HD), jnp.float32))
        out_specs.append(VMEM)
    return pl.pallas_call(
        functools.partial(
            attend_kernel, group, per_device, head, halo, slots, own_blocks, scale, routes
        ),
        out_shape=out_shape,
        in_specs=[SMEM, VMEM, VMEM] + [ANY] * (len(parcels) + len(extra)),
        out_specs=out_specs,
        scratch_shapes=[
            pltpu.VMEM((window * BLK, 2 * HD), jnp.bfloat16),
            pltpu.VMEM((blocks * BLK, 2 * HD), jnp.bfloat16),
            pltpu.VMEM((group, NOTE, HD), jnp.bfloat16),
            pltpu.SMEM((blocks, HD), jnp.int32),
            pltpu.VMEM((window, HD, BLK), jnp.bfloat16),
            pltpu.VMEM((window, HD, BLK), jnp.bfloat16),
            pltpu.VMEM((2 * BLK, 2 * HD), jnp.bfloat16),
            pltpu.VMEM((2 * BLK, 2 * HD), jnp.bfloat16),
            pltpu.VMEM((slots, BLK, 2 * BLK), jnp.float32),
            pltpu.VMEM((slots * BLK, 2 * BLK), jnp.bfloat16),
            pltpu.VMEM((window * BLK, 2 * HD), jnp.float32),
            pltpu.VMEM((4, blocks * BLK, HD), jnp.bfloat16),
            pltpu.VMEM((1, BLK), jnp.float32),
            pltpu.SemaphoreType.DMA((group + 1, 5)),
            pltpu.SemaphoreType.DMA,
            pltpu.SemaphoreType.DMA((group, 4)),
        ],
        compiler_params=PARAMS,
        cost_estimate=pl.CostEstimate(
            flops=blocks * slots * 64 * BLK * BLK * HD,
            bytes_accessed=blocks * BLK * HD * 16,
            transcendentals=blocks * slots * BLK * BLK,
        ),
        name="attend",
    )(sink, sink_in, marks_in, *parcels, *extra)


def local(queries, keys, values, out_grad, adjacency, counts, sink):
    seq = lax.axis_size("seq")
    group = min(seq, GROUP)
    groups = seq // group
    heads = sink.shape[0]
    per_device = heads // group
    slots = adjacency.shape[2]
    own_blocks = adjacency.shape[1]
    span = own_blocks * BLK
    size = 4 * span
    halo = RADIUS * own_blocks if groups > 1 else 0
    scale = HD ** (-0.5)
    spot = lax.rem(lax.axis_index("seq"), group)

    def swap(x, k, axis="seq"):
        return lax.ppermute(x, axis, [(i, i ^ k) for i in range(lax.axis_size(axis))])

    def between(buffers, route):
        pairs = zip(buffers[1:], route["steps"][1:])
        return [buffers[0]] + [swap(x, k) for x, k in pairs]

    def beside(x, step):
        route = [(i, i + step * group) for i in range(seq) if 0 <= i + step * group < seq]
        return lax.ppermute(x, "seq", route)

    def halos(parcels, route):
        stacked = jnp.stack(
            [parcels[n][row * size : (row + 1) * size] for n, row in route["arrived"]]
        )
        ends = []
        for side, step in ((group - RADIUS, 1), (0, -1)):
            near = [stacked[(side + r) ^ spot] for r in range(RADIUS)]
            near = [jnp.concatenate([x[:span], x[span : 2 * span]], axis=1) for x in near]
            ends.append(beside(jnp.concatenate(near, axis=0), step))
        return jnp.stack(ends)

    def add_halos(results, halo_grads, route):
        stacked = jnp.stack(
            [results[n][row * size : (row + 1) * size] for n, row in route["sent"]]
        )
        for side, step, half in ((group - RADIUS, -1, 0), (0, 1, 1)):
            grads = beside(halo_grads[half], step)
            for r in range(RADIUS):
                at = (side + r) ^ spot
                rows = stacked[at]
                more = grads[r * span : (r + 1) * span]
                more = jnp.concatenate([more[:, :HD], more[:, HD:]], axis=0)
                wide = rows[: 2 * span].astype(jnp.float32) + more
                rows = jnp.concatenate([wide.astype(jnp.bfloat16), rows[2 * span :]], axis=0)
                stacked = lax.dynamic_update_index_in_dim(stacked, rows, at, 0)
        results = list(results)
        for k, (n, row) in enumerate(route["sent"]):
            results[n] = results[n].at[row * size : (row + 1) * size].set(stacked[k])
        return results

    constrained = [
        pltpu.with_memory_space_constraint(x, pltpu.HBM)
        for x in (adjacency, counts, keys, values, queries, out_grad)
    ]
    adjacency, counts, *sources = constrained
    routes_out = [DIRECT] * (per_device - 1) + [PAIRED]

    arrived = []
    packed = []
    for head in range(per_device):
        packed = pack(
            adjacency, counts, sources, packed[:1], DIRECT, group, per_device, head
        )
        crossed = swap(packed[-1], 1)
        buffers = merge(crossed, packed[:-1], DIRECT, size)
        if head > 0:
            buffers[1:] = after(arrived[-1][1:-1], buffers[1:])
        arrived.append(between(buffers, DIRECT) + [crossed])

    sink_row = jnp.zeros((1, BLK), jnp.float32)
    marks = jnp.zeros((own_blocks * group, HD), jnp.int32)
    returned = []
    for head in range(per_device):
        routes = (DIRECT, routes_out[head])
        halo_in = halos(arrived[head], DIRECT) if halo else None
        done = attend(
            sink,
            sink_row,
            marks,
            arrived[head],
            halo_in,
            routes,
            group,
            per_device,
            head,
            halo,
            slots,
            own_blocks,
            scale,
        )
        count = len(routes[1]["rows"])
        results, sink_row, marks = list(done[:count]), done[count], done[count + 1]
        if halo:
            results = add_halos(results, done[count + 2], routes[1])
        if head < per_device - 1:
            results[1:] = after(arrived[head + 1][1:-1], results[1:])
        elif head > 0:
            *results[1:], sink_row = after(returned[-1][1:-1], results[1:] + [sink_row])
        crossed = swap(results[-1], 1)
        buffers = merge(crossed, results[:-1], routes[1], size)
        returned.append(between(buffers, routes[1]) + [crossed])
    outs = []
    for head in range(per_device):
        outs = unpack(returned[head], outs, routes_out[head], group, per_device, head)
    value_grad, key_grad, attended, query_grad = outs
    for axis in ("dp", "seq"):
        step = 1
        while step < lax.axis_size(axis):
            sink_row = sink_row + swap(sink_row, step, axis)
            step *= 2
    return attended, query_grad, key_grad, value_grad, sink_row[0, :heads]


def solution(mesh):
    tokens = P("dp", "seq", None)
    return jax.shard_map(
        local,
        mesh=mesh,
        in_specs=(tokens, tokens, tokens, tokens, tokens, P("dp", "seq"), P()),
        out_specs=(tokens, tokens, tokens, tokens, P()),
        check_vma=False,
    )
```

time: 153 us -> 121 us (0.79)
  waiting for transfers between devices: 65.5 us -> 39.4 us
  local copies, waits for them, and re-layouts: 6.17 us -> 1.17 us
  starting transfers between devices: 34.6 us -> 31.3 us
  Pallas kernels: 45.4 us -> 48 us
    ppermute x33 -> x27, waiting for transfers between devices: 65.5 us -> 39.4 us  [swap(): lax.ppermute(x, axis, [(i, i ^ k) for i in range(lax.axis_size(axis))])]
    unnamed x12 -> x2, local copies, waits for them, and re-layouts: 5.65 us -> 0.65 us
    pallas_call x2, Pallas kernels: 37.2 us -> 40.8 us  [attend(): pl.pallas_call(functools.partial(attend_kernel, group, per_device, head,...]
    ppermute x33 -> x27, starting transfers between devices: 34.6 us -> 31.3 us  [swap(): lax.ppermute(x, axis, [(i, i ^ k) for i in range(lax.axis_size(axis))])]
    pallas_call x4 -> x11, Pallas kernels: 8.17 us -> 7.25 us  [the longest x2 3.85 us: pack(): pl.pallas_call(functools.partial(pack_kernel, group, per_device, head, to...]
  transfers between devices with their start and end apart: 33 -> 27, of which waited for: 15 -> 9; matrix products, arithmetic and copies ran while one was open for 0% -> 0% of each run, Pallas kernels for 15% -> 37%
where the time goes in v2:
time: 121 us
  Pallas kernels  48 us (40%)
  waiting for transfers between devices  39.4 us (33%)
  starting transfers between devices  31.3 us (26%)
    pallas_call x2, Pallas kernels, attend(): pl.pallas_call(functools.partial(attend_kernel, group, per_device, head,...  40.8 us
    ppermute x27, waiting for transfers between devices, swap(): lax.ppermute(x, axis, [(i, i ^ k) for i in range(lax.axis_size(axis))])  39.4 us
    ppermute x27, starting transfers between devices, swap(): lax.ppermute(x, axis, [(i, i ^ k) for i in range(lax.axis_size(axis))])  31.3 us
    pallas_call x2, Pallas kernels, pack(): pl.pallas_call(functools.partial(pack_kernel, group, per_device, head, to...  3.85 us
    pallas_call x2, Pallas kernels, unpack(): pl.pallas_call(functools.partial(unpack_kernel, group, per_device, head,...  3.15 us
  transfers between devices with their start and end apart: 27, of which 9 were waited for; matrix products, arithmetic and copies ran while one was open for 0% of the time, Pallas kernels for 37%

profile of v2, /device:TPU:0, one launch (start us, length us, event | category | flops | bytes accessed | tf_op | source)
XLA Modules:
  0.0 120.7 jit_solution(14668453572731172422)
XLA Ops:
  0.6 1.9 %pack.2 = (bf16[1040,128]{1,0:T(8,128)(2,1)S(1)}, bf16[1040,128]{1,0:T(8,128)(2,1)S(1)}, bf16[1040,128]{1,0:T(8,128)(2,1)S(1)}, bf16[1040,128]{1,0:T(8,128)(2,1)...) custom-call(s32[1,2,8]{2,1,0:T(2,128)} %refs_0_.6, ...), custom_call_target="tpu_custom_call" | custom-call | bytes 4194304 | tf_op jit(solution)/shard_map/pack/pallas_call | solution.py:102
  3.1 1.9 %pack.3 = (bf16[1024,128]{1,0:T(8,128)(2,1)S(1)}, bf16[1024,128]{1,0:T(8,128)(2,1)S(1)}, bf16[1024,128]{1,0:T(8,128)(2,1)S(1)}, bf16[1024,128]{1,0:T(8,128)(2,1)...) custom-call(s32[1,2,8]{2,1,0:T(2,128)} %refs_0_.6, ...), custom_call_target="tpu_custom_call" | custom-call | bytes 4194304 | tf_op jit(solution)/shard_map/pack/pallas_call | solution.py:102
  5.2 4.0 %collective-permute-start.5 = (bf16[2080,128]{1,0:T(8,128)(2,1)S(1)}, bf16[2080,128]{1,0:T(8,128)(2,1)S(1)}, u32[]{:S(2)}, u32[]{:S(2)}) collective-permute-start(bf16[2080,128]{1,0:T(8,128)(2,1)S(1)} %merge.4), channel_id=1, source_target_pairs={{0,24},{4,28},{8,16},{12,20},{16,8},{20,12},{24,0},{28,4},{1,25},{... | collective-permute-start | bytes 1597448 | tf_op jit(solution)/shard_map/ppermute | solution.py:462
  9.2 0.5 collective-permute-start
  9.7 0.6 collective-permute-start.1
  10.8 1.9 %collective-permute-start.3 = (bf16[1040,128]{1,0:T(8,128)(2,1)S(1)}, bf16[1040,128]{1,0:T(8,128)(2,1)S(1)}, u32[]{:S(2)}, u32[]{:S(2)}) collective-permute-start(bf16[1040,128]{1,0:T(8,128)(2,1)S(1)} %get-tuple-element.65), channel_id=1, source_target_pairs={{0,20},{4,16},{8,28},{12,24},{16,4},{20,0},{24,12},{28,8},{1,21},{... | collective-permute-start | bytes 798728 | tf_op jit(solution)/shard_map/ppermute | solution.py:462
  12.7 15.7 %collective-permute-done.refs_4_.refs_5_ = bf16[1040,128]{1,0:T(8,128)(2,1)S(1)} collective-permute-done((bf16[1040,128]{1,0:T(8,128)(2,1)S(1)}, bf16[1040,128]{1,0:T(8,128)(2,1)S(1)}, u32[]{:S(2)}, u32[]{:S(2)}) %collective-permute-start) | collective-permute-done | bytes 266272 | tf_op jit(solution)/shard_map/ppermute | solution.py:462
  28.4 3.9 %collective-permute-done.1.refs_5_.refs_6_ = bf16[1040,128]{1,0:T(8,128)(2,1)S(1)} collective-permute-done((bf16[1040,128]{1,0:T(8,128)(2,1)S(1)}, bf16[1040,128]{1,0:T(8,128)(2,1)S(1)}, u32[]{:S(2)}, u32[]{:S(2)}) %collective-permute-start.1) | collective-permute-done | bytes 266272 | tf_op jit(solution)/shard_map/ppermute | solution.py:462
  32.2 0.6 collective-permute-done.3.refs_7_.refs_8_
  32.9 1.7 %collective-permute-start.7 = (bf16[1024,128]{1,0:T(8,128)(2,1)S(1)}, bf16[1024,128]{1,0:T(8,128)(2,1)S(1)}, u32[]{:S(2)}, u32[]{:S(2)}) collective-permute-start(bf16[1024,128]{1,0:T(8,128)(2,1)S(1)} %get-tuple-element.77), channel_id=1, source_target_pairs={{0,8},{4,12},{8,0},{12,4},{16,24},{20,28},{24,16},{28,20},{1,9},{5... | collective-permute-start | bytes 786440 | tf_op jit(solution)/shard_map/ppermute | solution.py:462
  34.5 1.5 %collective-permute-start.9 = (bf16[1024,128]{1,0:T(8,128)(2,1)S(1)}, bf16[1024,128]{1,0:T(8,128)(2,1)S(1)}, u32[]{:S(2)}, u32[]{:S(2)}) collective-permute-start(bf16[1024,128]{1,0:T(8,128)(2,1)S(1)} %get-tuple-element.79), channel_id=1, source_target_pairs={{0,16},{4,20},{8,24},{12,28},{16,0},{20,4},{24,8},{28,12},{1,17},{... | collective-permute-start | bytes 786440 | tf_op jit(solution)/shard_map/ppermute | solution.py:462
  36.4 2.6 %collective-permute-start.11 = (bf16[2048,128]{1,0:T(8,128)(2,1)S(1)}, bf16[2048,128]{1,0:T(8,128)(2,1)S(1)}, u32[]{:S(2)}, u32[]{:S(2)}) collective-permute-start(bf16[2048,128]{1,0:T(8,128)(2,1)S(1)} %get-tuple-element.81), channel_id=1, source_target_pairs={{0,24},{4,28},{8,16},{12,20},{16,8},{20,12},{24,0},{28,4},{1,25},{... | collective-permute-start | bytes 1572872 | tf_op jit(solution)/shard_map/ppermute | solution.py:462
  39.0 0.7 copy-done
  39.6 20.1 %attend.2 = (bf16[1024,128]{1,0:T(8,128)(2,1)S(1)}, bf16[1024,128]{1,0:T(8,128)(2,1)S(1)}, bf16[1024,128]{1,0:T(8,128)(2,1)S(1)}, bf16[1024,128]{1,0:T(8,128)(2,...) custom-call(f32[16]{0:T(128)S(1)} %copy-done, ...), custom_call_target="tpu_custom_call" | custom-call | flops 17179869184 | bytes 4194304 | tf_op jit(solution)/shard_map/attend/pallas_call | solution.py:412
  59.9 1.7 %collective-permute-start.12 = (bf16[1024,128]{1,0:T(8,128)(2,1)S(1)}, bf16[1024,128]{1,0:T(8,128)(2,1)S(1)}, u32[]{:S(2)}, u32[]{:S(2)}) collective-permute-start(bf16[1024,128]{1,0:T(8,128)(2,1)S(1)} %get-tuple-element.94), channel_id=1, source_target_pairs={{0,8},{4,12},{8,0},{12,4},{16,24},{20,28},{24,16},{28,20},{1,9},{5... | collective-permute-start | bytes 786440 | tf_op jit(solution)/shard_map/ppermute | solution.py:462
  61.8 1.6 %collective-permute-start.14 = (bf16[1024,128]{1,0:T(8,128)(2,1)S(1)}, bf16[1024,128]{1,0:T(8,128)(2,1)S(1)}, u32[]{:S(2)}, u32[]{:S(2)}) collective-permute-start(bf16[1024,128]{1,0:T(8,128)(2,1)S(1)} %get-tuple-element.96), channel_id=1, source_target_pairs={{0,16},{4,20},{8,24},{12,28},{16,0},{20,4},{24,8},{28,12},{1,17},{... | collective-permute-start | bytes 786440 | tf_op jit(solution)/shard_map/ppermute | solution.py:462
  63.5 2.6 %collective-permute-start.17 = (bf16[2048,128]{1,0:T(8,128)(2,1)S(1)}, bf16[2048,128]{1,0:T(8,128)(2,1)S(1)}, u32[]{:S(2)}, u32[]{:S(2)}) collective-permute-start(bf16[2048,128]{1,0:T(8,128)(2,1)S(1)} %merge.6), channel_id=1, source_target_pairs={{0,24},{4,28},{8,16},{12,20},{16,8},{20,12},{24,0},{28,4},{1,25},{... | collective-permute-start | bytes 1572872 | tf_op jit(solution)/shard_map/ppermute | solution.py:462
  66.1 20.6 %attend.3 = (bf16[1024,128]{1,0:T(8,128)(2,1)S(1)}, bf16[2048,128]{1,0:T(8,128)(2,1)S(1)}, bf16[2048,128]{1,0:T(8,128)(2,1)S(1)}, bf16[2048,128]{1,0:T(8,128)(2,...) custom-call(f32[16]{0:T(128)S(1)} %copy-done, ...), custom_call_target="tpu_custom_call" | custom-call | flops 17179869184 | bytes 4194304 | tf_op jit(solution)/shard_map/attend/pallas_call | solution.py:412
  87.0 2.6 %collective-permute-done.18.refs_0_.refs_4_ = bf16[4096,128]{1,0:T(8,128)(2,1)S(1)} collective-permute-done((bf16[4096,128]{1,0:T(8,128)(2,1)S(1)}, bf16[4096,128]{1,0:T(8,128)(2,1)S(1)}, u32[]{:S(2)}, u32[]{:S(2)}) %collective-permute-start.18) | collective-permute-done | bytes 1048608 | tf_op jit(solution)/shard_map/ppermute | solution.py:462
  89.7 1.5 %collective-permute-start.19 = (bf16[2048,128]{1,0:T(8,128)(2,1)S(1)}, bf16[2048,128]{1,0:T(8,128)(2,1)S(1)}, u32[]{:S(2)}, u32[]{:S(2)}) collective-permute-start(bf16[2048,128]{1,0:T(8,128)(2,1)S(1)} %get-tuple-element.104), channel_id=1, source_target_pairs={{0,8},{4,12},{8,0},{12,4},{16,24},{20,28},{24,16},{28,20},{1,9},{5... | collective-permute-start | bytes 1572872 | tf_op jit(solution)/shard_map/ppermute | solution.py:462
  91.2 1.5 %collective-permute-start.20 = (bf16[2048,128]{1,0:T(8,128)(2,1)S(1)}, bf16[2048,128]{1,0:T(8,128)(2,1)S(1)}, u32[]{:S(2)}, u32[]{:S(2)}) collective-permute-start(bf16[2048,128]{1,0:T(8,128)(2,1)S(1)} %get-tuple-element.105), channel_id=1, source_target_pairs={{0,16},{4,20},{8,24},{12,28},{16,0},{20,4},{24,8},{28,12},{1,17},{... | collective-permute-start | bytes 1572872 | tf_op jit(solution)/shard_map/ppermute | solution.py:462
  92.7 0.6 collective-permute-start.21
  93.3 1.5 %collective-permute-start.22 = (f32[1,128]{1,0:T(1,128)S(1)}, f32[1,128]{1,0:T(1,128)S(1)}, u32[]{:S(2)}, u32[]{:S(2)}) collective-permute-start(f32[1,128]{1,0:T(1,128)S(1)} %get-tuple-element.116), channel_id=1, source_target_pairs={{0,1},{1,0},{2,3},{3,2},{4,5},{5,4},{6,7},{7,6},{8,9},{9,8},{10,11... | collective-permute-start | bytes 1544 | tf_op jit(solution)/shard_map/ppermute | solution.py:462
  94.8 2.0 %collective-permute-done.22 = f32[1,128]{1,0:T(1,128)S(1)} collective-permute-done((f32[1,128]{1,0:T(1,128)S(1)}, f32[1,128]{1,0:T(1,128)S(1)}, u32[]{:S(2)}, u32[]{:S(2)}) %collective-permute-start.22) | collective-permute-done | bytes 544 | tf_op jit(solution)/shard_map/ppermute | solution.py:462
  96.8 2.5 %collective-permute-start.23 = (f32[1,128]{1,0:T(1,128)S(1)}, f32[1,128]{1,0:T(1,128)S(1)}, u32[]{:S(2)}, u32[]{:S(2)}) collective-permute-start(f32[1,128]{1,0:T(1,128)S(1)} %add.15), channel_id=1, source_target_pairs={{0,2},{1,3},{2,0},{3,1},{4,6},{5,7},{6,4},{7,5},{8,10},{9,11},{10,... | collective-permute-start | bytes 1544 | tf_op jit(solution)/shard_map/ppermute | solution.py:462
  99.4 1.9 %collective-permute-done.23 = f32[1,128]{1,0:T(1,128)S(1)} collective-permute-done((f32[1,128]{1,0:T(1,128)S(1)}, f32[1,128]{1,0:T(1,128)S(1)}, u32[]{:S(2)}, u32[]{:S(2)}) %collective-permute-start.23) | collective-permute-done | bytes 544 | tf_op jit(solution)/shard_map/ppermute | solution.py:462
  101.3 1.1 collective-permute-done.24
  102.4 1.4 %collective-permute-start.25 = (f32[1,128]{1,0:T(1,128)S(1)}, f32[1,128]{1,0:T(1,128)S(1)}, u32[]{:S(2)}, u32[]{:S(2)}) collective-permute-start(f32[1,128]{1,0:T(1,128)S(1)} %add.17), channel_id=1, source_target_pairs={{0,8},{4,12},{8,0},{12,4},{16,24},{20,28},{24,16},{28,20},{1,9},{5... | collective-permute-start | bytes 1544 | tf_op jit(solution)/shard_map/ppermute | solution.py:462
  103.8 11.2 %collective-permute-done.25 = f32[1,128]{1,0:T(1,128)S(1)} collective-permute-done((f32[1,128]{1,0:T(1,128)S(1)}, f32[1,128]{1,0:T(1,128)S(1)}, u32[]{:S(2)}, u32[]{:S(2)}) %collective-permute-start.25) | collective-permute-done | bytes 544 | tf_op jit(solution)/shard_map/ppermute | solution.py:462
  115.0 1.6 %collective-permute-start.26 = (f32[1,128]{1,0:T(1,128)S(1)}, f32[1,128]{1,0:T(1,128)S(1)}, u32[]{:S(2)}, u32[]{:S(2)}) collective-permute-start(f32[1,128]{1,0:T(1,128)S(1)} %add.18), channel_id=1, source_target_pairs={{0,16},{4,20},{8,24},{12,28},{16,0},{20,4},{24,8},{28,12},{1,17},{... | collective-permute-start | bytes 1544 | tf_op jit(solution)/shard_map/ppermute | solution.py:462
  116.6 1.6 %unpack.2 = (bf16[1,256,2048]{2,1,0:T(8,128)(2,1)}, bf16[1,256,2048]{2,1,0:T(8,128)(2,1)}, bf16[1,256,2048]{2,1,0:T(8,128)(2,1)}, bf16[1,256,2048]{2,1,0:T(8,128)(2,1)}) custom-call(bf16[1024,128]{1,0:T(8,128)(2,1)S(1)} %get-tuple-element.107.refs_0_, bf16[1024,128]{1,0:T(8,128)(2,1)S(1)} %collective-permute-done.12.refs_5_.refs_1_, ...), custom_call_target="tpu_custom_call" | custom-call | bytes 4194304 | tf_op jit(solution)/shard_map/unpack/pallas_call | solution.py:200
  119.1 1.6 %unpack.3 = (bf16[1,256,2048]{2,1,0:T(8,128)(2,1)}, bf16[1,256,2048]{2,1,0:T(8,128)(2,1)}, bf16[1,256,2048]{2,1,0:T(8,128)(2,1)}, bf16[1,256,2048]{2,1,0:T(8,128)(2,1)}) custom-call(bf16[1024,128]{1,0:T(8,128)(2,1)S(1)} %get-tuple-element.82.refs_0_, ...), custom_call_target="tpu_custom_call", output_to_operand_aliasing={{0}: (5, {}), {1}: (6, {}), {2}: (7, {}), {3}: (8, {})} | custom-call | bytes 4194304 | tf_op jit(solution)/shard_map/unpack/pallas_call | solution.py:200
  (45 shorter events, 3.2 us)
Async XLA Ops:
  2.6 2.6 %collective-permute-start.4 = (bf16[2064,128]{1,0:T(8,128)(2,1)S(1)}, bf16[2064,128]{1,0:T(8,128)(2,1)S(1)}, u32[]{:S(2)}, u32[]{:S(2)}) collective-permute-start(bf16[2064,128]{1,0:T(8,128)(2,1)S(1)} %get-tuple-element.66), channel_id=1, source_target_pairs={{0,4},{4,0},{8,12},{12,8},{16,20},{20,16},{24,28},{28,24},{1,5},{5... | collective-permute-start | bytes 1585160 | tf_op jit(solution)/shard_map/ppermute | solution.py:462
  5.0 5.8 %collective-permute-start.6 = (bf16[2048,128]{1,0:T(8,128)(2,1)S(1)}, bf16[2048,128]{1,0:T(8,128)(2,1)S(1)}, u32[]{:S(2)}, u32[]{:S(2)}) collective-permute-start(bf16[2048,128]{1,0:T(8,128)(2,1)S(1)} %get-tuple-element.75), channel_id=1, source_target_pairs={{0,4},{4,0},{8,12},{12,8},{16,20},{20,16},{24,28},{28,24},{1,5},{5... | collective-permute-start | bytes 1572872 | tf_op jit(solution)/shard_map/ppermute | solution.py:462
  5.2 27.7 %collective-permute-start.5 = (bf16[2080,128]{1,0:T(8,128)(2,1)S(1)}, bf16[2080,128]{1,0:T(8,128)(2,1)S(1)}, u32[]{:S(2)}, u32[]{:S(2)}) collective-permute-start(bf16[2080,128]{1,0:T(8,128)(2,1)S(1)} %merge.4), channel_id=1, source_target_pairs={{0,24},{4,28},{8,16},{12,20},{16,8},{20,12},{24,0},{28,4},{1,25},{... | collective-permute-start | bytes 1597448 | tf_op jit(solution)/shard_map/ppermute | solution.py:462
  9.2 19.2 %collective-permute-start = (bf16[1040,128]{1,0:T(8,128)(2,1)S(1)}, bf16[1040,128]{1,0:T(8,128)(2,1)S(1)}, u32[]{:S(2)}, u32[]{:S(2)}) collective-permute-start(bf16[1040,128]{1,0:T(8,128)(2,1)S(1)} %get-tuple-element.62), channel_id=1, source_target_pairs={{0,8},{4,12},{8,0},{12,4},{16,24},{20,28},{24,16},{28,20},{1,9},{5... | collective-permute-start | bytes 798728 | tf_op jit(solution)/shard_map/ppermute | solution.py:462
  9.7 22.5 %collective-permute-start.1 = (bf16[1040,128]{1,0:T(8,128)(2,1)S(1)}, bf16[1040,128]{1,0:T(8,128)(2,1)S(1)}, u32[]{:S(2)}, u32[]{:S(2)}) collective-permute-start(bf16[1040,128]{1,0:T(8,128)(2,1)S(1)} %get-tuple-element.63), channel_id=1, source_target_pairs={{0,12},{4,8},{8,4},{12,0},{16,28},{20,24},{24,20},{28,16},{1,13},{... | collective-permute-start | bytes 798728 | tf_op jit(solution)/shard_map/ppermute | solution.py:462
  10.3 22.0 %collective-permute-start.2 = (bf16[1040,128]{1,0:T(8,128)(2,1)S(1)}, bf16[1040,128]{1,0:T(8,128)(2,1)S(1)}, u32[]{:S(2)}, u32[]{:S(2)}) collective-permute-start(bf16[1040,128]{1,0:T(8,128)(2,1)S(1)} %get-tuple-element.64), channel_id=1, source_target_pairs={{0,16},{4,20},{8,24},{12,28},{16,0},{20,4},{24,8},{28,12},{1,17},{... | collective-permute-start | bytes 798728 | tf_op jit(solution)/shard_map/ppermute | solution.py:462
  10.8 22.1 %collective-permute-start.3 = (bf16[1040,128]{1,0:T(8,128)(2,1)S(1)}, bf16[1040,128]{1,0:T(8,128)(2,1)S(1)}, u32[]{:S(2)}, u32[]{:S(2)}) collective-permute-start(bf16[1040,128]{1,0:T(8,128)(2,1)S(1)} %get-tuple-element.65), channel_id=1, source_target_pairs={{0,20},{4,16},{8,28},{12,24},{16,4},{20,0},{24,12},{28,8},{1,21},{... | collective-permute-start | bytes 798728 | tf_op jit(solution)/shard_map/ppermute | solution.py:462
  32.9 26.9 %collective-permute-start.7 = (bf16[1024,128]{1,0:T(8,128)(2,1)S(1)}, bf16[1024,128]{1,0:T(8,128)(2,1)S(1)}, u32[]{:S(2)}, u32[]{:S(2)}) collective-permute-start(bf16[1024,128]{1,0:T(8,128)(2,1)S(1)} %get-tuple-element.77), channel_id=1, source_target_pairs={{0,8},{4,12},{8,0},{12,4},{16,24},{20,28},{24,16},{28,20},{1,9},{5... | collective-permute-start | bytes 786440 | tf_op jit(solution)/shard_map/ppermute | solution.py:462
  34.5 25.3 %collective-permute-start.8 = (bf16[1024,128]{1,0:T(8,128)(2,1)S(1)}, bf16[1024,128]{1,0:T(8,128)(2,1)S(1)}, u32[]{:S(2)}, u32[]{:S(2)}) collective-permute-start(bf16[1024,128]{1,0:T(8,128)(2,1)S(1)} %get-tuple-element.78), channel_id=1, source_target_pairs={{0,12},{4,8},{8,4},{12,0},{16,28},{20,24},{24,20},{28,16},{1,13},{... | collective-permute-start | bytes 786440 | tf_op jit(solution)/shard_map/ppermute | solution.py:462
  34.5 25.3 %collective-permute-start.9 = (bf16[1024,128]{1,0:T(8,128)(2,1)S(1)}, bf16[1024,128]{1,0:T(8,128)(2,1)S(1)}, u32[]{:S(2)}, u32[]{:S(2)}) collective-permute-start(bf16[1024,128]{1,0:T(8,128)(2,1)S(1)} %get-tuple-element.79), channel_id=1, source_target_pairs={{0,16},{4,20},{8,24},{12,28},{16,0},{20,4},{24,8},{28,12},{1,17},{... | collective-permute-start | bytes 786440 | tf_op jit(solution)/shard_map/ppermute | solution.py:462
  36.1 23.7 %collective-permute-start.10 = (bf16[1024,128]{1,0:T(8,128)(2,1)S(1)}, bf16[1024,128]{1,0:T(8,128)(2,1)S(1)}, u32[]{:S(2)}, u32[]{:S(2)}) collective-permute-start(bf16[1024,128]{1,0:T(8,128)(2,1)S(1)} %get-tuple-element.80), channel_id=1, source_target_pairs={{0,20},{4,16},{8,28},{12,24},{16,4},{20,0},{24,12},{28,8},{1,21},{... | collective-permute-start | bytes 786440 | tf_op jit(solution)/shard_map/ppermute | solution.py:462
  36.4 23.4 %collective-permute-start.11 = (bf16[2048,128]{1,0:T(8,128)(2,1)S(1)}, bf16[2048,128]{1,0:T(8,128)(2,1)S(1)}, u32[]{:S(2)}, u32[]{:S(2)}) collective-permute-start(bf16[2048,128]{1,0:T(8,128)(2,1)S(1)} %get-tuple-element.81), channel_id=1, source_target_pairs={{0,24},{4,28},{8,16},{12,20},{16,8},{20,12},{24,0},{28,4},{1,25},{... | collective-permute-start | bytes 1572872 | tf_op jit(solution)/shard_map/ppermute | solution.py:462
  39.0 0.7 copy-start
  59.8 3.6 %collective-permute-start.16 = (bf16[2048,128]{1,0:T(8,128)(2,1)S(1)}, bf16[2048,128]{1,0:T(8,128)(2,1)S(1)}, u32[]{:S(2)}, u32[]{:S(2)}) collective-permute-start(bf16[2048,128]{1,0:T(8,128)(2,1)S(1)} %get-tuple-element.98), channel_id=1, source_target_pairs={{0,4},{4,0},{8,12},{12,8},{16,20},{20,16},{24,28},{28,24},{1,5},{5... | collective-permute-start | bytes 1572872 | tf_op jit(solution)/shard_map/ppermute | solution.py:462
  59.9 26.9 %collective-permute-start.12 = (bf16[1024,128]{1,0:T(8,128)(2,1)S(1)}, bf16[1024,128]{1,0:T(8,128)(2,1)S(1)}, u32[]{:S(2)}, u32[]{:S(2)}) collective-permute-start(bf16[1024,128]{1,0:T(8,128)(2,1)S(1)} %get-tuple-element.94), channel_id=1, source_target_pairs={{0,8},{4,12},{8,0},{12,4},{16,24},{20,28},{24,16},{28,20},{1,9},{5... | collective-permute-start | bytes 786440 | tf_op jit(solution)/shard_map/ppermute | solution.py:462
  61.6 25.2 %collective-permute-start.13 = (bf16[1024,128]{1,0:T(8,128)(2,1)S(1)}, bf16[1024,128]{1,0:T(8,128)(2,1)S(1)}, u32[]{:S(2)}, u32[]{:S(2)}) collective-permute-start(bf16[1024,128]{1,0:T(8,128)(2,1)S(1)} %get-tuple-element.95), channel_id=1, source_target_pairs={{0,12},{4,8},{8,4},{12,0},{16,28},{20,24},{24,20},{28,16},{1,13},{... | collective-permute-start | bytes 786440 | tf_op jit(solution)/shard_map/ppermute | solution.py:462
  61.8 25.0 %collective-permute-start.14 = (bf16[1024,128]{1,0:T(8,128)(2,1)S(1)}, bf16[1024,128]{1,0:T(8,128)(2,1)S(1)}, u32[]{:S(2)}, u32[]{:S(2)}) collective-permute-start(bf16[1024,128]{1,0:T(8,128)(2,1)S(1)} %get-tuple-element.96), channel_id=1, source_target_pairs={{0,16},{4,20},{8,24},{12,28},{16,0},{20,4},{24,8},{28,12},{1,17},{... | collective-permute-start | bytes 786440 | tf_op jit(solution)/shard_map/ppermute | solution.py:462
  63.4 23.5 %collective-permute-start.15 = (bf16[1024,128]{1,0:T(8,128)(2,1)S(1)}, bf16[1024,128]{1,0:T(8,128)(2,1)S(1)}, u32[]{:S(2)}, u32[]{:S(2)}) collective-permute-start(bf16[1024,128]{1,0:T(8,128)(2,1)S(1)} %get-tuple-element.97), channel_id=1, source_target_pairs={{0,20},{4,16},{8,28},{12,24},{16,4},{20,0},{24,12},{28,8},{1,21},{... | collective-permute-start | bytes 786440 | tf_op jit(solution)/shard_map/ppermute | solution.py:462
  63.5 23.3 %collective-permute-start.17 = (bf16[2048,128]{1,0:T(8,128)(2,1)S(1)}, bf16[2048,128]{1,0:T(8,128)(2,1)S(1)}, u32[]{:S(2)}, u32[]{:S(2)}) collective-permute-start(bf16[2048,128]{1,0:T(8,128)(2,1)S(1)} %merge.6), channel_id=1, source_target_pairs={{0,24},{4,28},{8,16},{12,20},{16,8},{20,12},{24,0},{28,4},{1,25},{... | collective-permute-start | bytes 1572872 | tf_op jit(solution)/shard_map/ppermute | solution.py:462
  86.9 2.7 %collective-permute-start.18 = (bf16[4096,128]{1,0:T(8,128)(2,1)S(1)}, bf16[4096,128]{1,0:T(8,128)(2,1)S(1)}, u32[]{:S(2)}, u32[]{:S(2)}) collective-permute-start(bf16[4096,128]{1,0:T(8,128)(2,1)S(1)} %get-tuple-element.100), channel_id=1, source_target_pairs={{0,4},{4,0},{8,12},{12,8},{16,20},{20,16},{24,28},{28,24},{1,5},{5... | collective-permute-start | bytes 3145736 | tf_op jit(solution)/shard_map/ppermute | solution.py:462
  89.7 29.4 %collective-permute-start.19 = (bf16[2048,128]{1,0:T(8,128)(2,1)S(1)}, bf16[2048,128]{1,0:T(8,128)(2,1)S(1)}, u32[]{:S(2)}, u32[]{:S(2)}) collective-permute-start(bf16[2048,128]{1,0:T(8,128)(2,1)S(1)} %get-tuple-element.104), channel_id=1, source_target_pairs={{0,8},{4,12},{8,0},{12,4},{16,24},{20,28},{24,16},{28,20},{1,9},{5... | collective-permute-start | bytes 1572872 | tf_op jit(solution)/shard_map/ppermute | solution.py:462
  91.2 27.9 %collective-permute-start.20 = (bf16[2048,128]{1,0:T(8,128)(2,1)S(1)}, bf16[2048,128]{1,0:T(8,128)(2,1)S(1)}, u32[]{:S(2)}, u32[]{:S(2)}) collective-permute-start(bf16[2048,128]{1,0:T(8,128)(2,1)S(1)} %get-tuple-element.105), channel_id=1, source_target_pairs={{0,16},{4,20},{8,24},{12,28},{16,0},{20,4},{24,8},{28,12},{1,17},{... | collective-permute-start | bytes 1572872 | tf_op jit(solution)/shard_map/ppermute | solution.py:462
  92.7 26.4 %collective-permute-start.21 = (bf16[2048,128]{1,0:T(8,128)(2,1)S(1)}, bf16[2048,128]{1,0:T(8,128)(2,1)S(1)}, u32[]{:S(2)}, u32[]{:S(2)}) collective-permute-start(bf16[2048,128]{1,0:T(8,128)(2,1)S(1)} %get-tuple-element.106), channel_id=1, source_target_pairs={{0,24},{4,28},{8,16},{12,20},{16,8},{20,12},{24,0},{28,4},{1,25},{... | collective-permute-start | bytes 1572872 | tf_op jit(solution)/shard_map/ppermute | solution.py:462
  93.3 3.5 %collective-permute-start.22 = (f32[1,128]{1,0:T(1,128)S(1)}, f32[1,128]{1,0:T(1,128)S(1)}, u32[]{:S(2)}, u32[]{:S(2)}) collective-permute-start(f32[1,128]{1,0:T(1,128)S(1)} %get-tuple-element.116), channel_id=1, source_target_pairs={{0,1},{1,0},{2,3},{3,2},{4,5},{5,4},{6,7},{7,6},{8,9},{9,8},{10,11... | collective-permute-start | bytes 1544 | tf_op jit(solution)/shard_map/ppermute | solution.py:462
  96.8 4.4 %collective-permute-start.23 = (f32[1,128]{1,0:T(1,128)S(1)}, f32[1,128]{1,0:T(1,128)S(1)}, u32[]{:S(2)}, u32[]{:S(2)}) collective-permute-start(f32[1,128]{1,0:T(1,128)S(1)} %add.15), channel_id=1, source_target_pairs={{0,2},{1,3},{2,0},{3,1},{4,6},{5,7},{6,4},{7,5},{8,10},{9,11},{10,... | collective-permute-start | bytes 1544 | tf_op jit(solution)/shard_map/ppermute | solution.py:462
  101.3 1.1 collective-permute-start.24
  102.4 12.6 %collective-permute-start.25 = (f32[1,128]{1,0:T(1,128)S(1)}, f32[1,128]{1,0:T(1,128)S(1)}, u32[]{:S(2)}, u32[]{:S(2)}) collective-permute-start(f32[1,128]{1,0:T(1,128)S(1)} %add.17), channel_id=1, source_target_pairs={{0,8},{4,12},{8,0},{12,4},{16,24},{20,28},{24,16},{28,20},{1,9},{5... | collective-permute-start | bytes 1544 | tf_op jit(solution)/shard_map/ppermute | solution.py:462
  115.0 3.5 %collective-permute-start.26 = (f32[1,128]{1,0:T(1,128)S(1)}, f32[1,128]{1,0:T(1,128)S(1)}, u32[]{:S(2)}, u32[]{:S(2)}) collective-permute-start(f32[1,128]{1,0:T(1,128)S(1)} %add.18), channel_id=1, source_target_pairs={{0,16},{4,20},{8,24},{12,28},{16,0},{20,4},{24,8},{28,12},{1,17},{... | collective-permute-start | bytes 1544 | tf_op jit(solution)/shard_map/ppermute | solution.py:462

commit v3 on v2

--- a/solution.py
+++ b/solution.py
@@ -21,19 +21,24 @@
 VMEM = pl.BlockSpec(memory_space=pltpu.VMEM)
 PARAMS = pltpu.CompilerParams(vmem_limit_bytes=VMEM_LIMIT)
 
-DIRECT = {
-    "steps": (0, 2, 3, 4, 5, 6),
-    "rows": (1, 1, 1, 1, 1, 2, 2),
-    "sent": ((0, 0), (6, 0), (1, 0), (2, 0), (3, 0), (4, 0), (5, 0), (6, 1)),
-    "arrived": ((0, 0), (6, 0), (1, 0), (2, 0), (3, 0), (4, 0), (5, 0), (5, 1)),
-    "merged": ((1, 5),),
+
+ORDER = (1, 2, 3)
+STEPS = (0,) + tuple(2 * m for m in ORDER)
+PLACE = {m: n for n, m in enumerate((0,) + ORDER)}
+HALVES = tuple((PLACE[k // 2], k % 2) for k in range(GROUP))
+SWAP_BEFORE = {
+    "steps": STEPS + (1,),
+    "sizes": (1, 2, 2, 2, 4),
+    "sent": tuple((4, n) if e else (n, 0) for n, e in HALVES),
+    "arrived_sizes": (1, 2, 2, 2, 4),
+    "arrived": tuple((4, 0) if (n, e) == (0, 1) else (n, e) for n, e in HALVES),
 }
-PAIRED = {
-    "steps": (0, 2, 4, 6),
-    "rows": (1, 2, 2, 2, 4),
-    "sent": ((0, 0), (4, 0), (1, 0), (4, 1), (2, 0), (4, 2), (3, 0), (4, 3)),
-    "arrived": ((0, 0), (4, 0), (1, 0), (1, 1), (2, 0), (2, 1), (3, 0), (3, 1)),
-    "merged": ((1, 1), (2, 2), (3, 3)),
+SWAP_AFTER = {
+    "steps": STEPS,
+    "sizes": (2, 2, 2, 2),
+    "sent": HALVES,
+    "arrived_sizes": (2, 2, 2, 2, 4),
+    "arrived": tuple((4, n) if e else (n, 0) for n, e in HALVES),
 }
 
 
@@ -48,27 +53,26 @@
         copy.wait()
 
 
-def pack_kernel(group, per_device, head, tokens, layout, awaited, *refs):
+def pack_kernel(group, per_device, tokens, items, noted, awaited, *refs):
     adjacency, counts = refs[:2]
     sources, outs = refs[2:6], refs[6 + awaited : -5]
     slots_here, counts_here, note, sems, list_sems = refs[-5:]
     rank = lax.axis_index("seq")
     spot = lax.rem(rank, group)
     copies = []
-    for k in range(group):
-        n, row = layout[k]
+    for i, (head, k, n, row) in enumerate(items):
         column = pl.multiple_of(((spot ^ k) * per_device + head) * HD, HD)
         for a, source in enumerate(sources):
             copies.append(
                 pltpu.make_async_copy(
                     source.at[0, :, pl.ds(column, HD)],
                     outs[n].at[pl.ds(row + a * tokens, tokens)],
-                    sems.at[k, a],
+                    sems.at[i, a],
                 )
             )
     for copy in copies:
         copy.start()
-    if head == 0:
+    if noted:
         run_copies(
             (
                 pltpu.make_async_copy(adjacency, slots_here, list_sems.at[0]),
@@ -85,23 +89,21 @@
                 marks = jnp.where((rows == b) & (lanes == j), near, marks)
             marks = jnp.where((rows == b) & (lanes == slots), counts_here[0, b], marks)
         note[...] = marks.astype(jnp.float32)
-        for out in outs:
+        for out in outs[:noted]:
             row = out.shape[0] // (4 * tokens) * 4 * tokens
             out[row : row + NOTE, :] = note[...].astype(jnp.bfloat16)
     for copy in copies:
         copy.wait()
 
 
-def pack(adjacency, counts, sources, awaited, route, group, per_device, head):
+def pack(adjacency, counts, sources, awaited, items, parts, noted, group, per_device):
     tokens = sources[0].shape[1]
     size = 4 * tokens
-    layout = [(n, row * size) for n, row in route["sent"]]
-    rows = [n * size for n in route["rows"]]
-    if head == 0:
-        rows = [n * (size + NOTE) for n in route["rows"][:-1]] + [rows[-1] + NOTE]
+    items = [(head, k, n, part * size) for head, k, n, part in items]
+    rows = [n * size + (NOTE if i < noted else 0) for i, n in enumerate(parts)]
     return pl.pallas_call(
         functools.partial(
-            pack_kernel, group, per_device, head, tokens, layout, len(awaited)
+            pack_kernel, group, per_device, tokens, items, noted, len(awaited)
         ),
         out_shape=[jax.ShapeDtypeStruct((r, HD), jnp.bfloat16) for r in rows],
         in_specs=[ANY] * (6 + len(awaited)),
@@ -110,11 +112,11 @@
             pltpu.SMEM(adjacency.shape, jnp.int32),
             pltpu.SMEM(counts.shape, jnp.int32),
             pltpu.VMEM((NOTE, HD), jnp.float32),
-            pltpu.SemaphoreType.DMA((group, 4)),
+            pltpu.SemaphoreType.DMA((len(items), 4)),
             pltpu.SemaphoreType.DMA((2,)),
         ],
         compiler_params=PARAMS,
-        cost_estimate=bytes_cost(group * size * HD * 4),
+        cost_estimate=bytes_cost(len(items) * size * HD * 4),
         name="pack",
     )(adjacency, counts, *sources, *awaited)
 
@@ -136,47 +138,66 @@
     )(*arrays, *awaited)
 
 
-def merge_kernel(moves, *refs):
-    swapped, outs, sems = refs[0], refs[-1 - len(moves) : -1], refs[-1]
+def split_kernel(pairs, size, noted, *refs):
+    parcels, out, sems = refs[:pairs], refs[-2], refs[-1]
     copies = []
-    for n, parts in enumerate(moves):
-        for i, (row, to, count) in enumerate(parts):
+    for m in range(pairs):
+        moves = [(size, m * size, size)]
+        if noted:
+            moves.append((2 * size, pairs * size + m * NOTE, NOTE))
+        for i, (row, to, count) in enumerate(moves):
             copies.append(
                 pltpu.make_async_copy(
-                    swapped.at[pl.ds(row, count)], outs[n].at[pl.ds(to, count)], sems.at[n, i]
+                    parcels[m].at[pl.ds(row, count)], out.at[pl.ds(to, count)], sems.at[m, i]
                 )
             )
     run_copies(copies)
 
 
-def merge(swapped, buffers, route, size):
-    buffers = list(buffers)
-    noted = swapped.shape[0] % size != 0
-    moves = []
-    for row, _ in route["merged"]:
-        parts = [(row * size, size, size)]
-        if noted:
-            parts.append((route["rows"][-1] * size, 2 * size + NOTE, NOTE))
-        moves.append(parts)
-    held = [buffers[n] for _, n in route["merged"]]
-    filled = pl.pallas_call(
-        functools.partial(merge_kernel, moves),
-        out_shape=[jax.ShapeDtypeStruct(x.shape, x.dtype) for x in held],
-        in_specs=[VMEM] + [ANY] * len(held),
-        out_specs=[ANY] * len(held),
-        scratch_shapes=[pltpu.SemaphoreType.DMA((len(held), 2))],
-        input_output_aliases={1 + n: n for n in range(len(held))},
+def split(parcels, awaited, size):
+    pairs = len(parcels)
+    noted = parcels[0].shape[0] > 2 * size
+    rows = pairs * (size + NOTE * noted)
+    return pl.pallas_call(
+        functools.partial(split_kernel, pairs, size, noted),
+        out_shape=jax.ShapeDtypeStruct((rows, HD), jnp.bfloat16),
+        in_specs=[ANY] * (pairs + len(awaited)),
+        out_specs=VMEM,
+        scratch_shapes=[pltpu.SemaphoreType.DMA((pairs, 2))],
         compiler_params=PARAMS,
-        cost_estimate=bytes_cost(len(held) * size * HD * 4),
+        cost_estimate=bytes_cost(rows * HD * 4),
+        name="split",
+    )(*parcels, *awaited)
+
+
+def merge_kernel(size, *refs):
+    swapped, outs, sems = refs[0], refs[-4:-1], refs[-1]
+    run_copies(
+        [
+            pltpu.make_async_copy(
+                swapped.at[pl.ds((n + 1) * size, size)], out.at[pl.ds(size, size)], sems.at[n]
+            )
+            for n, out in enumerate(outs)
+        ]
+    )
+
+
+def merge(swapped, halves, size):
+    return pl.pallas_call(
+        functools.partial(merge_kernel, size),
+        out_shape=[jax.ShapeDtypeStruct(x.shape, x.dtype) for x in halves],
+        in_specs=[VMEM] + [ANY] * len(halves),
+        out_specs=[ANY] * len(halves),
+        scratch_shapes=[pltpu.SemaphoreType.DMA((len(halves),))],
+        input_output_aliases={1 + n: n for n in range(len(halves))},
+        compiler_params=PARAMS,
+        cost_estimate=bytes_cost(len(halves) * size * HD * 4),
         name="merge",
-    )(swapped, *held)
-    for (_, n), x in zip(route["merged"], filled):
-        buffers[n] = x
-    return buffers
-
-
-def unpack_kernel(group, per_device, head, tokens, count, layout, *refs):
-    parcels, outs, sems = refs[:count], refs[-5:-1], refs[-1]
+    )(swapped, *halves)
+
+
+def unpack_kernel(group, per_device, head, tokens, count, layout, passed, *refs):
+    parcels, outs, sems = refs[:count], refs[-5 - passed : -1 - passed], refs[-1]
     spot = lax.rem(lax.axis_index("seq"), group)
     copies = []
     for k, (n, from_row) in enumerate(layout):
@@ -192,32 +213,36 @@
     run_copies(copies)
 
 
-def unpack(parcels, outs, route, group, per_device, head):
+def unpack(parcels, outs, passed, route, group, per_device, head):
     count = len(parcels)
-    tokens = parcels[0].shape[0] // 4
+    tokens = parcels[0].shape[0] // (4 * route["sizes"][0])
     layout = [(n, row * 4 * tokens) for n, row in route["arrived"]]
     shape = jax.ShapeDtypeStruct((1, tokens, group * per_device * HD), jnp.bfloat16)
     return pl.pallas_call(
-        functools.partial(unpack_kernel, group, per_device, head, tokens, count, layout),
-        out_shape=[shape] * 4,
-        in_specs=[VMEM] * count + [ANY] * len(outs),
-        out_specs=[ANY] * 4,
+        functools.partial(
+            unpack_kernel, group, per_device, head, tokens, count, layout, len(passed)
+        ),
+        out_shape=[shape] * 4 + [jax.ShapeDtypeStruct(x.shape, x.dtype) for x in passed],
+        in_specs=[VMEM] * count + [ANY] * (len(outs) + len(passed)),
+        out_specs=[ANY] * (4 + len(passed)),
         scratch_shapes=[pltpu.SemaphoreType.DMA((group, 4))],
-        input_output_aliases={count + a: a for a in range(len(outs))},
+        input_output_aliases={
+            count + n: 4 - len(outs) + n for n in range(len(outs) + len(passed))
+        },
         compiler_params=PARAMS,
         cost_estimate=bytes_cost(group * tokens * HD * 16),
         name="unpack",
-    )(*parcels, *outs)
+    )(*parcels, *outs, *passed)
 
 
 def attend_kernel(group, per_device, head, halo, slots, own_blocks, scale, route, *refs):
     sink, sink_in, marks_in = refs[:3]
     arriving, leaving = route
-    count = len(arriving["rows"])
+    count = len(arriving["arrived_sizes"])
     parcels, refs = refs[3 : 3 + count], refs[3 + count :]
     if halo:
         halo_in, refs = refs[0], refs[1:]
-    count = len(leaving["rows"])
+    count = len(leaving["sizes"])
     results, sink_out, marks = refs[:count], refs[count], refs[count + 1]
     refs = refs[count + 2 :]
     if halo:
@@ -233,7 +258,7 @@
     number = spot * per_device + head
     note_copies, copies = [], []
     for k, (n, row) in enumerate(arriving["arrived"] if head == 0 else ()):
-        row = arriving["rows"][n] * 4 * span + row * NOTE
+        row = arriving["arrived_sizes"][n] * 4 * span + row * NOTE
         note_copies.append(
             pltpu.make_async_copy(
                 parcels[n].at[pl.ds(row, NOTE)], notes.at[spot ^ k], sems.at[k, 4]
@@ -399,7 +424,7 @@
     blocks = own_blocks * group
     window = blocks + 2 * halo
     out_shape = [
-        jax.ShapeDtypeStruct((n * 4 * span, HD), jnp.bfloat16) for n in routes[1]["rows"]
+        jax.ShapeDtypeStruct((n * 4 * span, HD), jnp.bfloat16) for n in routes[1]["sizes"]
     ]
     out_specs = [ANY] * len(out_shape) + [VMEM] * 2
     out_shape.append(jax.ShapeDtypeStruct((1, BLK), jnp.float32))
@@ -461,10 +486,6 @@
     def swap(x, k, axis="seq"):
         return lax.ppermute(x, axis, [(i, i ^ k) for i in range(lax.axis_size(axis))])
 
-    def between(buffers, route):
-        pairs = zip(buffers[1:], route["steps"][1:])
-        return [buffers[0]] + [swap(x, k) for x, k in pairs]
-
     def beside(x, step):
         route = [(i, i + step * group) for i in range(seq) if 0 <= i + step * group < seq]
         return lax.ppermute(x, "seq", route)
@@ -504,26 +525,41 @@
         for x in (adjacency, counts, keys, values, queries, out_grad)
     ]
     adjacency, counts, *sources = constrained
-    routes_out = [DIRECT] * (per_device - 1) + [PAIRED]
-
-    arrived = []
-    packed = []
-    for head in range(per_device):
-        packed = pack(
-            adjacency, counts, sources, packed[:1], DIRECT, group, per_device, head
-        )
-        crossed = swap(packed[-1], 1)
-        buffers = merge(crossed, packed[:-1], DIRECT, size)
-        if head > 0:
-            buffers[1:] = after(arrived[-1][1:-1], buffers[1:])
-        arrived.append(between(buffers, DIRECT) + [crossed])
-
+    shared = (adjacency, counts, sources)
+    items = [(0, k, n, part) for k, (n, part) in enumerate(SWAP_AFTER["sent"])]
+    sizes = list(SWAP_AFTER["sizes"])
+    noted = len(sizes)
+    cross = len(SWAP_BEFORE["sizes"]) - 1
+    sent = list(enumerate(SWAP_BEFORE["sent"]))
+    for head in range(1, per_device):
+        items += [(head, k, len(sizes), part) for k, (n, part) in sent if n == cross]
+        sizes.append(SWAP_BEFORE["sizes"][cross])
+    packed = pack(*shared, [], items, sizes, noted, group, per_device)
+    filled = []
+    for head in range(1, per_device):
+        items = [(head, k, n, part) for k, (n, part) in sent if n != cross]
+        own, *halves = pack(
+            *shared, packed[:1], items, SWAP_BEFORE["sizes"][:cross], 0, group, per_device
+        )
+        crossed = swap(packed[noted + head - 1], 1)
+        filled.append((own, merge(crossed, halves, size), crossed))
+    between = SWAP_AFTER["steps"][1:]
+    parcels = [packed[0]] + [swap(x, k) for x, k in zip(packed[1:noted], between)]
+    awaited = [halves[0] for _, halves, _ in filled]
+    arrived = [parcels + [swap(split(parcels, awaited, size), 1)]]
+    routes_in = [SWAP_AFTER] + [SWAP_BEFORE] * (per_device - 1)
+    for own, halves, crossed in filled:
+        halves = after(arrived[-1][1:-1], halves)
+        arrived.append([own] + [swap(x, k) for x, k in zip(halves, between)] + [crossed])
+
+    routes_out = [SWAP_AFTER] * (per_device - 1) + [SWAP_BEFORE]
     sink_row = jnp.zeros((1, BLK), jnp.float32)
     marks = jnp.zeros((own_blocks * group, HD), jnp.int32)
+    before = arrived[-1][1:-1] if per_device > 1 else []
     returned = []
     for head in range(per_device):
-        routes = (DIRECT, routes_out[head])
-        halo_in = halos(arrived[head], DIRECT) if halo else None
+        routes = (routes_in[head], routes_out[head])
+        halo_in = halos(arrived[head], routes[0]) if halo else None
         done = attend(
             sink,
             sink_row,
@@ -539,26 +575,33 @@
             own_blocks,
             scale,
         )
-        count = len(routes[1]["rows"])
+        count = len(routes[1]["sizes"])
         results, sink_row, marks = list(done[:count]), done[count], done[count + 1]
         if halo:
             results = add_halos(results, done[count + 2], routes[1])
-        if head < per_device - 1:
-            results[1:] = after(arrived[head + 1][1:-1], results[1:])
-        elif head > 0:
-            *results[1:], sink_row = after(returned[-1][1:-1], results[1:] + [sink_row])
-        crossed = swap(results[-1], 1)
-        buffers = merge(crossed, results[:-1], routes[1], size)
-        returned.append(between(buffers, routes[1]) + [crossed])
-    outs = []
-    for head in range(per_device):
-        outs = unpack(returned[head], outs, routes_out[head], group, per_device, head)
-    value_grad, key_grad, attended, query_grad = outs
-    for axis in ("dp", "seq"):
-        step = 1
+        if before:
+            results[1:] = after(before, results[1:])
+        own, *halves = results
+        if routes[1] is SWAP_BEFORE:
+            crossed = swap(halves.pop(), 1)
+            halves = merge(crossed, halves, size)
+        before = [swap(x, k) for x, k in zip(halves, between)]
+        returned.append([own] + before)
+    returned[-1].append(crossed)
+    for axis, step in (("dp", 1), ("seq", group)):
         while step < lax.axis_size(axis):
             sink_row = sink_row + swap(sink_row, step, axis)
             step *= 2
+    sink_row = sink_row + swap(sink_row, 1)
+    outs = []
+    for head in range(per_device - 1):
+        parcels = returned[head] + [swap(split(returned[head], [crossed], size), 1)]
+        *outs, sink_row = unpack(
+            parcels, outs, [sink_row], routes_out[head], group, per_device, head
+        )
+    sink_row = functools.reduce(jnp.add, [sink_row] + [swap(sink_row, k) for k in between])
+    outs = unpack(returned[-1], outs, [], routes_out[-1], group, per_device, per_device - 1)
+    value_grad, key_grad, attended, query_grad = outs
     return attended, query_grad, key_grad, value_grad, sink_row[0, :heads]
 
 

time: 121 us -> 116 us (0.959)
  starting transfers between devices: 31.3 us -> 23.2 us
  waiting for transfers between devices: 39.4 us -> 44.3 us
  Pallas kernels: 48 us -> 46.4 us
    ppermute x27 -> x22, starting transfers between devices: 31.3 us -> 23.2 us  [swap(): lax.ppermute(x, axis, [(i, i ^ k) for i in range(lax.axis_size(axis))])]
    ppermute x27 -> x22, waiting for transfers between devices: 39.4 us -> 44.3 us  [swap(): lax.ppermute(x, axis, [(i, i ^ k) for i in range(lax.axis_size(axis))])]
    pallas_call x2, Pallas kernels: 40.8 us -> 38.9 us  [attend(): pl.pallas_call(functools.partial(attend_kernel, group, per_device, head,...]
  transfers between devices with their start and end apart: 27 -> 22, of which waited for: 9 -> 10; matrix products, arithmetic and copies ran while one was open for 0% -> 0% of each run, Pallas kernels for 37% -> 38%
where the time goes in v3:
time: 116 us; the launch traced here: 115 us
  Pallas kernels  46.4 us (40%)
  waiting for transfers between devices  44.3 us (38%)
  starting transfers between devices  23.2 us (20%)
    ppermute x22, waiting for transfers between devices, swap(): lax.ppermute(x, axis, [(i, i ^ k) for i in range(lax.axis_size(axis))])  44.3 us
    pallas_call x2, Pallas kernels, attend(): pl.pallas_call(functools.partial(attend_kernel, group, per_device, head,...  38.9 us
    ppermute x22, starting transfers between devices, swap(): lax.ppermute(x, axis, [(i, i ^ k) for i in range(lax.axis_size(axis))])  23.2 us
    pallas_call x2, Pallas kernels, pack(): pl.pallas_call(functools.partial(pack_kernel, group, per_device, tokens,...  3.85 us
    pallas_call x2, Pallas kernels, unpack(): pl.pallas_call(functools.partial(unpack_kernel, group, per_device, head,...  3.14 us
  transfers between devices with their start and end apart: 22, of which 10 were waited for; matrix products, arithmetic and copies ran while one was open for 0% of the time, Pallas kernels for 38%

profile of v3, /device:TPU:0, one launch (start us, length us, event | category | flops | bytes accessed | tf_op | source)
XLA Modules:
  0.0 115.3 jit_solution(8766411402443863207)
XLA Ops:
  0.6 2.4 %pack.2 = (bf16[2064,128]{1,0:T(8,128)(2,1)S(1)}, bf16[2064,128]{1,0:T(8,128)(2,1)S(1)}, bf16[2064,128]{1,0:T(8,128)(2,1)S(1)}, bf16[2064,128]{1,0:T(8,128)(2,1)S(1)}, bf16[4096,128]{1,0:T(8,128)(2,1)S(1)}) custom-call(s32[1,2,8]{2,1,0:T(2,128)} %refs_0_.5, s32[1,2]{1,0:T(1,128)} %refs_1_.3, bf16[1,256,2048]{2,1,0:T(8,128)(2,1)} %refs_2_.3, ...), custom_call_target="tpu_custom_call" | custom-call | bytes 6291456 | tf_op jit(solution)/shard_map/pack/pallas_call | solution.py:104
  3.6 2.6 %collective-permute-start = (bf16[2064,128]{1,0:T(8,128)(2,1)S(1)}, bf16[2064,128]{1,0:T(8,128)(2,1)S(1)}, u32[]{:S(2)}, u32[]{:S(2)}) collective-permute-start(bf16[2064,128]{1,0:T(8,128)(2,1)S(1)} %get-tuple-element.52), channel_id=1, source_target_pairs={{0,8},{4,12},{8,0},{12,4},{16,24},{20,28},{24,16},{28,20},{1,9},{5... | collective-permute-start | bytes 1585160 | tf_op jit(solution)/shard_map/ppermute | solution.py:487
  6.2 1.5 %collective-permute-start.1 = (bf16[2064,128]{1,0:T(8,128)(2,1)S(1)}, bf16[2064,128]{1,0:T(8,128)(2,1)S(1)}, u32[]{:S(2)}, u32[]{:S(2)}) collective-permute-start(bf16[2064,128]{1,0:T(8,128)(2,1)S(1)} %get-tuple-element.53), channel_id=1, source_target_pairs={{0,16},{4,20},{8,24},{12,28},{16,0},{20,4},{24,8},{28,12},{1,17},{... | collective-permute-start | bytes 1585160 | tf_op jit(solution)/shard_map/ppermute | solution.py:487
  7.7 1.4 %pack.3 = (bf16[1024,128]{1,0:T(8,128)(2,1)S(1)}, bf16[2048,128]{1,0:T(8,128)(2,1)S(1)}, bf16[2048,128]{1,0:T(8,128)(2,1)S(1)}, bf16[2048,128]{1,0:T(8,128)(2,1)S(1)}) custom-call(s32[1,2,8]{2,1,0:T(2,128)} %refs_0_.5, s32[1,2]{1,0:T(1,128)} %refs_1_.3, bf16[1,256,2048]{2,1,0:T(8,128)(2,1)} %refs_2_.3, bf16[1,256,2048]{2,1,0:T(8,128)(2,1)} %refs_3_.3, ...), custom_call_target="tpu_custom_call" | custom-call | bytes 2097152 | tf_op jit(solution)/shard_map/pack/pallas_call | solution.py:104
  9.2 9.8 %collective-permute-done.refs_1_.refs_4_.refs_3_ = bf16[2064,128]{1,0:T(8,128)(2,1)S(1)} collective-permute-done((bf16[2064,128]{1,0:T(8,128)(2,1)S(1)}, bf16[2064,128]{1,0:T(8,128)(2,1)S(1)}, u32[]{:S(2)}, u32[]{:S(2)}) %collective-permute-start) | collective-permute-done | bytes 528416 | tf_op jit(solution)/shard_map/ppermute | solution.py:487
  19.0 12.5 %collective-permute-done.1.refs_2_.refs_5_.refs_4_ = bf16[2064,128]{1,0:T(8,128)(2,1)S(1)} collective-permute-done((bf16[2064,128]{1,0:T(8,128)(2,1)S(1)}, bf16[2064,128]{1,0:T(8,128)(2,1)S(1)}, u32[]{:S(2)}, u32[]{:S(2)}) %collective-permute-start.1) | collective-permute-done | bytes 528416 | tf_op jit(solution)/shard_map/ppermute | solution.py:487
  31.9 1.3 %collective-permute-start.5 = (bf16[2048,128]{1,0:T(8,128)(2,1)S(1)}, bf16[2048,128]{1,0:T(8,128)(2,1)S(1)}, u32[]{:S(2)}, u32[]{:S(2)}) collective-permute-start(bf16[2048,128]{1,0:T(8,128)(2,1)S(1)} %get-tuple-element.65), channel_id=1, source_target_pairs={{0,8},{4,12},{8,0},{12,4},{16,24},{20,28},{24,16},{28,20},{1,9},{5... | collective-permute-start | bytes 1572872 | tf_op jit(solution)/shard_map/ppermute | solution.py:487
  33.1 0.8 collective-permute-start.6
  34.0 1.4 %collective-permute-start.7 = (bf16[2048,128]{1,0:T(8,128)(2,1)S(1)}, bf16[2048,128]{1,0:T(8,128)(2,1)S(1)}, u32[]{:S(2)}, u32[]{:S(2)}) collective-permute-start(bf16[2048,128]{1,0:T(8,128)(2,1)S(1)} %get-tuple-element.67), channel_id=1, source_target_pairs={{0,24},{4,28},{8,16},{12,20},{16,8},{20,12},{24,0},{28,4},{1,25},{... | collective-permute-start | bytes 1572872 | tf_op jit(solution)/shard_map/ppermute | solution.py:487
  35.4 19.2 %attend.2 = (bf16[2048,128]{1,0:T(8,128)(2,1)S(1)}, bf16[2048,128]{1,0:T(8,128)(2,1)S(1)}, bf16[2048,128]{1,0:T(8,128)(2,1)S(1)}, bf16[2048,128]{1,0:T(8,128)(2,...) custom-call(f32[16]{0:T(128)S(1)} %copy-done, f32[1,128]{1,0:T(1,128)S(1)} %broadcast_in_dim.6.refs_1_, ...), custom_call_target="tpu_custom_call" | custom-call | flops 17179869184 | bytes 4194304 | tf_op jit(solution)/shard_map/attend/pallas_call | solution.py:437
  54.6 2.1 %collective-permute-done.6.refs_5_.refs_4_ = bf16[2048,128]{1,0:T(8,128)(2,1)S(1)} collective-permute-done((bf16[2048,128]{1,0:T(8,128)(2,1)S(1)}, bf16[2048,128]{1,0:T(8,128)(2,1)S(1)}, u32[]{:S(2)}, u32[]{:S(2)}) %collective-permute-start.6) | collective-permute-done | bytes 524320 | tf_op jit(solution)/shard_map/ppermute | solution.py:487
  56.7 1.6 %collective-permute-done.7.refs_6_.refs_5_ = bf16[2048,128]{1,0:T(8,128)(2,1)S(1)} collective-permute-done((bf16[2048,128]{1,0:T(8,128)(2,1)S(1)}, bf16[2048,128]{1,0:T(8,128)(2,1)S(1)}, u32[]{:S(2)}, u32[]{:S(2)}) %collective-permute-start.7) | collective-permute-done | bytes 524320 | tf_op jit(solution)/shard_map/ppermute | solution.py:487
  58.4 0.8 collective-permute-start.8
  59.2 1.5 %collective-permute-start.9 = (bf16[2048,128]{1,0:T(8,128)(2,1)S(1)}, bf16[2048,128]{1,0:T(8,128)(2,1)S(1)}, u32[]{:S(2)}, u32[]{:S(2)}) collective-permute-start(bf16[2048,128]{1,0:T(8,128)(2,1)S(1)} %get-tuple-element.77), channel_id=1, source_target_pairs={{0,16},{4,20},{8,24},{12,28},{16,0},{20,4},{24,8},{28,12},{1,17},{... | collective-permute-start | bytes 1572872 | tf_op jit(solution)/shard_map/ppermute | solution.py:487
  60.7 1.2 %collective-permute-start.10 = (bf16[2048,128]{1,0:T(8,128)(2,1)S(1)}, bf16[2048,128]{1,0:T(8,128)(2,1)S(1)}, u32[]{:S(2)}, u32[]{:S(2)}) collective-permute-start(bf16[2048,128]{1,0:T(8,128)(2,1)S(1)} %get-tuple-element.78), channel_id=1, source_target_pairs={{0,24},{4,28},{8,16},{12,20},{16,8},{20,12},{24,0},{28,4},{1,25},{... | collective-permute-start | bytes 1572872 | tf_op jit(solution)/shard_map/ppermute | solution.py:487
  61.9 19.7 %attend.3 = (bf16[1024,128]{1,0:T(8,128)(2,1)S(1)}, bf16[2048,128]{1,0:T(8,128)(2,1)S(1)}, bf16[2048,128]{1,0:T(8,128)(2,1)S(1)}, bf16[2048,128]{1,0:T(8,128)(2,...) custom-call(f32[16]{0:T(128)S(1)} %copy-done, ...), custom_call_target="tpu_custom_call" | custom-call | flops 17179869184 | bytes 4194304 | tf_op jit(solution)/shard_map/attend/pallas_call | solution.py:437
  81.6 1.8 %collective-permute-done.9.refs_5_.refs_2_ = bf16[2048,128]{1,0:T(8,128)(2,1)S(1)} collective-permute-done((bf16[2048,128]{1,0:T(8,128)(2,1)S(1)}, bf16[2048,128]{1,0:T(8,128)(2,1)S(1)}, u32[]{:S(2)}, u32[]{:S(2)}) %collective-permute-start.9) | collective-permute-done | bytes 524320 | tf_op jit(solution)/shard_map/ppermute | solution.py:487
  83.4 2.7 %collective-permute-done.11.refs_0_.refs_4_ = bf16[4096,128]{1,0:T(8,128)(2,1)S(1)} collective-permute-done((bf16[4096,128]{1,0:T(8,128)(2,1)S(1)}, bf16[4096,128]{1,0:T(8,128)(2,1)S(1)}, u32[]{:S(2)}, u32[]{:S(2)}) %collective-permute-start.11) | collective-permute-done | bytes 1048608 | tf_op jit(solution)/shard_map/ppermute | solution.py:487
  86.5 1.5 %collective-permute-start.12 = (bf16[2048,128]{1,0:T(8,128)(2,1)S(1)}, bf16[2048,128]{1,0:T(8,128)(2,1)S(1)}, u32[]{:S(2)}, u32[]{:S(2)}) collective-permute-start(bf16[2048,128]{1,0:T(8,128)(2,1)S(1)} %get-tuple-element.83), channel_id=1, source_target_pairs={{0,8},{4,12},{8,0},{12,4},{16,24},{20,28},{24,16},{28,20},{1,9},{5... | collective-permute-start | bytes 1572872 | tf_op jit(solution)/shard_map/ppermute | solution.py:487
  88.0 0.6 collective-permute-start.13
  88.6 1.5 %collective-permute-start.14 = (bf16[2048,128]{1,0:T(8,128)(2,1)S(1)}, bf16[2048,128]{1,0:T(8,128)(2,1)S(1)}, u32[]{:S(2)}, u32[]{:S(2)}) collective-permute-start(bf16[2048,128]{1,0:T(8,128)(2,1)S(1)} %get-tuple-element.85), channel_id=1, source_target_pairs={{0,24},{4,28},{8,16},{12,20},{16,8},{20,12},{24,0},{28,4},{1,25},{... | collective-permute-start | bytes 1572872 | tf_op jit(solution)/shard_map/ppermute | solution.py:487
  90.1 1.6 %collective-permute-start.16 = (f32[1,128]{1,0:T(1,128)S(1)}, f32[1,128]{1,0:T(1,128)S(1)}, u32[]{:S(2)}, u32[]{:S(2)}) collective-permute-start(f32[1,128]{1,0:T(1,128)S(1)} %get-tuple-element.87), channel_id=1, source_target_pairs={{0,1},{1,0},{2,3},{3,2},{4,5},{5,4},{6,7},{7,6},{8,9},{9,8},{10,11... | collective-permute-start | bytes 1544 | tf_op jit(solution)/shard_map/ppermute | solution.py:487
  91.6 2.0 %collective-permute-done.16 = f32[1,128]{1,0:T(1,128)S(1)} collective-permute-done((f32[1,128]{1,0:T(1,128)S(1)}, f32[1,128]{1,0:T(1,128)S(1)}, u32[]{:S(2)}, u32[]{:S(2)}) %collective-permute-start.16) | collective-permute-done | bytes 544 | tf_op jit(solution)/shard_map/ppermute | solution.py:487
  93.6 2.6 %collective-permute-start.17 = (f32[1,128]{1,0:T(1,128)S(1)}, f32[1,128]{1,0:T(1,128)S(1)}, u32[]{:S(2)}, u32[]{:S(2)}) collective-permute-start(f32[1,128]{1,0:T(1,128)S(1)} %add.18), channel_id=1, source_target_pairs={{0,2},{1,3},{2,0},{3,1},{4,6},{5,7},{6,4},{7,5},{8,10},{9,11},{10,... | collective-permute-start | bytes 1544 | tf_op jit(solution)/shard_map/ppermute | solution.py:487
  96.2 1.9 %collective-permute-done.17 = f32[1,128]{1,0:T(1,128)S(1)} collective-permute-done((f32[1,128]{1,0:T(1,128)S(1)}, f32[1,128]{1,0:T(1,128)S(1)}, u32[]{:S(2)}, u32[]{:S(2)}) %collective-permute-start.17) | collective-permute-done | bytes 544 | tf_op jit(solution)/shard_map/ppermute | solution.py:487
  98.1 1.1 collective-permute-done.18
  99.2 1.6 %unpack.2 = (bf16[1,256,2048]{2,1,0:T(8,128)(2,1)}, bf16[1,256,2048]{2,1,0:T(8,128)(2,1)}, bf16[1,256,2048]{2,1,0:T(8,128)(2,1)}, bf16[1,256,2048]{2,1,0:T(8,128)(2,1)}, f32[1,128]{1,0:T(1,128)S(1)}) custom-call(bf16[2048,128]{1,0:T(8,128)(2,1)S(1)} %get-tuple-element.86.refs_0_, ...), custom_call_target="tpu_custom_call", output_to_operand_aliasing={{4}: (5, {})} | custom-call | bytes 4194304 | tf_op jit(solution)/shard_map/unpack/pallas_call | solution.py:221
  100.8 1.5 %collective-permute-start.21 = (f32[1,128]{1,0:T(1,128)S(1)}, f32[1,128]{1,0:T(1,128)S(1)}, u32[]{:S(2)}, u32[]{:S(2)}) collective-permute-start(f32[1,128]{1,0:T(1,128)S(1)} %get-tuple-element.96), channel_id=1, source_target_pairs={{0,24},{4,28},{8,16},{12,20},{16,8},{20,12},{24,0},{28,4},{1,25},{... | collective-permute-start | bytes 1544 | tf_op jit(solution)/shard_map/ppermute | solution.py:487
  102.3 1.5 %collective-permute-start.20 = (f32[1,128]{1,0:T(1,128)S(1)}, f32[1,128]{1,0:T(1,128)S(1)}, u32[]{:S(2)}, u32[]{:S(2)}) collective-permute-start(f32[1,128]{1,0:T(1,128)S(1)} %get-tuple-element.96), channel_id=1, source_target_pairs={{0,16},{4,20},{8,24},{12,28},{16,0},{20,4},{24,8},{28,12},{1,17},{... | collective-permute-start | bytes 1544 | tf_op jit(solution)/shard_map/ppermute | solution.py:487
  103.7 0.6 collective-permute-start.19
  104.3 8.9 %collective-permute-done.13.refs_2_ = bf16[2048,128]{1,0:T(8,128)(2,1)S(1)} collective-permute-done((bf16[2048,128]{1,0:T(8,128)(2,1)S(1)}, bf16[2048,128]{1,0:T(8,128)(2,1)S(1)}, u32[]{:S(2)}, u32[]{:S(2)}) %collective-permute-start.13) | collective-permute-done | bytes 524320 | tf_op jit(solution)/shard_map/ppermute | solution.py:487
  113.2 1.6 %unpack.3 = (bf16[1,256,2048]{2,1,0:T(8,128)(2,1)}, bf16[1,256,2048]{2,1,0:T(8,128)(2,1)}, bf16[1,256,2048]{2,1,0:T(8,128)(2,1)}, bf16[1,256,2048]{2,1,0:T(8,128)(2,1)}) custom-call(bf16[1024,128]{1,0:T(8,128)(2,1)S(1)} %get-tuple-element.68.refs_0_, ...), custom_call_target="tpu_custom_call", output_to_operand_aliasing={{0}: (5, {}), {1}: (6, {}), {2}: (7, {}), {3}: (8, {})} | custom-call | bytes 4194304 | tf_op jit(solution)/shard_map/unpack/pallas_call | solution.py:221
  (34 shorter events, 1.9 us)
Async XLA Ops:
  3.1 6.1 %collective-permute-start.3 = (bf16[4096,128]{1,0:T(8,128)(2,1)S(1)}, bf16[4096,128]{1,0:T(8,128)(2,1)S(1)}, u32[]{:S(2)}, u32[]{:S(2)}) collective-permute-start(bf16[4096,128]{1,0:T(8,128)(2,1)S(1)} %get-tuple-element.55), channel_id=1, source_target_pairs={{0,4},{4,0},{8,12},{12,8},{16,20},{20,16},{24,28},{28,24},{1,5},{5... | collective-permute-start | bytes 3145736 | tf_op jit(solution)/shard_map/ppermute | solution.py:487
  3.6 15.4 %collective-permute-start = (bf16[2064,128]{1,0:T(8,128)(2,1)S(1)}, bf16[2064,128]{1,0:T(8,128)(2,1)S(1)}, u32[]{:S(2)}, u32[]{:S(2)}) collective-permute-start(bf16[2064,128]{1,0:T(8,128)(2,1)S(1)} %get-tuple-element.52), channel_id=1, source_target_pairs={{0,8},{4,12},{8,0},{12,4},{16,24},{20,28},{24,16},{28,20},{1,9},{5... | collective-permute-start | bytes 1585160 | tf_op jit(solution)/shard_map/ppermute | solution.py:487
  6.2 25.4 %collective-permute-start.1 = (bf16[2064,128]{1,0:T(8,128)(2,1)S(1)}, bf16[2064,128]{1,0:T(8,128)(2,1)S(1)}, u32[]{:S(2)}, u32[]{:S(2)}) collective-permute-start(bf16[2064,128]{1,0:T(8,128)(2,1)S(1)} %get-tuple-element.53), channel_id=1, source_target_pairs={{0,16},{4,20},{8,24},{12,28},{16,0},{20,4},{24,8},{28,12},{1,17},{... | collective-permute-start | bytes 1585160 | tf_op jit(solution)/shard_map/ppermute | solution.py:487
  7.7 23.9 %collective-permute-start.2 = (bf16[2064,128]{1,0:T(8,128)(2,1)S(1)}, bf16[2064,128]{1,0:T(8,128)(2,1)S(1)}, u32[]{:S(2)}, u32[]{:S(2)}) collective-permute-start(bf16[2064,128]{1,0:T(8,128)(2,1)S(1)} %get-tuple-element.54), channel_id=1, source_target_pairs={{0,24},{4,28},{8,16},{12,20},{16,8},{20,12},{24,0},{28,4},{1,25},{... | collective-permute-start | bytes 1585160 | tf_op jit(solution)/shard_map/ppermute | solution.py:487
  31.7 3.7 %collective-permute-start.4 = (bf16[4160,128]{1,0:T(8,128)(2,1)S(1)}, bf16[4160,128]{1,0:T(8,128)(2,1)S(1)}, u32[]{:S(2)}, u32[]{:S(2)}) collective-permute-start(bf16[4160,128]{1,0:T(8,128)(2,1)S(1)} %split.2), channel_id=1, source_target_pairs={{0,4},{4,0},{8,12},{12,8},{16,20},{20,16},{24,28},{28,24},{1,5},{5... | collective-permute-start | bytes 3194888 | tf_op jit(solution)/shard_map/ppermute | solution.py:487
  31.8 3.6 %copy-start = (f32[16]{0:T(128)S(1)}, f32[16]{0:T(128)}, u32[]{:S(2)}) copy-start(f32[16]{0:T(128)} %refs_0_.7) | copy-start | bytes 196
  31.9 22.8 %collective-permute-start.5 = (bf16[2048,128]{1,0:T(8,128)(2,1)S(1)}, bf16[2048,128]{1,0:T(8,128)(2,1)S(1)}, u32[]{:S(2)}, u32[]{:S(2)}) collective-permute-start(bf16[2048,128]{1,0:T(8,128)(2,1)S(1)} %get-tuple-element.65), channel_id=1, source_target_pairs={{0,8},{4,12},{8,0},{12,4},{16,24},{20,28},{24,16},{28,20},{1,9},{5... | collective-permute-start | bytes 1572872 | tf_op jit(solution)/shard_map/ppermute | solution.py:487
  33.1 23.6 %collective-permute-start.6 = (bf16[2048,128]{1,0:T(8,128)(2,1)S(1)}, bf16[2048,128]{1,0:T(8,128)(2,1)S(1)}, u32[]{:S(2)}, u32[]{:S(2)}) collective-permute-start(bf16[2048,128]{1,0:T(8,128)(2,1)S(1)} %get-tuple-element.66), channel_id=1, source_target_pairs={{0,16},{4,20},{8,24},{12,28},{16,0},{20,4},{24,8},{28,12},{1,17},{... | collective-permute-start | bytes 1572872 | tf_op jit(solution)/shard_map/ppermute | solution.py:487
  34.0 24.4 %collective-permute-start.7 = (bf16[2048,128]{1,0:T(8,128)(2,1)S(1)}, bf16[2048,128]{1,0:T(8,128)(2,1)S(1)}, u32[]{:S(2)}, u32[]{:S(2)}) collective-permute-start(bf16[2048,128]{1,0:T(8,128)(2,1)S(1)} %get-tuple-element.67), channel_id=1, source_target_pairs={{0,24},{4,28},{8,16},{12,20},{16,8},{20,12},{24,0},{28,4},{1,25},{... | collective-permute-start | bytes 1572872 | tf_op jit(solution)/shard_map/ppermute | solution.py:487
  58.4 23.2 %collective-permute-start.8 = (bf16[2048,128]{1,0:T(8,128)(2,1)S(1)}, bf16[2048,128]{1,0:T(8,128)(2,1)S(1)}, u32[]{:S(2)}, u32[]{:S(2)}) collective-permute-start(bf16[2048,128]{1,0:T(8,128)(2,1)S(1)} %get-tuple-element.76), channel_id=1, source_target_pairs={{0,8},{4,12},{8,0},{12,4},{16,24},{20,28},{24,16},{28,20},{1,9},{5... | collective-permute-start | bytes 1572872 | tf_op jit(solution)/shard_map/ppermute | solution.py:487
  59.2 24.2 %collective-permute-start.9 = (bf16[2048,128]{1,0:T(8,128)(2,1)S(1)}, bf16[2048,128]{1,0:T(8,128)(2,1)S(1)}, u32[]{:S(2)}, u32[]{:S(2)}) collective-permute-start(bf16[2048,128]{1,0:T(8,128)(2,1)S(1)} %get-tuple-element.77), channel_id=1, source_target_pairs={{0,16},{4,20},{8,24},{12,28},{16,0},{20,4},{24,8},{28,12},{1,17},{... | collective-permute-start | bytes 1572872 | tf_op jit(solution)/shard_map/ppermute | solution.py:487
  60.7 22.7 %collective-permute-start.10 = (bf16[2048,128]{1,0:T(8,128)(2,1)S(1)}, bf16[2048,128]{1,0:T(8,128)(2,1)S(1)}, u32[]{:S(2)}, u32[]{:S(2)}) collective-permute-start(bf16[2048,128]{1,0:T(8,128)(2,1)S(1)} %get-tuple-element.78), channel_id=1, source_target_pairs={{0,24},{4,28},{8,16},{12,20},{16,8},{20,12},{24,0},{28,4},{1,25},{... | collective-permute-start | bytes 1572872 | tf_op jit(solution)/shard_map/ppermute | solution.py:487
  83.4 2.7 %collective-permute-start.11 = (bf16[4096,128]{1,0:T(8,128)(2,1)S(1)}, bf16[4096,128]{1,0:T(8,128)(2,1)S(1)}, u32[]{:S(2)}, u32[]{:S(2)}) collective-permute-start(bf16[4096,128]{1,0:T(8,128)(2,1)S(1)} %get-tuple-element.79), channel_id=1, source_target_pairs={{0,4},{4,0},{8,12},{12,8},{16,20},{20,16},{24,28},{28,24},{1,5},{5... | collective-permute-start | bytes 3145736 | tf_op jit(solution)/shard_map/ppermute | solution.py:487
  86.2 13.0 %collective-permute-start.15 = (bf16[4096,128]{1,0:T(8,128)(2,1)S(1)}, bf16[4096,128]{1,0:T(8,128)(2,1)S(1)}, u32[]{:S(2)}, u32[]{:S(2)}) collective-permute-start(bf16[4096,128]{1,0:T(8,128)(2,1)S(1)} %split.3), channel_id=1, source_target_pairs={{0,4},{4,0},{8,12},{12,8},{16,20},{20,16},{24,28},{28,24},{1,5},{5... | collective-permute-start | bytes 3145736 | tf_op jit(solution)/shard_map/ppermute | solution.py:487
  86.5 17.2 %collective-permute-start.12 = (bf16[2048,128]{1,0:T(8,128)(2,1)S(1)}, bf16[2048,128]{1,0:T(8,128)(2,1)S(1)}, u32[]{:S(2)}, u32[]{:S(2)}) collective-permute-start(bf16[2048,128]{1,0:T(8,128)(2,1)S(1)} %get-tuple-element.83), channel_id=1, source_target_pairs={{0,8},{4,12},{8,0},{12,4},{16,24},{20,28},{24,16},{28,20},{1,9},{5... | collective-permute-start | bytes 1572872 | tf_op jit(solution)/shard_map/ppermute | solution.py:487
  88.0 25.2 %collective-permute-start.13 = (bf16[2048,128]{1,0:T(8,128)(2,1)S(1)}, bf16[2048,128]{1,0:T(8,128)(2,1)S(1)}, u32[]{:S(2)}, u32[]{:S(2)}) collective-permute-start(bf16[2048,128]{1,0:T(8,128)(2,1)S(1)} %get-tuple-element.84), channel_id=1, source_target_pairs={{0,16},{4,20},{8,24},{12,28},{16,0},{20,4},{24,8},{28,12},{1,17},{... | collective-permute-start | bytes 1572872 | tf_op jit(solution)/shard_map/ppermute | solution.py:487
  88.6 24.6 %collective-permute-start.14 = (bf16[2048,128]{1,0:T(8,128)(2,1)S(1)}, bf16[2048,128]{1,0:T(8,128)(2,1)S(1)}, u32[]{:S(2)}, u32[]{:S(2)}) collective-permute-start(bf16[2048,128]{1,0:T(8,128)(2,1)S(1)} %get-tuple-element.85), channel_id=1, source_target_pairs={{0,24},{4,28},{8,16},{12,20},{16,8},{20,12},{24,0},{28,4},{1,25},{... | collective-permute-start | bytes 1572872 | tf_op jit(solution)/shard_map/ppermute | solution.py:487
  90.1 3.5 %collective-permute-start.16 = (f32[1,128]{1,0:T(1,128)S(1)}, f32[1,128]{1,0:T(1,128)S(1)}, u32[]{:S(2)}, u32[]{:S(2)}) collective-permute-start(f32[1,128]{1,0:T(1,128)S(1)} %get-tuple-element.87), channel_id=1, source_target_pairs={{0,1},{1,0},{2,3},{3,2},{4,5},{5,4},{6,7},{7,6},{8,9},{9,8},{10,11... | collective-permute-start | bytes 1544 | tf_op jit(solution)/shard_map/ppermute | solution.py:487
  93.6 4.4 %collective-permute-start.17 = (f32[1,128]{1,0:T(1,128)S(1)}, f32[1,128]{1,0:T(1,128)S(1)}, u32[]{:S(2)}, u32[]{:S(2)}) collective-permute-start(f32[1,128]{1,0:T(1,128)S(1)} %add.18), channel_id=1, source_target_pairs={{0,2},{1,3},{2,0},{3,1},{4,6},{5,7},{6,4},{7,5},{8,10},{9,11},{10,... | collective-permute-start | bytes 1544 | tf_op jit(solution)/shard_map/ppermute | solution.py:487
  98.0 1.1 collective-permute-start.18
  100.8 14.0 %collective-permute-start.21 = (f32[1,128]{1,0:T(1,128)S(1)}, f32[1,128]{1,0:T(1,128)S(1)}, u32[]{:S(2)}, u32[]{:S(2)}) collective-permute-start(f32[1,128]{1,0:T(1,128)S(1)} %get-tuple-element.96), channel_id=1, source_target_pairs={{0,24},{4,28},{8,16},{12,20},{16,8},{20,12},{24,0},{28,4},{1,25},{... | collective-permute-start | bytes 1544 | tf_op jit(solution)/shard_map/ppermute | solution.py:487
  102.3 12.5 %collective-permute-start.20 = (f32[1,128]{1,0:T(1,128)S(1)}, f32[1,128]{1,0:T(1,128)S(1)}, u32[]{:S(2)}, u32[]{:S(2)}) collective-permute-start(f32[1,128]{1,0:T(1,128)S(1)} %get-tuple-element.96), channel_id=1, source_target_pairs={{0,16},{4,20},{8,24},{12,28},{16,0},{20,4},{24,8},{28,12},{1,17},{... | collective-permute-start | bytes 1544 | tf_op jit(solution)/shard_map/ppermute | solution.py:487
  103.7 11.0 %collective-permute-start.19 = (f32[1,128]{1,0:T(1,128)S(1)}, f32[1,128]{1,0:T(1,128)S(1)}, u32[]{:S(2)}, u32[]{:S(2)}) collective-permute-start(f32[1,128]{1,0:T(1,128)S(1)} %get-tuple-element.96), channel_id=1, source_target_pairs={{0,8},{4,12},{8,0},{12,4},{16,24},{20,28},{24,16},{28,20},{1,9},{5... | collective-permute-start | bytes 1544 | tf_op jit(solution)/shard_map/ppermute | solution.py:487

commit v4 on v3

--- a/solution.py
+++ b/solution.py
@@ -12,6 +12,7 @@
 RADIUS = 2
 GROUP = 8
 NOTE = 16
+WORK = 20_000_000_000
 LOG2E = 1.4426950408889634
 VMEM_LIMIT = 48 * 1024 * 1024
 NT = (((1,), (1,)), ((), ()))
@@ -33,12 +34,26 @@
     "arrived_sizes": (1, 2, 2, 2, 4),
     "arrived": tuple((4, 0) if (n, e) == (0, 1) else (n, e) for n, e in HALVES),
 }
+SWAP_SOME = {
+    "steps": (0, 4, 6, 2, 3, 1),
+    "sizes": (1, 2, 2, 1, 1, 3),
+    "sent": ((0, 0), (5, 0), (3, 0), (4, 0), (1, 0), (5, 1), (2, 0), (5, 2)),
+    "arrived_sizes": (1, 2, 2, 1, 1, 3),
+    "arrived": ((0, 0), (5, 0), (3, 0), (4, 0), (1, 0), (1, 1), (2, 0), (2, 1)),
+}
 SWAP_AFTER = {
     "steps": STEPS,
     "sizes": (2, 2, 2, 2),
     "sent": HALVES,
     "arrived_sizes": (2, 2, 2, 2, 4),
     "arrived": tuple((4, n) if e else (n, 0) for n, e in HALVES),
+}
+SWAP_TWICE = {
+    "steps": STEPS,
+    "sizes": (2, 2, 2, 2),
+    "sent": HALVES,
+    "arrived_sizes": (2, 2, 2, 2, 2, 2),
+    "arrived": tuple((4 + n // 2, n % 2) if e else (n, 0) for n, e in HALVES),
 }
 
 
@@ -154,7 +169,7 @@
     run_copies(copies)
 
 
-def split(parcels, awaited, size):
+def split(parcels, awaited, size, work=0):
     pairs = len(parcels)
     noted = parcels[0].shape[0] > 2 * size
     rows = pairs * (size + NOTE * noted)
@@ -165,13 +180,19 @@
         out_specs=VMEM,
         scratch_shapes=[pltpu.SemaphoreType.DMA((pairs, 2))],
         compiler_params=PARAMS,
-        cost_estimate=bytes_cost(rows * HD * 4),
+        cost_estimate=pl.CostEstimate(
+            flops=work, bytes_accessed=rows * HD * 4, transcendentals=0
+        ),
         name="split",
     )(*parcels, *awaited)
 
 
-def merge_kernel(size, *refs):
-    swapped, outs, sems = refs[0], refs[-4:-1], refs[-1]
+def merge_kernel(size, count, noted, *refs):
+    swapped, sems = refs[0], refs[-1]
+    outs = refs[1 + count + noted : 1 + 2 * count + noted]
+    if noted:
+        rows = swapped[(count + 1) * size :, :].astype(jnp.float32)
+        refs[-2][...] = refs[1][...] + jnp.sum(rows, axis=0, keepdims=True)
     run_copies(
         [
             pltpu.make_async_copy(
@@ -182,57 +203,70 @@
     )
 
 
-def merge(swapped, halves, size):
+def merge(swapped, rows, halves, size):
+    held = list(halves) + list(rows)
     return pl.pallas_call(
-        functools.partial(merge_kernel, size),
-        out_shape=[jax.ShapeDtypeStruct(x.shape, x.dtype) for x in halves],
-        in_specs=[VMEM] + [ANY] * len(halves),
-        out_specs=[ANY] * len(halves),
+        functools.partial(merge_kernel, size, len(halves), len(rows)),
+        out_shape=[jax.ShapeDtypeStruct(x.shape, x.dtype) for x in held],
+        in_specs=[VMEM] * (1 + len(rows)) + [ANY] * len(halves),
+        out_specs=[ANY] * len(halves) + [VMEM] * len(rows),
         scratch_shapes=[pltpu.SemaphoreType.DMA((len(halves),))],
-        input_output_aliases={1 + n: n for n in range(len(halves))},
+        input_output_aliases={1 + len(rows) + n: n for n in range(len(halves))},
         compiler_params=PARAMS,
         cost_estimate=bytes_cost(len(halves) * size * HD * 4),
         name="merge",
-    )(swapped, *halves)
-
-
-def unpack_kernel(group, per_device, head, tokens, count, layout, passed, *refs):
-    parcels, outs, sems = refs[:count], refs[-5 - passed : -1 - passed], refs[-1]
+    )(swapped, *rows, *halves)
+
+
+def unpack_kernel(group, per_device, head, tokens, count, layout, passed, rows, *refs):
+    parcels, sems = refs[:count], refs[-1]
+    tail = passed + (rows > 0)
+    outs = refs[-5 - tail : -1 - tail]
+    if rows:
+        total = functools.reduce(jnp.add, [row[...] for row in refs[count : count + rows]])
+        refs[-2][...] = total[0, : group * per_device]
     spot = lax.rem(lax.axis_index("seq"), group)
     copies = []
-    for k, (n, from_row) in enumerate(layout):
+    for i, (k, n, from_row) in enumerate(layout):
         column = pl.multiple_of(((spot ^ k) * per_device + head) * HD, HD)
         for a, out in enumerate(outs):
             copies.append(
                 pltpu.make_async_copy(
                     parcels[n].at[pl.ds(from_row + a * tokens, tokens)],
                     out.at[0, :, pl.ds(column, HD)],
-                    sems.at[k, a],
+                    sems.at[i, a],
                 )
             )
     run_copies(copies)
 
 
-def unpack(parcels, outs, passed, route, group, per_device, head):
-    count = len(parcels)
-    tokens = parcels[0].shape[0] // (4 * route["sizes"][0])
-    layout = [(n, row * 4 * tokens) for n, row in route["arrived"]]
+def unpack(parcels, which, outs, passed, route, tokens, group, per_device, head, work=0, rows=()):
+    count = len(which)
+    layout = [
+        (k, which.index(n), row * 4 * tokens)
+        for k, (n, row) in enumerate(route["arrived"])
+        if n in which
+    ]
+    parcels = [parcels[n] for n in which]
+    total = [jax.ShapeDtypeStruct((group * per_device,), jnp.float32)] if rows else []
     shape = jax.ShapeDtypeStruct((1, tokens, group * per_device * HD), jnp.bfloat16)
     return pl.pallas_call(
         functools.partial(
-            unpack_kernel, group, per_device, head, tokens, count, layout, len(passed)
+            unpack_kernel, group, per_device, head, tokens, count, layout, len(passed), len(rows)
         ),
-        out_shape=[shape] * 4 + [jax.ShapeDtypeStruct(x.shape, x.dtype) for x in passed],
-        in_specs=[VMEM] * count + [ANY] * (len(outs) + len(passed)),
-        out_specs=[ANY] * (4 + len(passed)),
-        scratch_shapes=[pltpu.SemaphoreType.DMA((group, 4))],
+        out_shape=[shape] * 4 + [jax.ShapeDtypeStruct(x.shape, x.dtype) for x in passed] + total,
+        in_specs=[VMEM] * (count + len(rows)) + [ANY] * (len(outs) + len(passed)),
+        out_specs=[ANY] * (4 + len(passed)) + [VMEM] * len(total),
+        scratch_shapes=[pltpu.SemaphoreType.DMA((len(layout), 4))],
         input_output_aliases={
-            count + n: 4 - len(outs) + n for n in range(len(outs) + len(passed))
+            count + len(rows) + n: 4 - len(outs) + n for n in range(len(outs) + len(passed))
         },
         compiler_params=PARAMS,
-        cost_estimate=bytes_cost(group * tokens * HD * 16),
+        cost_estimate=pl.CostEstimate(
+            flops=work, bytes_accessed=len(layout) * tokens * HD * 16, transcendentals=0
+        ),
         name="unpack",
-    )(*parcels, *outs, *passed)
+    )(*parcels, *rows, *outs, *passed)
 
 
 def attend_kernel(group, per_device, head, halo, slots, own_blocks, scale, route, *refs):
@@ -248,7 +282,7 @@
     if halo:
         halo_out, refs = refs[0], refs[1:]
     kv, qd, notes, lists, kt, vt, diag, diag_back, scored, paired, acc, out = refs[:12]
-    sink_acc, sems, list_sem, out_sems = refs[12:]
+    sink_acc, sink_note, sems, list_sem, out_sems = refs[12:]
 
     blocks = own_blocks * group
     span = own_blocks * BLK
@@ -394,8 +428,19 @@
     lax.fori_loop(0, blocks, finish, 0)
     lanes = lax.broadcasted_iota(jnp.int32, (1, BLK), 1)
     sink_sum = jnp.sum(sink_acc[...], axis=1, keepdims=True)
-    sink_out[...] = sink_in[...] - jnp.where(lanes == number, sink_sum, 0.0)
+    sink_row = sink_in[...] - jnp.where(lanes == number, sink_sum, 0.0)
+    sink_out[...] = sink_row
     copies = []
+    if leaving is SWAP_SOME:
+        lines = lax.broadcasted_iota(jnp.int32, (NOTE, BLK), 0)
+        rest, rows = sink_row, jnp.zeros((NOTE, BLK), jnp.float32)
+        for line in range(3):
+            piece = rest.astype(jnp.bfloat16).astype(jnp.float32)
+            rows = jnp.where(lines == line, piece, rows)
+            rest = rest - piece
+        sink_note[...] = rows.astype(jnp.bfloat16)
+        room = results[-1].at[pl.ds(leaving["sizes"][-1] * 4 * span, NOTE)]
+        copies.append(pltpu.make_async_copy(sink_note, room, out_sems.at[group, 0]))
     for k in range(group):
         row = pl.multiple_of((spot ^ k) * span, span)
         n, part = leaving["sent"][k]
@@ -423,9 +468,10 @@
     edge = halo * BLK
     blocks = own_blocks * group
     window = blocks + 2 * halo
-    out_shape = [
-        jax.ShapeDtypeStruct((n * 4 * span, HD), jnp.bfloat16) for n in routes[1]["sizes"]
-    ]
+    rows = [n * 4 * span for n in routes[1]["sizes"]]
+    if routes[1] is SWAP_SOME:
+        rows[-1] += NOTE
+    out_shape = [jax.ShapeDtypeStruct((n, HD), jnp.bfloat16) for n in rows]
     out_specs = [ANY] * len(out_shape) + [VMEM] * 2
     out_shape.append(jax.ShapeDtypeStruct((1, BLK), jnp.float32))
     out_shape.append(jax.ShapeDtypeStruct((blocks, HD), jnp.int32))
@@ -455,9 +501,10 @@
             pltpu.VMEM((window * BLK, 2 * HD), jnp.float32),
             pltpu.VMEM((4, blocks * BLK, HD), jnp.bfloat16),
             pltpu.VMEM((1, BLK), jnp.float32),
+            pltpu.VMEM((NOTE, BLK), jnp.bfloat16),
             pltpu.SemaphoreType.DMA((group + 1, 5)),
             pltpu.SemaphoreType.DMA,
-            pltpu.SemaphoreType.DMA((group, 4)),
+            pltpu.SemaphoreType.DMA((group + 1, 4)),
         ],
         compiler_params=PARAMS,
         cost_estimate=pl.CostEstimate(
@@ -485,6 +532,12 @@
 
     def swap(x, k, axis="seq"):
         return lax.ppermute(x, axis, [(i, i ^ k) for i in range(lax.axis_size(axis))])
+
+    def summed(x, axis, step, end):
+        while step < end:
+            x = x + swap(x, step, axis)
+            step *= 2
+        return x
 
     def beside(x, step):
         route = [(i, i + step * group) for i in range(seq) if 0 <= i + step * group < seq]
@@ -526,15 +579,22 @@
     ]
     adjacency, counts, *sources = constrained
     shared = (adjacency, counts, sources)
-    items = [(0, k, n, part) for k, (n, part) in enumerate(SWAP_AFTER["sent"])]
-    sizes = list(SWAP_AFTER["sizes"])
+    ahead = STEPS[1]
+    items = [(0, k, 0, part) for k, (_, part) in enumerate(SWAP_AFTER["sent"]) if k // 2 * 2 == ahead]
+    (soon,) = pack(*shared, [], items, SWAP_AFTER["sizes"][:1], 1, group, per_device)
+    items = [
+        (0, k, n - (n > 1), part)
+        for k, (n, part) in enumerate(SWAP_AFTER["sent"])
+        if k // 2 * 2 != ahead
+    ]
+    sizes = list(SWAP_AFTER["sizes"][:-1])
     noted = len(sizes)
     cross = len(SWAP_BEFORE["sizes"]) - 1
     sent = list(enumerate(SWAP_BEFORE["sent"]))
     for head in range(1, per_device):
         items += [(head, k, len(sizes), part) for k, (n, part) in sent if n == cross]
         sizes.append(SWAP_BEFORE["sizes"][cross])
-    packed = pack(*shared, [], items, sizes, noted, group, per_device)
+    packed = list(pack(*shared, [soon], items, sizes, noted, group, per_device))
     filled = []
     for head in range(1, per_device):
         items = [(head, k, n, part) for k, (n, part) in sent if n != cross]
@@ -542,17 +602,19 @@
             *shared, packed[:1], items, SWAP_BEFORE["sizes"][:cross], 0, group, per_device
         )
         crossed = swap(packed[noted + head - 1], 1)
-        filled.append((own, merge(crossed, halves, size), crossed))
+        filled.append((own, merge(crossed, [], halves, size), crossed))
     between = SWAP_AFTER["steps"][1:]
-    parcels = [packed[0]] + [swap(x, k) for x, k in zip(packed[1:noted], between)]
+    parcels = [packed[0]] + [swap(x, k) for x, k in zip([soon] + packed[1:noted], between)]
     awaited = [halves[0] for _, halves, _ in filled]
-    arrived = [parcels + [swap(split(parcels, awaited, size), 1)]]
-    routes_in = [SWAP_AFTER] + [SWAP_BEFORE] * (per_device - 1)
+    first = split(parcels[:2], [], size, work=WORK)
+    second = split(parcels[2:], [first] + awaited, size)
+    arrived = [parcels + [swap(first, 1), swap(second, 1)]]
+    routes_in = [SWAP_TWICE] + [SWAP_BEFORE] * (per_device - 1)
     for own, halves, crossed in filled:
-        halves = after(arrived[-1][1:-1], halves)
+        halves = after(arrived[-1][1:4], halves)
         arrived.append([own] + [swap(x, k) for x, k in zip(halves, between)] + [crossed])
 
-    routes_out = [SWAP_AFTER] * (per_device - 1) + [SWAP_BEFORE]
+    routes_out = [SWAP_AFTER] * (per_device - 1) + [SWAP_SOME]
     sink_row = jnp.zeros((1, BLK), jnp.float32)
     marks = jnp.zeros((own_blocks * group, HD), jnp.int32)
     before = arrived[-1][1:-1] if per_device > 1 else []
@@ -582,27 +644,26 @@
         if before:
             results[1:] = after(before, results[1:])
         own, *halves = results
-        if routes[1] is SWAP_BEFORE:
+        steps = routes[1]["steps"][1:]
+        if routes[1] is SWAP_SOME:
             crossed = swap(halves.pop(), 1)
-            halves = merge(crossed, halves, size)
-        before = [swap(x, k) for x, k in zip(halves, between)]
+            *halves[:2], sink_row = merge(crossed, [sink_row], halves[:2], size)
+        before = [swap(x, k) for x, k in zip(halves, steps)]
         returned.append([own] + before)
     returned[-1].append(crossed)
-    for axis, step in (("dp", 1), ("seq", group)):
-        while step < lax.axis_size(axis):
-            sink_row = sink_row + swap(sink_row, step, axis)
-            step *= 2
-    sink_row = sink_row + swap(sink_row, 1)
-    outs = []
+    last = (routes_out[-1], span, group, per_device, per_device - 1)
+    outs = unpack(returned[-1], (0, 3, 4), [], [], *last, work=WORK)
+    sink_row = summed(sink_row, "dp", 1, lax.axis_size("dp"))
+    sink_row = summed(sink_row, "seq", group, seq)
     for head in range(per_device - 1):
         parcels = returned[head] + [swap(split(returned[head], [crossed], size), 1)]
         *outs, sink_row = unpack(
-            parcels, outs, [sink_row], routes_out[head], group, per_device, head
-        )
-    sink_row = functools.reduce(jnp.add, [sink_row] + [swap(sink_row, k) for k in between])
-    outs = unpack(returned[-1], outs, [], routes_out[-1], group, per_device, per_device - 1)
+            parcels, range(5), outs, [sink_row], routes_out[head], span, group, per_device, head
+        )
+    rows = [sink_row] + [swap(sink_row, k) for k in between]
+    *outs, sink_grad = unpack(returned[-1], (1, 2, 5), outs, [], *last, rows=rows)
     value_grad, key_grad, attended, query_grad = outs
-    return attended, query_grad, key_grad, value_grad, sink_row[0, :heads]
+    return attended, query_grad, key_grad, value_grad, sink_grad
 
 
 def solution(mesh):

time: 116 us -> 115 us (level)
  waiting for transfers between devices: 44.3 us -> 41 us
  starting transfers between devices: 23.2 us -> 24.4 us
    ppermute x22 -> x23, waiting for transfers between devices: 44.3 us -> 41 us  [swap(): lax.ppermute(x, axis, [(i, i ^ k) for i in range(lax.axis_size(axis))])]
    ppermute x22 -> x23, starting transfers between devices: 23.2 us -> 24.4 us  [swap(): lax.ppermute(x, axis, [(i, i ^ k) for i in range(lax.axis_size(axis))])]
    pallas_call x2 -> x3, Pallas kernels: 3.14 us -> 4.28 us  [unpack(): pl.pallas_call(functools.partial(unpack_kernel, group, per_device, head,...]
    pallas_call x2 -> x3, Pallas kernels: 3.85 us -> 4.76 us  [pack(): pl.pallas_call(functools.partial(pack_kernel, group, per_device, tokens,...]
  transfers between devices with their start and end apart: 22 -> 23, of which waited for: 10 -> 10; matrix products, arithmetic and copies ran while one was open for 0% -> 0% of each run, Pallas kernels for 38% -> 39%
where the time goes in v4:
time: 115 us; the launch traced here: 114 us
  Pallas kernels  47.4 us (41%)
  waiting for transfers between devices  41 us (36%)
  starting transfers between devices  24.4 us (21%)
    ppermute x23, waiting for transfers between devices, swap(): lax.ppermute(x, axis, [(i, i ^ k) for i in range(lax.axis_size(axis))])  41 us
    pallas_call x2, Pallas kernels, attend(): pl.pallas_call(functools.partial(attend_kernel, group, per_device, head,...  37.9 us
    ppermute x23, starting transfers between devices, swap(): lax.ppermute(x, axis, [(i, i ^ k) for i in range(lax.axis_size(axis))])  24.4 us
    pallas_call x3, Pallas kernels, pack(): pl.pallas_call(functools.partial(pack_kernel, group, per_device, tokens,...  4.76 us
    pallas_call x3, Pallas kernels, unpack(): pl.pallas_call(functools.partial(unpack_kernel, group, per_device, head,...  4.28 us
  transfers between devices with their start and end apart: 23, of which 10 were waited for; matrix products, arithmetic and copies ran while one was open for 0% of the time, Pallas kernels for 39%

profile of v4, /device:TPU:0, one launch (start us, length us, event | category | flops | bytes accessed | tf_op | source)
XLA Modules:
  0.0 114.3 jit_solution(7435763222356551420)
XLA Ops:
  0.6 1.2 %pack.3.refs_6_ = bf16[2064,128]{1,0:T(8,128)(2,1)S(1)} custom-call(s32[1,2,8]{2,1,0:T(2,128)} %refs_0_.7, s32[1,2]{1,0:T(1,128)} %refs_1_.5, bf16[1,256,2048]{2,1,0:T(8,128)(2,1)} %refs_2_.5, bf16[1,256,2048]{2,1,0:T(8,128)(2,1)} %refs_3_.5, bf16[1,256,2048]{2,1,0:T(8,128)(2,1)} %refs_4_.5, bf16[1,256,2048]{2,1,0:T(8,128)(2,1)} %refs_5_.5), custom_call_target="tpu_custom_call" | custom-call | bytes 1048576 | tf_op jit(solution)/shard_map/pack/pallas_call | solution.py:119
  1.8 3.0 %collective-permute-start = (bf16[2064,128]{1,0:T(8,128)(2,1)S(1)}, bf16[2064,128]{1,0:T(8,128)(2,1)S(1)}, u32[]{:S(2)}, u32[]{:S(2)}) collective-permute-start(bf16[2064,128]{1,0:T(8,128)(2,1)S(1)} %pack.3.refs_6_), channel_id=1, source_target_pairs={{0,8},{4,12},{8,0},{12,4},{16,24},{20,28},{24,16},{28,20},{1,9},{5... | collective-permute-start | bytes 1585160 | tf_op jit(solution)/shard_map/ppermute | solution.py:534
  4.8 2.2 %pack.4 = (bf16[2064,128]{1,0:T(8,128)(2,1)S(1)}, bf16[2064,128]{1,0:T(8,128)(2,1)S(1)}, bf16[2064,128]{1,0:T(8,128)(2,1)S(1)}, bf16[4096,128]{1,0:T(8,128)(2,1)S(1)}) custom-call(s32[1,2,8]{2,1,0:T(2,128)} %refs_0_.7, s32[1,2]{1,0:T(1,128)} %refs_1_.5, bf16[1,256,2048]{2,1,0:T(8,128)(2,1)} %refs_2_.5, bf16[1,256,2048]{2,1,0:T(8,128)(2,1)} %refs_3_.5, ...), custom_call_target="tpu_custom_call" | custom-call | bytes 5242880 | tf_op jit(solution)/shard_map/pack/pallas_call | solution.py:119
  7.0 1.6 %collective-permute-start.1 = (bf16[2064,128]{1,0:T(8,128)(2,1)S(1)}, bf16[2064,128]{1,0:T(8,128)(2,1)S(1)}, u32[]{:S(2)}, u32[]{:S(2)}) collective-permute-start(bf16[2064,128]{1,0:T(8,128)(2,1)S(1)} %get-tuple-element.58), channel_id=1, source_target_pairs={{0,16},{4,20},{8,24},{12,28},{16,0},{20,4},{24,8},{28,12},{1,17},{... | collective-permute-start | bytes 1585160 | tf_op jit(solution)/shard_map/ppermute | solution.py:534
  8.6 1.4 %pack.5 = (bf16[1024,128]{1,0:T(8,128)(2,1)S(1)}, bf16[2048,128]{1,0:T(8,128)(2,1)S(1)}, bf16[2048,128]{1,0:T(8,128)(2,1)S(1)}, bf16[2048,128]{1,0:T(8,128)(2,1)S(1)}) custom-call(s32[1,2,8]{2,1,0:T(2,128)} %refs_0_.7, s32[1,2]{1,0:T(1,128)} %refs_1_.5, bf16[1,256,2048]{2,1,0:T(8,128)(2,1)} %refs_2_.5, bf16[1,256,2048]{2,1,0:T(8,128)(2,1)} %refs_3_.5, ...), custom_call_target="tpu_custom_call" | custom-call | bytes 2097152 | tf_op jit(solution)/shard_map/pack/pallas_call | solution.py:119
  10.1 7.6 %collective-permute-done.refs_1_.refs_4_.refs_3_ = bf16[2064,128]{1,0:T(8,128)(2,1)S(1)} collective-permute-done((bf16[2064,128]{1,0:T(8,128)(2,1)S(1)}, bf16[2064,128]{1,0:T(8,128)(2,1)S(1)}, u32[]{:S(2)}, u32[]{:S(2)}) %collective-permute-start) | collective-permute-done | bytes 528416 | tf_op jit(solution)/shard_map/ppermute | solution.py:534
  17.9 13.9 %collective-permute-done.1.refs_0_.refs_5_.refs_4_ = bf16[2064,128]{1,0:T(8,128)(2,1)S(1)} collective-permute-done((bf16[2064,128]{1,0:T(8,128)(2,1)S(1)}, bf16[2064,128]{1,0:T(8,128)(2,1)S(1)}, u32[]{:S(2)}, u32[]{:S(2)}) %collective-permute-start.1) | collective-permute-done | bytes 528416 | tf_op jit(solution)/shard_map/ppermute | solution.py:534
  32.4 1.7 %collective-permute-start.7 = (bf16[2048,128]{1,0:T(8,128)(2,1)S(1)}, bf16[2048,128]{1,0:T(8,128)(2,1)S(1)}, u32[]{:S(2)}, u32[]{:S(2)}) collective-permute-start(bf16[2048,128]{1,0:T(8,128)(2,1)S(1)} %get-tuple-element.71), channel_id=1, source_target_pairs={{0,16},{4,20},{8,24},{12,28},{16,0},{20,4},{24,8},{28,12},{1,17},{... | collective-permute-start | bytes 1572872 | tf_op jit(solution)/shard_map/ppermute | solution.py:534
  34.2 1.4 %collective-permute-start.8 = (bf16[2048,128]{1,0:T(8,128)(2,1)S(1)}, bf16[2048,128]{1,0:T(8,128)(2,1)S(1)}, u32[]{:S(2)}, u32[]{:S(2)}) collective-permute-start(bf16[2048,128]{1,0:T(8,128)(2,1)S(1)} %get-tuple-element.72), channel_id=1, source_target_pairs={{0,24},{4,28},{8,16},{12,20},{16,8},{20,12},{24,0},{28,4},{1,25},{... | collective-permute-start | bytes 1572872 | tf_op jit(solution)/shard_map/ppermute | solution.py:534
  35.6 0.6 copy-done
  36.3 18.8 %attend.2 = (bf16[2048,128]{1,0:T(8,128)(2,1)S(1)}, bf16[2048,128]{1,0:T(8,128)(2,1)S(1)}, bf16[2048,128]{1,0:T(8,128)(2,1)S(1)}, bf16[2048,128]{1,0:T(8,128)(2,...) custom-call(f32[16]{0:T(128)S(1)} %copy-done, f32[1,128]{1,0:T(1,128)S(1)} %broadcast_in_dim.6.refs_1_, ...), custom_call_target="tpu_custom_call" | custom-call | flops 17179869184 | bytes 4194304 | tf_op jit(solution)/shard_map/attend/pallas_call | solution.py:483
  55.0 1.9 %collective-permute-done.7.refs_5_.refs_4_ = bf16[2048,128]{1,0:T(8,128)(2,1)S(1)} collective-permute-done((bf16[2048,128]{1,0:T(8,128)(2,1)S(1)}, bf16[2048,128]{1,0:T(8,128)(2,1)S(1)}, u32[]{:S(2)}, u32[]{:S(2)}) %collective-permute-start.7) | collective-permute-done | bytes 524320 | tf_op jit(solution)/shard_map/ppermute | solution.py:534
  56.9 1.6 %collective-permute-done.8.refs_6_.refs_5_ = bf16[2048,128]{1,0:T(8,128)(2,1)S(1)} collective-permute-done((bf16[2048,128]{1,0:T(8,128)(2,1)S(1)}, bf16[2048,128]{1,0:T(8,128)(2,1)S(1)}, u32[]{:S(2)}, u32[]{:S(2)}) %collective-permute-start.8) | collective-permute-done | bytes 524320 | tf_op jit(solution)/shard_map/ppermute | solution.py:534
  58.6 0.8 collective-permute-start.9
  59.4 1.5 %collective-permute-start.10 = (bf16[2048,128]{1,0:T(8,128)(2,1)S(1)}, bf16[2048,128]{1,0:T(8,128)(2,1)S(1)}, u32[]{:S(2)}, u32[]{:S(2)}) collective-permute-start(bf16[2048,128]{1,0:T(8,128)(2,1)S(1)} %get-tuple-element.82), channel_id=1, source_target_pairs={{0,16},{4,20},{8,24},{12,28},{16,0},{20,4},{24,8},{28,12},{1,17},{... | collective-permute-start | bytes 1572872 | tf_op jit(solution)/shard_map/ppermute | solution.py:534
  60.9 1.2 %collective-permute-start.11 = (bf16[2048,128]{1,0:T(8,128)(2,1)S(1)}, bf16[2048,128]{1,0:T(8,128)(2,1)S(1)}, u32[]{:S(2)}, u32[]{:S(2)}) collective-permute-start(bf16[2048,128]{1,0:T(8,128)(2,1)S(1)} %get-tuple-element.83), channel_id=1, source_target_pairs={{0,24},{4,28},{8,16},{12,20},{16,8},{20,12},{24,0},{28,4},{1,25},{... | collective-permute-start | bytes 1572872 | tf_op jit(solution)/shard_map/ppermute | solution.py:534
  62.1 19.1 %attend.3 = (bf16[1024,128]{1,0:T(8,128)(2,1)S(1)}, bf16[2048,128]{1,0:T(8,128)(2,1)S(1)}, bf16[2048,128]{1,0:T(8,128)(2,1)S(1)}, bf16[1024,128]{1,0:T(8,128)(2,...) custom-call(f32[16]{0:T(128)S(1)} %copy-done, ...), custom_call_target="tpu_custom_call" | custom-call | flops 17179869184 | bytes 4194304 | tf_op jit(solution)/shard_map/attend/pallas_call | solution.py:483
  81.2 2.4 %collective-permute-done.10.refs_6_.refs_2_ = bf16[2048,128]{1,0:T(8,128)(2,1)S(1)} collective-permute-done((bf16[2048,128]{1,0:T(8,128)(2,1)S(1)}, bf16[2048,128]{1,0:T(8,128)(2,1)S(1)}, u32[]{:S(2)}, u32[]{:S(2)}) %collective-permute-start.10) | collective-permute-done | bytes 524320 | tf_op jit(solution)/shard_map/ppermute | solution.py:534
  83.6 1.5 %collective-permute-start.16 = (bf16[1024,128]{1,0:T(8,128)(2,1)S(1)}, bf16[1024,128]{1,0:T(8,128)(2,1)S(1)}, u32[]{:S(2)}, u32[]{:S(2)}) collective-permute-start(bf16[1024,128]{1,0:T(8,128)(2,1)S(1)} %get-tuple-element.92), channel_id=1, source_target_pairs={{0,8},{4,12},{8,0},{12,4},{16,24},{20,28},{24,16},{28,20},{1,9},{5... | collective-permute-start | bytes 786440 | tf_op jit(solution)/shard_map/ppermute | solution.py:534
  85.9 1.6 %collective-permute-start.18 = (f32[1,128]{1,0:T(1,128)S(1)}, f32[1,128]{1,0:T(1,128)S(1)}, u32[]{:S(2)}, u32[]{:S(2)}) collective-permute-start(f32[1,128]{1,0:T(1,128)S(1)} %get-tuple-element.98), channel_id=1, source_target_pairs={{0,1},{1,0},{2,3},{3,2},{4,5},{5,4},{6,7},{7,6},{8,9},{9,8},{10,11... | collective-permute-start | bytes 1544 | tf_op jit(solution)/shard_map/ppermute | solution.py:534
  87.6 1.4 %collective-permute-start.13 = (bf16[2048,128]{1,0:T(8,128)(2,1)S(1)}, bf16[2048,128]{1,0:T(8,128)(2,1)S(1)}, u32[]{:S(2)}, u32[]{:S(2)}) collective-permute-start(bf16[2048,128]{1,0:T(8,128)(2,1)S(1)} %get-tuple-element.88), channel_id=1, source_target_pairs={{0,16},{4,20},{8,24},{12,28},{16,0},{20,4},{24,8},{28,12},{1,17},{... | collective-permute-start | bytes 1572872 | tf_op jit(solution)/shard_map/ppermute | solution.py:534
  89.0 1.5 %collective-permute-start.14 = (bf16[2048,128]{1,0:T(8,128)(2,1)S(1)}, bf16[2048,128]{1,0:T(8,128)(2,1)S(1)}, u32[]{:S(2)}, u32[]{:S(2)}) collective-permute-start(bf16[2048,128]{1,0:T(8,128)(2,1)S(1)} %get-tuple-element.89), channel_id=1, source_target_pairs={{0,24},{4,28},{8,16},{12,20},{16,8},{20,12},{24,0},{28,4},{1,25},{... | collective-permute-start | bytes 1572872 | tf_op jit(solution)/shard_map/ppermute | solution.py:534
  90.8 2.0 %collective-permute-done.16.refs_1_ = bf16[1024,128]{1,0:T(8,128)(2,1)S(1)} collective-permute-done((bf16[1024,128]{1,0:T(8,128)(2,1)S(1)}, bf16[1024,128]{1,0:T(8,128)(2,1)S(1)}, u32[]{:S(2)}, u32[]{:S(2)}) %collective-permute-start.16) | collective-permute-done | bytes 262176 | tf_op jit(solution)/shard_map/ppermute | solution.py:534
  92.7 2.6 %collective-permute-start.19 = (f32[1,128]{1,0:T(1,128)S(1)}, f32[1,128]{1,0:T(1,128)S(1)}, u32[]{:S(2)}, u32[]{:S(2)}) collective-permute-start(f32[1,128]{1,0:T(1,128)S(1)} %add.6), channel_id=1, source_target_pairs={{0,2},{1,3},{2,0},{3,1},{4,6},{5,7},{6,4},{7,5},{8,10},{9,11},{10,... | collective-permute-start | bytes 1544 | tf_op jit(solution)/shard_map/ppermute | solution.py:534
  95.3 2.1 %collective-permute-done.17.refs_2_ = bf16[1024,128]{1,0:T(8,128)(2,1)S(1)} collective-permute-done((bf16[1024,128]{1,0:T(8,128)(2,1)S(1)}, bf16[1024,128]{1,0:T(8,128)(2,1)S(1)}, u32[]{:S(2)}, u32[]{:S(2)}) %collective-permute-start.17) | collective-permute-done | bytes 262176 | tf_op jit(solution)/shard_map/ppermute | solution.py:534
  97.5 1.0 unpack.3
  98.5 1.6 %unpack.4 = (bf16[1,256,2048]{2,1,0:T(8,128)(2,1)}, bf16[1,256,2048]{2,1,0:T(8,128)(2,1)}, bf16[1,256,2048]{2,1,0:T(8,128)(2,1)}, bf16[1,256,2048]{2,1,0:T(8,128)(2,1)}, f32[1,128]{1,0:T(1,128)S(1)}) custom-call(bf16[2048,128]{1,0:T(8,128)(2,1)S(1)} %get-tuple-element.90.refs_0_, ...), custom_call_target="tpu_custom_call", output_to_operand_aliasing={{0}: (5, {}), {1}: (6, {}), {2}: (7, {}), {3}: (8, {}), {4}... | custom-call | bytes 4194304 | tf_op jit(solution)/shard_map/unpack/pallas_call | solution.py:253
  100.1 1.5 %collective-permute-start.22 = (f32[1,128]{1,0:T(1,128)S(1)}, f32[1,128]{1,0:T(1,128)S(1)}, u32[]{:S(2)}, u32[]{:S(2)}) collective-permute-start(f32[1,128]{1,0:T(1,128)S(1)} %get-tuple-element.99.refs_3_), channel_id=1, source_target_pairs={{0,24},{4,28},{8,16},{12,20},{16,8},{20,12},{24,0},{28,4},{1,25},{... | collective-permute-start | bytes 1544 | tf_op jit(solution)/shard_map/ppermute | solution.py:534
  101.6 1.5 %collective-permute-start.21 = (f32[1,128]{1,0:T(1,128)S(1)}, f32[1,128]{1,0:T(1,128)S(1)}, u32[]{:S(2)}, u32[]{:S(2)}) collective-permute-start(f32[1,128]{1,0:T(1,128)S(1)} %get-tuple-element.99.refs_3_), channel_id=1, source_target_pairs={{0,16},{4,20},{8,24},{12,28},{16,0},{20,4},{24,8},{28,12},{1,17},{... | collective-permute-start | bytes 1544 | tf_op jit(solution)/shard_map/ppermute | solution.py:534
  103.0 0.6 collective-permute-start.20
  103.6 8.9 %collective-permute-done.13.refs_0_ = bf16[2048,128]{1,0:T(8,128)(2,1)S(1)} collective-permute-done((bf16[2048,128]{1,0:T(8,128)(2,1)S(1)}, bf16[2048,128]{1,0:T(8,128)(2,1)S(1)}, u32[]{:S(2)}, u32[]{:S(2)}) %collective-permute-start.13) | collective-permute-done | bytes 524320 | tf_op jit(solution)/shard_map/ppermute | solution.py:534
  112.6 1.7 %unpack.5 = (bf16[1,256,2048]{2,1,0:T(8,128)(2,1)}, bf16[1,256,2048]{2,1,0:T(8,128)(2,1)}, bf16[1,256,2048]{2,1,0:T(8,128)(2,1)}, bf16[1,256,2048]{2,1,0:T(8,128)(2,1)}, f32[16]{0:T(128)}) custom-call(bf16[2048,128]{1,0:T(8,128)(2,1)S(1)} %collective-permute-done.13.refs_0_, ...), custom_call_target="tpu_custom_call", output_to_operand_aliasing={{0}: (7, {}), {1}: (8, {}), {2}: (9, {}), {3}: (10, {})} | custom-call | bytes 2621440 | tf_op jit(solution)/shard_map/unpack/pallas_call | solution.py:253
  (36 shorter events, 2.0 us)
Async XLA Ops:
  1.8 15.8 %collective-permute-start = (bf16[2064,128]{1,0:T(8,128)(2,1)S(1)}, bf16[2064,128]{1,0:T(8,128)(2,1)S(1)}, u32[]{:S(2)}, u32[]{:S(2)}) collective-permute-start(bf16[2064,128]{1,0:T(8,128)(2,1)S(1)} %pack.3.refs_6_), channel_id=1, source_target_pairs={{0,8},{4,12},{8,0},{12,4},{16,24},{20,28},{24,16},{28,20},{1,9},{5... | collective-permute-start | bytes 1585160 | tf_op jit(solution)/shard_map/ppermute | solution.py:534
  7.0 24.9 %collective-permute-start.1 = (bf16[2064,128]{1,0:T(8,128)(2,1)S(1)}, bf16[2064,128]{1,0:T(8,128)(2,1)S(1)}, u32[]{:S(2)}, u32[]{:S(2)}) collective-permute-start(bf16[2064,128]{1,0:T(8,128)(2,1)S(1)} %get-tuple-element.58), channel_id=1, source_target_pairs={{0,16},{4,20},{8,24},{12,28},{16,0},{20,4},{24,8},{28,12},{1,17},{... | collective-permute-start | bytes 1585160 | tf_op jit(solution)/shard_map/ppermute | solution.py:534
  8.6 23.3 %collective-permute-start.2 = (bf16[2064,128]{1,0:T(8,128)(2,1)S(1)}, bf16[2064,128]{1,0:T(8,128)(2,1)S(1)}, u32[]{:S(2)}, u32[]{:S(2)}) collective-permute-start(bf16[2064,128]{1,0:T(8,128)(2,1)S(1)} %get-tuple-element.59), channel_id=1, source_target_pairs={{0,24},{4,28},{8,16},{12,20},{16,8},{20,12},{24,0},{28,4},{1,25},{... | collective-permute-start | bytes 1585160 | tf_op jit(solution)/shard_map/ppermute | solution.py:534
  8.6 9.2 %collective-permute-start.4 = (bf16[4096,128]{1,0:T(8,128)(2,1)S(1)}, bf16[4096,128]{1,0:T(8,128)(2,1)S(1)}, u32[]{:S(2)}, u32[]{:S(2)}) collective-permute-start(bf16[4096,128]{1,0:T(8,128)(2,1)S(1)} %get-tuple-element.60), channel_id=1, source_target_pairs={{0,4},{4,0},{8,12},{12,8},{16,20},{20,16},{24,28},{28,24},{1,5},{5... | collective-permute-start | bytes 3145736 | tf_op jit(solution)/shard_map/ppermute | solution.py:534
  17.8 17.8 %collective-permute-start.3 = (bf16[2080,128]{1,0:T(8,128)(2,1)S(1)}, bf16[2080,128]{1,0:T(8,128)(2,1)S(1)}, u32[]{:S(2)}, u32[]{:S(2)}) collective-permute-start(bf16[2080,128]{1,0:T(8,128)(2,1)S(1)} %split.3.refs_2_), channel_id=1, source_target_pairs={{0,4},{4,0},{8,12},{12,8},{16,20},{20,16},{24,28},{28,24},{1,5},{5... | collective-permute-start | bytes 1597448 | tf_op jit(solution)/shard_map/ppermute | solution.py:534
  31.9 3.7 %collective-permute-start.5 = (bf16[2080,128]{1,0:T(8,128)(2,1)S(1)}, bf16[2080,128]{1,0:T(8,128)(2,1)S(1)}, u32[]{:S(2)}, u32[]{:S(2)}) collective-permute-start(bf16[2080,128]{1,0:T(8,128)(2,1)S(1)} %split.4), channel_id=1, source_target_pairs={{0,4},{4,0},{8,12},{12,8},{16,20},{20,16},{24,28},{28,24},{1,5},{5... | collective-permute-start | bytes 1597448 | tf_op jit(solution)/shard_map/ppermute | solution.py:534
  32.0 23.0 %collective-permute-start.6 = (bf16[2048,128]{1,0:T(8,128)(2,1)S(1)}, bf16[2048,128]{1,0:T(8,128)(2,1)S(1)}, u32[]{:S(2)}, u32[]{:S(2)}) collective-permute-start(bf16[2048,128]{1,0:T(8,128)(2,1)S(1)} %get-tuple-element.70), channel_id=1, source_target_pairs={{0,8},{4,12},{8,0},{12,4},{16,24},{20,28},{24,16},{28,20},{1,9},{5... | collective-permute-start | bytes 1572872 | tf_op jit(solution)/shard_map/ppermute | solution.py:534
  32.4 24.5 %collective-permute-start.7 = (bf16[2048,128]{1,0:T(8,128)(2,1)S(1)}, bf16[2048,128]{1,0:T(8,128)(2,1)S(1)}, u32[]{:S(2)}, u32[]{:S(2)}) collective-permute-start(bf16[2048,128]{1,0:T(8,128)(2,1)S(1)} %get-tuple-element.71), channel_id=1, source_target_pairs={{0,16},{4,20},{8,24},{12,28},{16,0},{20,4},{24,8},{28,12},{1,17},{... | collective-permute-start | bytes 1572872 | tf_op jit(solution)/shard_map/ppermute | solution.py:534
  34.2 24.4 %collective-permute-start.8 = (bf16[2048,128]{1,0:T(8,128)(2,1)S(1)}, bf16[2048,128]{1,0:T(8,128)(2,1)S(1)}, u32[]{:S(2)}, u32[]{:S(2)}) collective-permute-start(bf16[2048,128]{1,0:T(8,128)(2,1)S(1)} %get-tuple-element.72), channel_id=1, source_target_pairs={{0,24},{4,28},{8,16},{12,20},{16,8},{20,12},{24,0},{28,4},{1,25},{... | collective-permute-start | bytes 1572872 | tf_op jit(solution)/shard_map/ppermute | solution.py:534
  35.6 0.7 copy-start
  58.6 22.6 %collective-permute-start.9 = (bf16[2048,128]{1,0:T(8,128)(2,1)S(1)}, bf16[2048,128]{1,0:T(8,128)(2,1)S(1)}, u32[]{:S(2)}, u32[]{:S(2)}) collective-permute-start(bf16[2048,128]{1,0:T(8,128)(2,1)S(1)} %get-tuple-element.81), channel_id=1, source_target_pairs={{0,8},{4,12},{8,0},{12,4},{16,24},{20,28},{24,16},{28,20},{1,9},{5... | collective-permute-start | bytes 1572872 | tf_op jit(solution)/shard_map/ppermute | solution.py:534
  59.4 24.2 %collective-permute-start.10 = (bf16[2048,128]{1,0:T(8,128)(2,1)S(1)}, bf16[2048,128]{1,0:T(8,128)(2,1)S(1)}, u32[]{:S(2)}, u32[]{:S(2)}) collective-permute-start(bf16[2048,128]{1,0:T(8,128)(2,1)S(1)} %get-tuple-element.82), channel_id=1, source_target_pairs={{0,16},{4,20},{8,24},{12,28},{16,0},{20,4},{24,8},{28,12},{1,17},{... | collective-permute-start | bytes 1572872 | tf_op jit(solution)/shard_map/ppermute | solution.py:534
  60.9 22.7 %collective-permute-start.11 = (bf16[2048,128]{1,0:T(8,128)(2,1)S(1)}, bf16[2048,128]{1,0:T(8,128)(2,1)S(1)}, u32[]{:S(2)}, u32[]{:S(2)}) collective-permute-start(bf16[2048,128]{1,0:T(8,128)(2,1)S(1)} %get-tuple-element.83), channel_id=1, source_target_pairs={{0,24},{4,28},{8,16},{12,20},{16,8},{20,12},{24,0},{28,4},{1,25},{... | collective-permute-start | bytes 1572872 | tf_op jit(solution)/shard_map/ppermute | solution.py:534
  83.6 2.3 %collective-permute-start.12 = (bf16[3088,128]{1,0:T(8,128)(2,1)S(1)}, bf16[3088,128]{1,0:T(8,128)(2,1)S(1)}, u32[]{:S(2)}, u32[]{:S(2)}) collective-permute-start(bf16[3088,128]{1,0:T(8,128)(2,1)S(1)} %get-tuple-element.84), channel_id=1, source_target_pairs={{0,4},{4,0},{8,12},{12,8},{16,20},{20,16},{24,28},{28,24},{1,5},{5... | collective-permute-start | bytes 2371592 | tf_op jit(solution)/shard_map/ppermute | solution.py:534
  83.6 9.2 %collective-permute-start.16 = (bf16[1024,128]{1,0:T(8,128)(2,1)S(1)}, bf16[1024,128]{1,0:T(8,128)(2,1)S(1)}, u32[]{:S(2)}, u32[]{:S(2)}) collective-permute-start(bf16[1024,128]{1,0:T(8,128)(2,1)S(1)} %get-tuple-element.92), channel_id=1, source_target_pairs={{0,8},{4,12},{8,0},{12,4},{16,24},{20,28},{24,16},{28,20},{1,9},{5... | collective-permute-start | bytes 786440 | tf_op jit(solution)/shard_map/ppermute | solution.py:534
  85.1 12.4 %collective-permute-start.17 = (bf16[1024,128]{1,0:T(8,128)(2,1)S(1)}, bf16[1024,128]{1,0:T(8,128)(2,1)S(1)}, u32[]{:S(2)}, u32[]{:S(2)}) collective-permute-start(bf16[1024,128]{1,0:T(8,128)(2,1)S(1)} %get-tuple-element.93), channel_id=1, source_target_pairs={{0,12},{4,8},{8,4},{12,0},{16,28},{20,24},{24,20},{28,16},{1,13},{... | collective-permute-start | bytes 786440 | tf_op jit(solution)/shard_map/ppermute | solution.py:534
  85.9 4.7 %collective-permute-start.18 = (f32[1,128]{1,0:T(1,128)S(1)}, f32[1,128]{1,0:T(1,128)S(1)}, u32[]{:S(2)}, u32[]{:S(2)}) collective-permute-start(f32[1,128]{1,0:T(1,128)S(1)} %get-tuple-element.98), channel_id=1, source_target_pairs={{0,1},{1,0},{2,3},{3,2},{4,5},{5,4},{6,7},{7,6},{8,9},{9,8},{10,11... | collective-permute-start | bytes 1544 | tf_op jit(solution)/shard_map/ppermute | solution.py:534
  87.6 24.9 %collective-permute-start.13 = (bf16[2048,128]{1,0:T(8,128)(2,1)S(1)}, bf16[2048,128]{1,0:T(8,128)(2,1)S(1)}, u32[]{:S(2)}, u32[]{:S(2)}) collective-permute-start(bf16[2048,128]{1,0:T(8,128)(2,1)S(1)} %get-tuple-element.88), channel_id=1, source_target_pairs={{0,16},{4,20},{8,24},{12,28},{16,0},{20,4},{24,8},{28,12},{1,17},{... | collective-permute-start | bytes 1572872 | tf_op jit(solution)/shard_map/ppermute | solution.py:534
  89.0 23.5 %collective-permute-start.14 = (bf16[2048,128]{1,0:T(8,128)(2,1)S(1)}, bf16[2048,128]{1,0:T(8,128)(2,1)S(1)}, u32[]{:S(2)}, u32[]{:S(2)}) collective-permute-start(bf16[2048,128]{1,0:T(8,128)(2,1)S(1)} %get-tuple-element.89), channel_id=1, source_target_pairs={{0,24},{4,28},{8,16},{12,20},{16,8},{20,12},{24,0},{28,4},{1,25},{... | collective-permute-start | bytes 1572872 | tf_op jit(solution)/shard_map/ppermute | solution.py:534
  90.7 7.8 %collective-permute-start.15 = (bf16[4096,128]{1,0:T(8,128)(2,1)S(1)}, bf16[4096,128]{1,0:T(8,128)(2,1)S(1)}, u32[]{:S(2)}, u32[]{:S(2)}) collective-permute-start(bf16[4096,128]{1,0:T(8,128)(2,1)S(1)} %split.5), channel_id=1, source_target_pairs={{0,4},{4,0},{8,12},{12,8},{16,20},{20,16},{24,28},{28,24},{1,5},{5... | collective-permute-start | bytes 3145736 | tf_op jit(solution)/shard_map/ppermute | solution.py:534
  92.7 5.7 %collective-permute-start.19 = (f32[1,128]{1,0:T(1,128)S(1)}, f32[1,128]{1,0:T(1,128)S(1)}, u32[]{:S(2)}, u32[]{:S(2)}) collective-permute-start(f32[1,128]{1,0:T(1,128)S(1)} %add.6), channel_id=1, source_target_pairs={{0,2},{1,3},{2,0},{3,1},{4,6},{5,7},{6,4},{7,5},{8,10},{9,11},{10,... | collective-permute-start | bytes 1544 | tf_op jit(solution)/shard_map/ppermute | solution.py:534
  100.1 12.5 %collective-permute-start.22 = (f32[1,128]{1,0:T(1,128)S(1)}, f32[1,128]{1,0:T(1,128)S(1)}, u32[]{:S(2)}, u32[]{:S(2)}) collective-permute-start(f32[1,128]{1,0:T(1,128)S(1)} %get-tuple-element.99.refs_3_), channel_id=1, source_target_pairs={{0,24},{4,28},{8,16},{12,20},{16,8},{20,12},{24,0},{28,4},{1,25},{... | collective-permute-start | bytes 1544 | tf_op jit(solution)/shard_map/ppermute | solution.py:534
  101.6 11.0 %collective-permute-start.21 = (f32[1,128]{1,0:T(1,128)S(1)}, f32[1,128]{1,0:T(1,128)S(1)}, u32[]{:S(2)}, u32[]{:S(2)}) collective-permute-start(f32[1,128]{1,0:T(1,128)S(1)} %get-tuple-element.99.refs_3_), channel_id=1, source_target_pairs={{0,16},{4,20},{8,24},{12,28},{16,0},{20,4},{24,8},{28,12},{1,17},{... | collective-permute-start | bytes 1544 | tf_op jit(solution)/shard_map/ppermute | solution.py:534
  103.0 9.6 %collective-permute-start.20 = (f32[1,128]{1,0:T(1,128)S(1)}, f32[1,128]{1,0:T(1,128)S(1)}, u32[]{:S(2)}, u32[]{:S(2)}) collective-permute-start(f32[1,128]{1,0:T(1,128)S(1)} %get-tuple-element.99.refs_3_), channel_id=1, source_target_pairs={{0,8},{4,12},{8,0},{12,4},{16,24},{20,28},{24,16},{28,20},{1,9},{5... | collective-permute-start | bytes 1544 | tf_op jit(solution)/shard_map/ppermute | solution.py:534

commit v5 on v4

--- a/solution.py
+++ b/solution.py
@@ -641,7 +641,10 @@
         results, sink_row, marks = list(done[:count]), done[count], done[count + 1]
         if halo:
             results = add_halos(results, done[count + 2], routes[1])
-        if before:
+        if before and head < per_device - 1:
+            results[1:2] = after(before[:1], results[1:2])
+            results[2:] = after(before[1:] + results[1:2], results[2:])
+        elif before:
             results[1:] = after(before, results[1:])
         own, *halves = results
         steps = routes[1]["steps"][1:]

time: 115 us -> 114 us (level)
  starting transfers between devices: 24.4 us -> 22.8 us
    ppermute x23, starting transfers between devices: 24.4 us -> 22.8 us  [swap(): lax.ppermute(x, axis, [(i, i ^ k) for i in range(lax.axis_size(axis))])]
where the time goes in v5:
time: 114 us
  Pallas kernels  47.9 us (42%)
  waiting for transfers between devices  41.8 us (37%)
  starting transfers between devices  22.8 us (20%)
    ppermute x23, waiting for transfers between devices, swap(): lax.ppermute(x, axis, [(i, i ^ k) for i in range(lax.axis_size(axis))])  41.8 us
    pallas_call x2, Pallas kernels, attend(): pl.pallas_call(functools.partial(attend_kernel, group, per_device, head,...  38.4 us
    ppermute x23, starting transfers between devices, swap(): lax.ppermute(x, axis, [(i, i ^ k) for i in range(lax.axis_size(axis))])  22.8 us
    pallas_call x3, Pallas kernels, pack(): pl.pallas_call(functools.partial(pack_kernel, group, per_device, tokens,...  4.76 us
    pallas_call x3, Pallas kernels, unpack(): pl.pallas_call(functools.partial(unpack_kernel, group, per_device, head,...  4.28 us
  transfers between devices with their start and end apart: 23, of which 10 were waited for; matrix products, arithmetic and copies ran while one was open for 0% of the time, Pallas kernels for 39%

profile of v5, /device:TPU:0, one launch (start us, length us, event | category | flops | bytes accessed | tf_op | source)
XLA Modules:
  0.0 114.1 jit_solution(16035215280529421847)
XLA Ops:
  0.6 1.2 %pack.3.refs_6_ = bf16[2064,128]{1,0:T(8,128)(2,1)S(1)} custom-call(s32[1,2,8]{2,1,0:T(2,128)} %refs_0_.7, s32[1,2]{1,0:T(1,128)} %refs_1_.5, bf16[1,256,2048]{2,1,0:T(8,128)(2,1)} %refs_2_.5, bf16[1,256,2048]{2,1,0:T(8,128)(2,1)} %refs_3_.5, bf16[1,256,2048]{2,1,0:T(8,128)(2,1)} %refs_4_.5, bf16[1,256,2048]{2,1,0:T(8,128)(2,1)} %refs_5_.5), custom_call_target="tpu_custom_call" | custom-call | bytes 1048576 | tf_op jit(solution)/shard_map/pack/pallas_call | solution.py:119
  1.8 3.0 %collective-permute-start = (bf16[2064,128]{1,0:T(8,128)(2,1)S(1)}, bf16[2064,128]{1,0:T(8,128)(2,1)S(1)}, u32[]{:S(2)}, u32[]{:S(2)}) collective-permute-start(bf16[2064,128]{1,0:T(8,128)(2,1)S(1)} %pack.3.refs_6_), channel_id=1, source_target_pairs={{0,8},{4,12},{8,0},{12,4},{16,24},{20,28},{24,16},{28,20},{1,9},{5... | collective-permute-start | bytes 1585160 | tf_op jit(solution)/shard_map/ppermute | solution.py:534
  4.8 2.2 %pack.4 = (bf16[2064,128]{1,0:T(8,128)(2,1)S(1)}, bf16[2064,128]{1,0:T(8,128)(2,1)S(1)}, bf16[2064,128]{1,0:T(8,128)(2,1)S(1)}, bf16[4096,128]{1,0:T(8,128)(2,1)S(1)}) custom-call(s32[1,2,8]{2,1,0:T(2,128)} %refs_0_.7, s32[1,2]{1,0:T(1,128)} %refs_1_.5, bf16[1,256,2048]{2,1,0:T(8,128)(2,1)} %refs_2_.5, bf16[1,256,2048]{2,1,0:T(8,128)(2,1)} %refs_3_.5, ...), custom_call_target="tpu_custom_call" | custom-call | bytes 5242880 | tf_op jit(solution)/shard_map/pack/pallas_call | solution.py:119
  7.0 1.6 %collective-permute-start.1 = (bf16[2064,128]{1,0:T(8,128)(2,1)S(1)}, bf16[2064,128]{1,0:T(8,128)(2,1)S(1)}, u32[]{:S(2)}, u32[]{:S(2)}) collective-permute-start(bf16[2064,128]{1,0:T(8,128)(2,1)S(1)} %get-tuple-element.57), channel_id=1, source_target_pairs={{0,16},{4,20},{8,24},{12,28},{16,0},{20,4},{24,8},{28,12},{1,17},{... | collective-permute-start | bytes 1585160 | tf_op jit(solution)/shard_map/ppermute | solution.py:534
  8.6 1.4 %pack.5 = (bf16[1024,128]{1,0:T(8,128)(2,1)S(1)}, bf16[2048,128]{1,0:T(8,128)(2,1)S(1)}, bf16[2048,128]{1,0:T(8,128)(2,1)S(1)}, bf16[2048,128]{1,0:T(8,128)(2,1)S(1)}) custom-call(s32[1,2,8]{2,1,0:T(2,128)} %refs_0_.7, s32[1,2]{1,0:T(1,128)} %refs_1_.5, bf16[1,256,2048]{2,1,0:T(8,128)(2,1)} %refs_2_.5, bf16[1,256,2048]{2,1,0:T(8,128)(2,1)} %refs_3_.5, ...), custom_call_target="tpu_custom_call" | custom-call | bytes 2097152 | tf_op jit(solution)/shard_map/pack/pallas_call | solution.py:119
  10.1 7.6 %collective-permute-done.refs_1_.refs_4_.refs_3_ = bf16[2064,128]{1,0:T(8,128)(2,1)S(1)} collective-permute-done((bf16[2064,128]{1,0:T(8,128)(2,1)S(1)}, bf16[2064,128]{1,0:T(8,128)(2,1)S(1)}, u32[]{:S(2)}, u32[]{:S(2)}) %collective-permute-start) | collective-permute-done | bytes 528416 | tf_op jit(solution)/shard_map/ppermute | solution.py:534
  17.9 13.9 %collective-permute-done.1.refs_0_.refs_5_.refs_4_ = bf16[2064,128]{1,0:T(8,128)(2,1)S(1)} collective-permute-done((bf16[2064,128]{1,0:T(8,128)(2,1)S(1)}, bf16[2064,128]{1,0:T(8,128)(2,1)S(1)}, u32[]{:S(2)}, u32[]{:S(2)}) %collective-permute-start.1) | collective-permute-done | bytes 528416 | tf_op jit(solution)/shard_map/ppermute | solution.py:534
  32.4 1.7 %collective-permute-start.7 = (bf16[2048,128]{1,0:T(8,128)(2,1)S(1)}, bf16[2048,128]{1,0:T(8,128)(2,1)S(1)}, u32[]{:S(2)}, u32[]{:S(2)}) collective-permute-start(bf16[2048,128]{1,0:T(8,128)(2,1)S(1)} %get-tuple-element.70), channel_id=1, source_target_pairs={{0,16},{4,20},{8,24},{12,28},{16,0},{20,4},{24,8},{28,12},{1,17},{... | collective-permute-start | bytes 1572872 | tf_op jit(solution)/shard_map/ppermute | solution.py:534
  34.2 1.4 %collective-permute-start.8 = (bf16[2048,128]{1,0:T(8,128)(2,1)S(1)}, bf16[2048,128]{1,0:T(8,128)(2,1)S(1)}, u32[]{:S(2)}, u32[]{:S(2)}) collective-permute-start(bf16[2048,128]{1,0:T(8,128)(2,1)S(1)} %get-tuple-element.71), channel_id=1, source_target_pairs={{0,24},{4,28},{8,16},{12,20},{16,8},{20,12},{24,0},{28,4},{1,25},{... | collective-permute-start | bytes 1572872 | tf_op jit(solution)/shard_map/ppermute | solution.py:534
  35.6 0.6 copy-done
  36.3 19.0 %attend.2 = (bf16[2048,128]{1,0:T(8,128)(2,1)S(1)}, bf16[2048,128]{1,0:T(8,128)(2,1)S(1)}, bf16[2048,128]{1,0:T(8,128)(2,1)S(1)}, bf16[2048,128]{1,0:T(8,128)(2,...) custom-call(f32[16]{0:T(128)S(1)} %copy-done, f32[1,128]{1,0:T(1,128)S(1)} %broadcast_in_dim.6.refs_1_, ...), custom_call_target="tpu_custom_call" | custom-call | flops 17179869184 | bytes 4194304 | tf_op jit(solution)/shard_map/attend/pallas_call | solution.py:483
  55.7 1.2 %collective-permute-done.7.refs_5_.refs_2_ = bf16[2048,128]{1,0:T(8,128)(2,1)S(1)} collective-permute-done((bf16[2048,128]{1,0:T(8,128)(2,1)S(1)}, bf16[2048,128]{1,0:T(8,128)(2,1)S(1)}, u32[]{:S(2)}, u32[]{:S(2)}) %collective-permute-start.7) | collective-permute-done | bytes 524320 | tf_op jit(solution)/shard_map/ppermute | solution.py:534
  56.9 1.6 %collective-permute-done.8.refs_6_.refs_3_ = bf16[2048,128]{1,0:T(8,128)(2,1)S(1)} collective-permute-done((bf16[2048,128]{1,0:T(8,128)(2,1)S(1)}, bf16[2048,128]{1,0:T(8,128)(2,1)S(1)}, u32[]{:S(2)}, u32[]{:S(2)}) %collective-permute-start.8) | collective-permute-done | bytes 524320 | tf_op jit(solution)/shard_map/ppermute | solution.py:534
  58.6 0.8 collective-permute-start.10
  59.4 1.4 %collective-permute-start.11 = (bf16[2048,128]{1,0:T(8,128)(2,1)S(1)}, bf16[2048,128]{1,0:T(8,128)(2,1)S(1)}, u32[]{:S(2)}, u32[]{:S(2)}) collective-permute-start(bf16[2048,128]{1,0:T(8,128)(2,1)S(1)} %get-tuple-element.81), channel_id=1, source_target_pairs={{0,24},{4,28},{8,16},{12,20},{16,8},{20,12},{24,0},{28,4},{1,25},{... | collective-permute-start | bytes 1572872 | tf_op jit(solution)/shard_map/ppermute | solution.py:534
  60.8 19.4 %attend.3 = (bf16[1024,128]{1,0:T(8,128)(2,1)S(1)}, bf16[2048,128]{1,0:T(8,128)(2,1)S(1)}, bf16[2048,128]{1,0:T(8,128)(2,1)S(1)}, bf16[1024,128]{1,0:T(8,128)(2,...) custom-call(f32[16]{0:T(128)S(1)} %copy-done, ...), custom_call_target="tpu_custom_call" | custom-call | flops 17179869184 | bytes 4194304 | tf_op jit(solution)/shard_map/attend/pallas_call | solution.py:483
  80.2 3.1 %collective-permute-done.10.refs_6_.refs_2_ = bf16[2048,128]{1,0:T(8,128)(2,1)S(1)} collective-permute-done((bf16[2048,128]{1,0:T(8,128)(2,1)S(1)}, bf16[2048,128]{1,0:T(8,128)(2,1)S(1)}, u32[]{:S(2)}, u32[]{:S(2)}) %collective-permute-start.10) | collective-permute-done | bytes 524320 | tf_op jit(solution)/shard_map/ppermute | solution.py:534
  83.4 0.6 collective-permute-start.16
  84.0 1.2 %collective-permute-start.17 = (bf16[1024,128]{1,0:T(8,128)(2,1)S(1)}, bf16[1024,128]{1,0:T(8,128)(2,1)S(1)}, u32[]{:S(2)}, u32[]{:S(2)}) collective-permute-start(bf16[1024,128]{1,0:T(8,128)(2,1)S(1)} %get-tuple-element.91), channel_id=1, source_target_pairs={{0,12},{4,8},{8,4},{12,0},{16,28},{20,24},{24,20},{28,16},{1,13},{... | collective-permute-start | bytes 786440 | tf_op jit(solution)/shard_map/ppermute | solution.py:534
  85.7 1.6 %collective-permute-start.18 = (f32[1,128]{1,0:T(1,128)S(1)}, f32[1,128]{1,0:T(1,128)S(1)}, u32[]{:S(2)}, u32[]{:S(2)}) collective-permute-start(f32[1,128]{1,0:T(1,128)S(1)} %get-tuple-element.96), channel_id=1, source_target_pairs={{0,1},{1,0},{2,3},{3,2},{4,5},{5,4},{6,7},{7,6},{8,9},{9,8},{10,11... | collective-permute-start | bytes 1544 | tf_op jit(solution)/shard_map/ppermute | solution.py:534
  87.3 0.6 collective-permute-start.13
  87.9 1.5 %collective-permute-start.14 = (bf16[2048,128]{1,0:T(8,128)(2,1)S(1)}, bf16[2048,128]{1,0:T(8,128)(2,1)S(1)}, u32[]{:S(2)}, u32[]{:S(2)}) collective-permute-start(bf16[2048,128]{1,0:T(8,128)(2,1)S(1)} %get-tuple-element.87), channel_id=1, source_target_pairs={{0,24},{4,28},{8,16},{12,20},{16,8},{20,12},{24,0},{28,4},{1,25},{... | collective-permute-start | bytes 1572872 | tf_op jit(solution)/shard_map/ppermute | solution.py:534
  89.7 2.9 %collective-permute-done.16.refs_1_ = bf16[1024,128]{1,0:T(8,128)(2,1)S(1)} collective-permute-done((bf16[1024,128]{1,0:T(8,128)(2,1)S(1)}, bf16[1024,128]{1,0:T(8,128)(2,1)S(1)}, u32[]{:S(2)}, u32[]{:S(2)}) %collective-permute-start.16) | collective-permute-done | bytes 262176 | tf_op jit(solution)/shard_map/ppermute | solution.py:534
  92.5 2.6 %collective-permute-start.19 = (f32[1,128]{1,0:T(1,128)S(1)}, f32[1,128]{1,0:T(1,128)S(1)}, u32[]{:S(2)}, u32[]{:S(2)}) collective-permute-start(f32[1,128]{1,0:T(1,128)S(1)} %add.6), channel_id=1, source_target_pairs={{0,2},{1,3},{2,0},{3,1},{4,6},{5,7},{6,4},{7,5},{8,10},{9,11},{10,... | collective-permute-start | bytes 1544 | tf_op jit(solution)/shard_map/ppermute | solution.py:534
  95.1 2.1 %collective-permute-done.17.refs_2_ = bf16[1024,128]{1,0:T(8,128)(2,1)S(1)} collective-permute-done((bf16[1024,128]{1,0:T(8,128)(2,1)S(1)}, bf16[1024,128]{1,0:T(8,128)(2,1)S(1)}, u32[]{:S(2)}, u32[]{:S(2)}) %collective-permute-start.17) | collective-permute-done | bytes 262176 | tf_op jit(solution)/shard_map/ppermute | solution.py:534
  97.2 1.0 unpack.3
  98.2 1.6 %unpack.4 = (bf16[1,256,2048]{2,1,0:T(8,128)(2,1)}, bf16[1,256,2048]{2,1,0:T(8,128)(2,1)}, bf16[1,256,2048]{2,1,0:T(8,128)(2,1)}, bf16[1,256,2048]{2,1,0:T(8,128)(2,1)}, f32[1,128]{1,0:T(1,128)S(1)}) custom-call(bf16[2048,128]{1,0:T(8,128)(2,1)S(1)} %get-tuple-element.88.refs_0_, ...), custom_call_target="tpu_custom_call", output_to_operand_aliasing={{0}: (5, {}), {1}: (6, {}), {2}: (7, {}), {3}: (8, {}), {4}... | custom-call | bytes 4194304 | tf_op jit(solution)/shard_map/unpack/pallas_call | solution.py:253
  99.8 1.5 %collective-permute-start.22 = (f32[1,128]{1,0:T(1,128)S(1)}, f32[1,128]{1,0:T(1,128)S(1)}, u32[]{:S(2)}, u32[]{:S(2)}) collective-permute-start(f32[1,128]{1,0:T(1,128)S(1)} %get-tuple-element.97.refs_3_), channel_id=1, source_target_pairs={{0,24},{4,28},{8,16},{12,20},{16,8},{20,12},{24,0},{28,4},{1,25},{... | collective-permute-start | bytes 1544 | tf_op jit(solution)/shard_map/ppermute | solution.py:534
  101.3 0.6 collective-permute-start.21
  101.9 1.4 %collective-permute-start.20 = (f32[1,128]{1,0:T(1,128)S(1)}, f32[1,128]{1,0:T(1,128)S(1)}, u32[]{:S(2)}, u32[]{:S(2)}) collective-permute-start(f32[1,128]{1,0:T(1,128)S(1)} %get-tuple-element.97.refs_3_), channel_id=1, source_target_pairs={{0,8},{4,12},{8,0},{12,4},{16,24},{20,28},{24,16},{28,20},{1,9},{5... | collective-permute-start | bytes 1544 | tf_op jit(solution)/shard_map/ppermute | solution.py:534
  103.4 8.9 %collective-permute-done.13.refs_0_ = bf16[2048,128]{1,0:T(8,128)(2,1)S(1)} collective-permute-done((bf16[2048,128]{1,0:T(8,128)(2,1)S(1)}, bf16[2048,128]{1,0:T(8,128)(2,1)S(1)}, u32[]{:S(2)}, u32[]{:S(2)}) %collective-permute-start.13) | collective-permute-done | bytes 524320 | tf_op jit(solution)/shard_map/ppermute | solution.py:534
  112.3 1.7 %unpack.5 = (bf16[1,256,2048]{2,1,0:T(8,128)(2,1)}, bf16[1,256,2048]{2,1,0:T(8,128)(2,1)}, bf16[1,256,2048]{2,1,0:T(8,128)(2,1)}, bf16[1,256,2048]{2,1,0:T(8,128)(2,1)}, f32[16]{0:T(128)}) custom-call(bf16[2048,128]{1,0:T(8,128)(2,1)S(1)} %collective-permute-done.13.refs_0_, ...), custom_call_target="tpu_custom_call", output_to_operand_aliasing={{0}: (7, {}), {1}: (8, {}), {2}: (9, {}), {3}: (10, {})} | custom-call | bytes 2621440 | tf_op jit(solution)/shard_map/unpack/pallas_call | solution.py:253
  (37 shorter events, 2.1 us)
Async XLA Ops:
  1.8 15.8 %collective-permute-start = (bf16[2064,128]{1,0:T(8,128)(2,1)S(1)}, bf16[2064,128]{1,0:T(8,128)(2,1)S(1)}, u32[]{:S(2)}, u32[]{:S(2)}) collective-permute-start(bf16[2064,128]{1,0:T(8,128)(2,1)S(1)} %pack.3.refs_6_), channel_id=1, source_target_pairs={{0,8},{4,12},{8,0},{12,4},{16,24},{20,28},{24,16},{28,20},{1,9},{5... | collective-permute-start | bytes 1585160 | tf_op jit(solution)/shard_map/ppermute | solution.py:534
  7.0 24.9 %collective-permute-start.1 = (bf16[2064,128]{1,0:T(8,128)(2,1)S(1)}, bf16[2064,128]{1,0:T(8,128)(2,1)S(1)}, u32[]{:S(2)}, u32[]{:S(2)}) collective-permute-start(bf16[2064,128]{1,0:T(8,128)(2,1)S(1)} %get-tuple-element.57), channel_id=1, source_target_pairs={{0,16},{4,20},{8,24},{12,28},{16,0},{20,4},{24,8},{28,12},{1,17},{... | collective-permute-start | bytes 1585160 | tf_op jit(solution)/shard_map/ppermute | solution.py:534
  8.6 23.3 %collective-permute-start.2 = (bf16[2064,128]{1,0:T(8,128)(2,1)S(1)}, bf16[2064,128]{1,0:T(8,128)(2,1)S(1)}, u32[]{:S(2)}, u32[]{:S(2)}) collective-permute-start(bf16[2064,128]{1,0:T(8,128)(2,1)S(1)} %get-tuple-element.58), channel_id=1, source_target_pairs={{0,24},{4,28},{8,16},{12,20},{16,8},{20,12},{24,0},{28,4},{1,25},{... | collective-permute-start | bytes 1585160 | tf_op jit(solution)/shard_map/ppermute | solution.py:534
  8.6 9.2 %collective-permute-start.4 = (bf16[4096,128]{1,0:T(8,128)(2,1)S(1)}, bf16[4096,128]{1,0:T(8,128)(2,1)S(1)}, u32[]{:S(2)}, u32[]{:S(2)}) collective-permute-start(bf16[4096,128]{1,0:T(8,128)(2,1)S(1)} %get-tuple-element.59), channel_id=1, source_target_pairs={{0,4},{4,0},{8,12},{12,8},{16,20},{20,16},{24,28},{28,24},{1,5},{5... | collective-permute-start | bytes 3145736 | tf_op jit(solution)/shard_map/ppermute | solution.py:534
  17.8 17.8 %collective-permute-start.3 = (bf16[2080,128]{1,0:T(8,128)(2,1)S(1)}, bf16[2080,128]{1,0:T(8,128)(2,1)S(1)}, u32[]{:S(2)}, u32[]{:S(2)}) collective-permute-start(bf16[2080,128]{1,0:T(8,128)(2,1)S(1)} %split.3.refs_2_), channel_id=1, source_target_pairs={{0,4},{4,0},{8,12},{12,8},{16,20},{20,16},{24,28},{28,24},{1,5},{5... | collective-permute-start | bytes 1597448 | tf_op jit(solution)/shard_map/ppermute | solution.py:534
  31.9 3.7 %collective-permute-start.5 = (bf16[2080,128]{1,0:T(8,128)(2,1)S(1)}, bf16[2080,128]{1,0:T(8,128)(2,1)S(1)}, u32[]{:S(2)}, u32[]{:S(2)}) collective-permute-start(bf16[2080,128]{1,0:T(8,128)(2,1)S(1)} %split.4), channel_id=1, source_target_pairs={{0,4},{4,0},{8,12},{12,8},{16,20},{20,16},{24,28},{28,24},{1,5},{5... | collective-permute-start | bytes 1597448 | tf_op jit(solution)/shard_map/ppermute | solution.py:534
  32.0 23.3 %collective-permute-start.6 = (bf16[2048,128]{1,0:T(8,128)(2,1)S(1)}, bf16[2048,128]{1,0:T(8,128)(2,1)S(1)}, u32[]{:S(2)}, u32[]{:S(2)}) collective-permute-start(bf16[2048,128]{1,0:T(8,128)(2,1)S(1)} %get-tuple-element.69), channel_id=1, source_target_pairs={{0,8},{4,12},{8,0},{12,4},{16,24},{20,28},{24,16},{28,20},{1,9},{5... | collective-permute-start | bytes 1572872 | tf_op jit(solution)/shard_map/ppermute | solution.py:534
  32.4 24.5 %collective-permute-start.7 = (bf16[2048,128]{1,0:T(8,128)(2,1)S(1)}, bf16[2048,128]{1,0:T(8,128)(2,1)S(1)}, u32[]{:S(2)}, u32[]{:S(2)}) collective-permute-start(bf16[2048,128]{1,0:T(8,128)(2,1)S(1)} %get-tuple-element.70), channel_id=1, source_target_pairs={{0,16},{4,20},{8,24},{12,28},{16,0},{20,4},{24,8},{28,12},{1,17},{... | collective-permute-start | bytes 1572872 | tf_op jit(solution)/shard_map/ppermute | solution.py:534
  34.2 24.4 %collective-permute-start.8 = (bf16[2048,128]{1,0:T(8,128)(2,1)S(1)}, bf16[2048,128]{1,0:T(8,128)(2,1)S(1)}, u32[]{:S(2)}, u32[]{:S(2)}) collective-permute-start(bf16[2048,128]{1,0:T(8,128)(2,1)S(1)} %get-tuple-element.71), channel_id=1, source_target_pairs={{0,24},{4,28},{8,16},{12,20},{16,8},{20,12},{24,0},{28,4},{1,25},{... | collective-permute-start | bytes 1572872 | tf_op jit(solution)/shard_map/ppermute | solution.py:534
  35.6 0.7 copy-start
  55.3 28.0 %collective-permute-start.9 = (bf16[2048,128]{1,0:T(8,128)(2,1)S(1)}, bf16[2048,128]{1,0:T(8,128)(2,1)S(1)}, u32[]{:S(2)}, u32[]{:S(2)}) collective-permute-start(bf16[2048,128]{1,0:T(8,128)(2,1)S(1)} %after.5.refs_4_), channel_id=1, source_target_pairs={{0,8},{4,12},{8,0},{12,4},{16,24},{20,28},{24,16},{28,20},{1,9},{5... | collective-permute-start | bytes 1572872 | tf_op jit(solution)/shard_map/ppermute | solution.py:534
  58.6 24.7 %collective-permute-start.10 = (bf16[2048,128]{1,0:T(8,128)(2,1)S(1)}, bf16[2048,128]{1,0:T(8,128)(2,1)S(1)}, u32[]{:S(2)}, u32[]{:S(2)}) collective-permute-start(bf16[2048,128]{1,0:T(8,128)(2,1)S(1)} %get-tuple-element.80), channel_id=1, source_target_pairs={{0,16},{4,20},{8,24},{12,28},{16,0},{20,4},{24,8},{28,12},{1,17},{... | collective-permute-start | bytes 1572872 | tf_op jit(solution)/shard_map/ppermute | solution.py:534
  59.4 23.9 %collective-permute-start.11 = (bf16[2048,128]{1,0:T(8,128)(2,1)S(1)}, bf16[2048,128]{1,0:T(8,128)(2,1)S(1)}, u32[]{:S(2)}, u32[]{:S(2)}) collective-permute-start(bf16[2048,128]{1,0:T(8,128)(2,1)S(1)} %get-tuple-element.81), channel_id=1, source_target_pairs={{0,24},{4,28},{8,16},{12,20},{16,8},{20,12},{24,0},{28,4},{1,25},{... | collective-permute-start | bytes 1572872 | tf_op jit(solution)/shard_map/ppermute | solution.py:534
  83.3 2.4 %collective-permute-start.12 = (bf16[3088,128]{1,0:T(8,128)(2,1)S(1)}, bf16[3088,128]{1,0:T(8,128)(2,1)S(1)}, u32[]{:S(2)}, u32[]{:S(2)}) collective-permute-start(bf16[3088,128]{1,0:T(8,128)(2,1)S(1)} %get-tuple-element.82), channel_id=1, source_target_pairs={{0,4},{4,0},{8,12},{12,8},{16,20},{20,16},{24,28},{28,24},{1,5},{5... | collective-permute-start | bytes 2371592 | tf_op jit(solution)/shard_map/ppermute | solution.py:534
  83.4 9.2 %collective-permute-start.16 = (bf16[1024,128]{1,0:T(8,128)(2,1)S(1)}, bf16[1024,128]{1,0:T(8,128)(2,1)S(1)}, u32[]{:S(2)}, u32[]{:S(2)}) collective-permute-start(bf16[1024,128]{1,0:T(8,128)(2,1)S(1)} %get-tuple-element.90), channel_id=1, source_target_pairs={{0,8},{4,12},{8,0},{12,4},{16,24},{20,28},{24,16},{28,20},{1,9},{5... | collective-permute-start | bytes 786440 | tf_op jit(solution)/shard_map/ppermute | solution.py:534
  84.0 13.2 %collective-permute-start.17 = (bf16[1024,128]{1,0:T(8,128)(2,1)S(1)}, bf16[1024,128]{1,0:T(8,128)(2,1)S(1)}, u32[]{:S(2)}, u32[]{:S(2)}) collective-permute-start(bf16[1024,128]{1,0:T(8,128)(2,1)S(1)} %get-tuple-element.91), channel_id=1, source_target_pairs={{0,12},{4,8},{8,4},{12,0},{16,28},{20,24},{24,20},{28,16},{1,13},{... | collective-permute-start | bytes 786440 | tf_op jit(solution)/shard_map/ppermute | solution.py:534
  85.7 3.8 %collective-permute-start.18 = (f32[1,128]{1,0:T(1,128)S(1)}, f32[1,128]{1,0:T(1,128)S(1)}, u32[]{:S(2)}, u32[]{:S(2)}) collective-permute-start(f32[1,128]{1,0:T(1,128)S(1)} %get-tuple-element.96), channel_id=1, source_target_pairs={{0,1},{1,0},{2,3},{3,2},{4,5},{5,4},{6,7},{7,6},{8,9},{9,8},{10,11... | collective-permute-start | bytes 1544 | tf_op jit(solution)/shard_map/ppermute | solution.py:534
  87.3 24.9 %collective-permute-start.13 = (bf16[2048,128]{1,0:T(8,128)(2,1)S(1)}, bf16[2048,128]{1,0:T(8,128)(2,1)S(1)}, u32[]{:S(2)}, u32[]{:S(2)}) collective-permute-start(bf16[2048,128]{1,0:T(8,128)(2,1)S(1)} %get-tuple-element.86), channel_id=1, source_target_pairs={{0,16},{4,20},{8,24},{12,28},{16,0},{20,4},{24,8},{28,12},{1,17},{... | collective-permute-start | bytes 1572872 | tf_op jit(solution)/shard_map/ppermute | solution.py:534
  87.9 24.4 %collective-permute-start.14 = (bf16[2048,128]{1,0:T(8,128)(2,1)S(1)}, bf16[2048,128]{1,0:T(8,128)(2,1)S(1)}, u32[]{:S(2)}, u32[]{:S(2)}) collective-permute-start(bf16[2048,128]{1,0:T(8,128)(2,1)S(1)} %get-tuple-element.87), channel_id=1, source_target_pairs={{0,24},{4,28},{8,16},{12,20},{16,8},{20,12},{24,0},{28,4},{1,25},{... | collective-permute-start | bytes 1572872 | tf_op jit(solution)/shard_map/ppermute | solution.py:534
  89.6 8.7 %collective-permute-start.15 = (bf16[4096,128]{1,0:T(8,128)(2,1)S(1)}, bf16[4096,128]{1,0:T(8,128)(2,1)S(1)}, u32[]{:S(2)}, u32[]{:S(2)}) collective-permute-start(bf16[4096,128]{1,0:T(8,128)(2,1)S(1)} %split.5), channel_id=1, source_target_pairs={{0,4},{4,0},{8,12},{12,8},{16,20},{20,16},{24,28},{28,24},{1,5},{5... | collective-permute-start | bytes 3145736 | tf_op jit(solution)/shard_map/ppermute | solution.py:534
  92.5 5.7 %collective-permute-start.19 = (f32[1,128]{1,0:T(1,128)S(1)}, f32[1,128]{1,0:T(1,128)S(1)}, u32[]{:S(2)}, u32[]{:S(2)}) collective-permute-start(f32[1,128]{1,0:T(1,128)S(1)} %add.6), channel_id=1, source_target_pairs={{0,2},{1,3},{2,0},{3,1},{4,6},{5,7},{6,4},{7,5},{8,10},{9,11},{10,... | collective-permute-start | bytes 1544 | tf_op jit(solution)/shard_map/ppermute | solution.py:534
  99.8 12.5 %collective-permute-start.22 = (f32[1,128]{1,0:T(1,128)S(1)}, f32[1,128]{1,0:T(1,128)S(1)}, u32[]{:S(2)}, u32[]{:S(2)}) collective-permute-start(f32[1,128]{1,0:T(1,128)S(1)} %get-tuple-element.97.refs_3_), channel_id=1, source_target_pairs={{0,24},{4,28},{8,16},{12,20},{16,8},{20,12},{24,0},{28,4},{1,25},{... | collective-permute-start | bytes 1544 | tf_op jit(solution)/shard_map/ppermute | solution.py:534
  101.3 11.0 %collective-permute-start.21 = (f32[1,128]{1,0:T(1,128)S(1)}, f32[1,128]{1,0:T(1,128)S(1)}, u32[]{:S(2)}, u32[]{:S(2)}) collective-permute-start(f32[1,128]{1,0:T(1,128)S(1)} %get-tuple-element.97.refs_3_), channel_id=1, source_target_pairs={{0,16},{4,20},{8,24},{12,28},{16,0},{20,4},{24,8},{28,12},{1,17},{... | collective-permute-start | bytes 1544 | tf_op jit(solution)/shard_map/ppermute | solution.py:534
  101.9 10.4 %collective-permute-start.20 = (f32[1,128]{1,0:T(1,128)S(1)}, f32[1,128]{1,0:T(1,128)S(1)}, u32[]{:S(2)}, u32[]{:S(2)}) collective-permute-start(f32[1,128]{1,0:T(1,128)S(1)} %get-tuple-element.97.refs_3_), channel_id=1, source_target_pairs={{0,8},{4,12},{8,0},{12,4},{16,24},{20,28},{24,16},{28,20},{1,9},{5... | collective-permute-start | bytes 1544 | tf_op jit(solution)/shard_map/ppermute | solution.py:534
